TPU v7x, 32 devices: a whole 2x2x4 slice. The times are simulated.
32 devices in a mesh: row: 8 (over y, x, core), col: 4 (over z).
Axes of the slice: x: 2, y: 2, z: 4, core: 2. Of those that a mesh axis runs over, the one named last changes fastest.
Arguments:
- z_trunk: bfloat16 [512, 512, 128], P('row', 'col'), may hold values from -6 to 6
- coords: int32 [3, 512], P(None, ('row', 'col')), may hold values from 0 to 255
- token_mask: int32 [512], P(('row', 'col')), may hold values 0 or 1
- w_dist: bfloat16 [39, 128], replicated, may hold values from -6 to 6
- w_attn: bfloat16 [128, 512], replicated, may hold values from -0.5 to 0.5
- w_bias: bfloat16 [128, 4], replicated, may hold values from -100 to 100
- w_out: bfloat16 [128, 128], replicated, may hold values from -2 to 2
- w_pae: bfloat16 [128, 64], replicated, may hold values from -0.5 to 0.5
- w_pde: bfloat16 [128, 64], replicated, may hold values from -0.5 to 0.5
Outputs:
- logits: float32 [512, 512, 128], P('row', 'col')
All inputs are finite; a program needn't handle non-finite values. No bound on the sum of `token_mask` on one device may be relied on, other than what follows from the above.
Results may differ from a plain program's by a relative error of at most 0.0055.
The roundings to bfloat16 on the way count: a program that leaves them out, or rounds other values in their place, can miss the bound.
Values may be sent and summed in bfloat16 or wider, within the bound.
No kernel may reach another device: no remote copies, remote signals or barrier semaphores. Data moves between devices by JAX's collectives and lax.ppermute only.
A program may use at most 192 MiB of HBM per device.

v0:
```python
import jax
import jax.numpy as jnp
from jax import lax
from jax.sharding import PartitionSpec as P


def layer_norm(values):
    widened = values.astype(jnp.float32)
    average = jnp.mean(widened, axis=-1, keepdims=True)
    centred = widened - average
    variance = jnp.mean(centred * centred, axis=-1, keepdims=True)
    return (centred * lax.rsqrt(variance + 1e-05)).astype(jnp.bfloat16)


def distance_bins(coord_rows, coord_cols, class_count):
    offsets = coord_rows[:, :, None] - coord_cols[:, None, :]
    squared = jnp.sum(offsets * offsets, axis=0)
    bin_edges = 27 + 4 * jnp.arange(class_count - 1, dtype=jnp.int32)
    above = (squared[:, :, None] > (bin_edges * bin_edges)[None, None, :]).astype(jnp.int32)
    return jnp.sum(above, axis=-1)


def attend_column(query_rows, key_rows, value_rows, bias_full, key_bias):
    length_all = query_rows.shape[0]
    block_rows = min(512, length_all)

    def one_block(first_row):
        query_block = lax.dynamic_slice_in_dim(query_rows, first_row, block_rows, 0)
        bias_block = lax.dynamic_slice_in_dim(bias_full, first_row, block_rows, 2)
        scores = jnp.einsum(
            "khd,ihd->hki", key_rows, query_block, preferred_element_type=jnp.float32
        )
        scores = scores + bias_block + key_bias[None, :, None]
        highest = jnp.max(scores, axis=1, keepdims=True)
        raised = jnp.exp(scores - highest)
        weights = (raised / jnp.sum(raised, axis=1, keepdims=True)).astype(jnp.bfloat16)
        return jnp.einsum("hki,khd->ihd", weights, value_rows, preferred_element_type=jnp.float32)

    starts = jnp.arange(length_all // block_rows, dtype=jnp.int32) * block_rows
    blocks_out = lax.map(one_block, starts)
    return blocks_out.reshape(length_all, query_rows.shape[1], query_rows.shape[2])


def error_logits(updated, mirrored, w_pae, w_pde):
    width = updated.shape[-1]
    symmetric = updated.astype(jnp.float32) + mirrored.astype(jnp.float32)
    pae_part = jnp.dot(
        layer_norm(updated).reshape(-1, width), w_pae, preferred_element_type=jnp.float32
    )
    pde_part = jnp.dot(
        layer_norm(symmetric).reshape(-1, width), w_pde, preferred_element_type=jnp.float32
    )
    return jnp.concatenate([pae_part, pde_part], axis=1).reshape(
        updated.shape[0], updated.shape[1], -1
    )


def per_device(z_trunk, coords, token_mask, w_dist, w_attn, w_bias, w_out, w_pae, w_pde):
    all_coords, all_mask = (
        lax.all_gather(coords, ("row", "col"), axis=1, tiled=True),
        lax.all_gather(token_mask, ("row", "col"), axis=0, tiled=True),
    )
    rows_dev = z_trunk.shape[0]
    cols_dev = z_trunk.shape[1]
    width = z_trunk.shape[2]
    n_rows = lax.axis_size("row")
    n_cols = lax.axis_size("col")
    total = rows_dev * n_rows
    slab = rows_dev // n_cols
    heads = w_bias.shape[1]
    head_dim = width // heads
    classes = w_dist.shape[0]
    row_first = lax.axis_index("row") * rows_dev
    col_first = lax.axis_index("col") * cols_dev
    coord_rows = lax.dynamic_slice_in_dim(all_coords, row_first, rows_dev, 1)
    coord_cols = lax.dynamic_slice_in_dim(all_coords, col_first, cols_dev, 1)
    bins_tile = distance_bins(coord_rows, coord_cols, classes)
    one_hot = (bins_tile[:, :, None] == jnp.arange(classes, dtype=jnp.int32)[None, None, :]).astype(
        jnp.bfloat16
    )
    embedded = jnp.dot(one_hot.reshape(-1, classes), w_dist, preferred_element_type=jnp.float32)
    pair = (z_trunk.astype(jnp.float32) + embedded.reshape(rows_dev, cols_dev, width)).astype(
        jnp.bfloat16
    )
    pair_cols = lax.all_to_all(pair, "row", split_axis=1, concat_axis=0, tiled=True)
    normed = layer_norm(pair_cols)
    flat_normed = normed.reshape(-1, width)
    projected = jnp.dot(flat_normed, w_attn, preferred_element_type=jnp.float32)
    query_all = (
        (projected[:, :width] * head_dim ** (-0.5))
        .astype(jnp.bfloat16)
        .reshape(total, slab, heads, head_dim)
    )
    key_all = (
        projected[:, width : 2 * width].astype(jnp.bfloat16).reshape(total, slab, heads, head_dim)
    )
    value_all = (
        projected[:, 2 * width : 3 * width]
        .astype(jnp.bfloat16)
        .reshape(total, slab, heads, head_dim)
    )
    gate_all = projected[:, 3 * width :].astype(jnp.bfloat16)
    bias_local = jnp.einsum("kic,ch->hki", normed, w_bias, preferred_element_type=jnp.float32)
    bias_half = lax.all_gather(bias_local, "row", axis=2, tiled=True)
    bias_full = lax.all_gather(bias_half, "col", axis=2, tiled=True)
    key_bias = (all_mask.astype(jnp.float32) - 1.0) * 30000.0

    def one_column(operands):
        query_rows, key_rows, value_rows = operands
        return attend_column(query_rows, key_rows, value_rows, bias_full, key_bias)

    attended = lax.map(
        one_column,
        (jnp.swapaxes(query_all, 0, 1), jnp.swapaxes(key_all, 0, 1), jnp.swapaxes(value_all, 0, 1)),
    )
    attended = jnp.swapaxes(attended, 0, 1).reshape(total * slab, width)
    gated = (jax.nn.sigmoid(gate_all.astype(jnp.float32)) * attended).astype(jnp.bfloat16)
    update = jnp.dot(gated, w_out, preferred_element_type=jnp.float32)
    updated = (pair_cols.reshape(-1, width).astype(jnp.float32) + update).astype(jnp.bfloat16)
    updated = updated.reshape(total, slab, width)
    pieces = updated.reshape(n_cols, n_rows, slab, slab, width).transpose(1, 0, 2, 3, 4)
    flat_pieces = pieces.reshape(n_rows * n_cols, slab, slab, width)
    moved = lax.all_to_all(flat_pieces, ("row", "col"), split_axis=0, concat_axis=0, tiled=True)
    moved = moved.reshape(n_rows, n_cols, slab, slab, width)
    mirrored = moved.transpose(1, 0, 3, 2, 4).reshape(total, slab, width)
    logits_cols = error_logits(updated, mirrored, w_pae, w_pde)
    return lax.all_to_all(
        logits_cols.astype(jnp.bfloat16), "row", split_axis=0, concat_axis=1, tiled=True
    ).astype(logits_cols.dtype)


def solution(mesh):
    in_specs = (
        P("row", "col", None),
        P(None, ("row", "col")),
        P(("row", "col")),
        P(),
        P(),
        P(),
        P(),
        P(),
        P(),
    )
    out_specs = P("row", "col", None)
    return jax.shard_map(
        per_device, mesh=mesh, in_specs=in_specs, out_specs=out_specs, check_vma=False
    )
```

profile of v0, /device:TPU:4, one launch (start us, length us, event | category | flops | bytes accessed | tf_op | source)
XLA Modules:
  0.0 581.6 jit_solution(11121970672807428057)
XLA Ops:
  6.5 68.0 %all-gather = s32[32,16,3]{1,2,0:T(4,128)S(1)} all-gather(s32[1,16,3]{1,2,0:T(4,128)} %bitcast.112), channel_id=1, replica_groups=mesh['row'=8,'col'=4] {'row','col'}, dimensions={0}, use_global_device_ids=true | all-gather | bytes 6336 | tf_op jit(solution)/shard_map/all_gather | solution.py:60
  79.3 29.1 %all_to_all.23 = bf16[64,128,128]{2,0,1:T(8,128)(2,1)S(1)} all-to-all(bf16[64,128,128]{2,0,1:T(8,128)(2,1)S(1)} %copy.116), channel_id=1, replica_groups=mesh['row'=8,'col'=4] {'row'}, dimensions={1} | all-to-all | bytes 4194304 | tf_op jit(solution)/shard_map/all_to_all | solution.py:85
  130.6 38.8 %all-reduce = s32[512]{0:T(512)S(1)} all-reduce(s32[512]{0:T(512)S(1)} %dynamic-update-slice), channel_id=1, replica_groups=mesh['row'=8,'col'=4] {'row','col'}, use_global_device_ids=true, to_apply=%add | all-reduce | flops 512 | bytes 4096
  169.7 6.1 %fusion.22 = bf16[8192,128]{1,0:T(8,128)(2,1)S(1)} fusion(f32[8,64,16,128]{3,2,1,0:T(8,128)} %copy-done.3, f32[8192]{0:T(1024)S(1)} %rsqrt.32, f32[8192]{0:T(1024)S(1)} %div.38), kind=kLoop, calls=%fused_computation.37 | loop fusion | flops 3145728 | bytes 6356992 | tf_op jit(solution)/shard_map/convert_element_type | solution.py:12
  175.8 8.2 %fusion.39 = (bf16[8192,512]{1,0:T(8,128)(2,1)S(1)}, f32[8192,512]{1,0:T(8,128)}) fusion(bf16[8192,128]{1,0:T(8,128)(2,1)S(1)} %fusion.22, bf16[128,512]{1,0:T(8,128)(2,1)S(1)} %copy-done), kind=kOutput, calls=%fused_computation.73 | convolution fusion | flops 1077936128 | bytes 27394048 | tf_op jit(solution)/shard_map/dot_general | solution.py:88
  187.9 6.2 %reshape.165 = bf16[512,16,4,32]{3,2,1,0:T(4,128)(2,1)} reshape(bf16[8192,128]{1,0:T(8,128)(2,1)S(1)} %get-tuple-element.129) | data formatting | bytes 4194304 | tf_op jit(solution)/shard_map/reshape | solution.py:95
  194.1 12.2 %copy.131 = bf16[16,512,4,32]{1,3,2,0:T(8,128)(2,1)} copy(bf16[16,512,4,32]{3,2,0,1:T(4,128)(2,1)} %bitcast.100) | data formatting | bytes 4194304 | tf_op jit(solution)/shard_map/while | solution.py:112
  208.8 6.1 %reshape.166 = bf16[512,16,4,32]{3,2,1,0:T(4,128)(2,1)} reshape(bf16[8192,128]{1,0:T(8,128)(2,1)S(1)} %fusion.18) | data formatting | bytes 4194304 | tf_op jit(solution)/shard_map/reshape | solution.py:92
  214.9 12.4 %copy.132 = bf16[16,512,4,32]{1,3,2,0:T(8,128)(2,1)} copy(bf16[16,512,4,32]{3,2,0,1:T(4,128)(2,1)} %bitcast.101) | data formatting | bytes 4194304 | tf_op jit(solution)/shard_map/while | solution.py:112
  227.3 6.1 %reshape.164 = bf16[512,16,4,32]{3,2,1,0:T(4,128)(2,1)} reshape(bf16[8192,128]{1,0:T(8,128)(2,1)S(1)} %copy-done.5) | data formatting | bytes 4194304 | tf_op jit(solution)/shard_map/reshape | solution.py:100
  233.4 10.8 %copy.130 = bf16[16,512,4,32]{1,3,2,0:T(8,128)(2,1)S(1)} copy(bf16[16,512,4,32]{3,2,0,1:T(4,128)(2,1)} %bitcast.102) | data formatting | bytes 4194304 | tf_op jit(solution)/shard_map/while | solution.py:112
  244.2 6.1 %all-gather.6.cloned.1.call-done = f32[4,512,512]{1,0,2:T(4,128)} async-done(((f32[4,512,128]{1,0,2:T(4,128)}), f32[4,512,512]{1,0,2:T(4,128)}) %all-gather.6.cloned.1.call-update) | async-done | bytes 4194320 | tf_op jit(solution)/shard_map/all_gather | solution.py:105
  255.6 179.9 %while.10 = (s32[]{:T(128)}, f32[16,512,4,32]{1,3,2,0:T(8,128)}, bf16[16,512,4,32]{1,3,2,0:T(8,128)(2,1)S(1)}, bf16[16,512,4,32]{1,3,2,0:T(8,128)(2,1)}, bf16[16...) while((s32[]{:T(128)}, f32[16,512,4,32]{1,3,2,0:T(8,128)}, ...), condition=%wide.region_7.0_spmd, body=%wide.region_4.7_spmd.sunk | while | flops 141560832 | bytes 38424696 | solution.py:112
  295.3 5.3 fusion.61
  317.7 5.3 fusion.61
  340.2 5.3 fusion.61
  362.7 5.3 fusion.61
  374.0 5.3 fusion.61
  418.9 5.3 fusion.61
  435.4 14.9 %copy.134 = f32[512,16,4,32]{3,2,1,0:T(4,128)} copy(f32[512,16,4,32]{0,3,2,1:T(8,128)} %bitcast.109) | data formatting | bytes 8388608 | tf_op jit(solution)/shard_map/transpose | solution.py:116
  450.3 13.5 %reshape.167 = f32[8192,128]{1,0:T(8,128)} reshape(f32[512,16,4,32]{3,2,1,0:T(4,128)} %copy.134) | data formatting | bytes 8388608 | tf_op jit(solution)/shard_map/reshape | solution.py:116
  463.8 5.6 convert_reduce_fusion
  474.7 47.4 %all-to-all-done.1 = bf16[32,16,16,128]{3,2,1,0:T(8,128)(2,1)} async-done(((bf16[32,16,16,128]{3,2,1,0:T(8,128)(2,1)}), bf16[32,16,16,128]{3,2,1,0:T(8,128)(2,1)}, u32[]{:S(2)}, u32[]{:S(2)}) %all-to-all-start.1) | async-done | bytes 2097184 | tf_op jit(solution)/shard_map/all_to_all | solution.py:123
  541.5 30.2 %all_to_all.24 = bf16[512,16,128]{2,1,0:T(8,128)(2,1)S(1)} all-to-all(bf16[512,16,128]{2,1,0:T(8,128)(2,1)} %bitcast.108), channel_id=1, replica_groups=mesh['row'=8,'col'=4] {'row'}, dimensions={0} | all-to-all | bytes 4194304 | tf_op jit(solution)/shard_map/all_to_all | solution.py:127
  (146 shorter events, 214.3 us)
Async XLA Ops:
  6.5 169.3 %copy-start = (bf16[128,512]{1,0:T(8,128)(2,1)S(1)}, bf16[128,512]{1,0:T(8,128)(2,1)}, u32[]{:S(2)}) copy-start(bf16[128,512]{1,0:T(8,128)(2,1)} %param.15) | copy-start | bytes 393220
  6.5 163.1 %all-gather.4.cloned.1.call-start = ((), (), s32[]{:S(2)}) async-start(), calls=%async_computation.3 | async-start | bytes 1179648 | tf_op jit(solution)/shard_map/all_gather | solution.py:104
  118.7 2.0 copy-start.3
  118.7 5.6 copy-start.7
  120.7 9.7 %copy-start.10 = (s32[16]{0:T(128)S(1)}, s32[16]{0:T(128)}, u32[]{:S(2)}) copy-start(s32[16]{0:T(128)} %param.13) | copy-start | bytes 196
  130.3 120.0 %all-gather.6.cloned.1.call-start = ((), (), s32[]{:S(2)}) async-start(), calls=%async_computation.4 | async-start | bytes 5242880 | tf_op jit(solution)/shard_map/all_gather | solution.py:105
  184.1 3.9 copy-start.4
  214.9 12.4 %copy-start.5 = (bf16[8192,128]{1,0:T(8,128)(2,1)S(1)}, bf16[8192,128]{1,0:T(8,128)(2,1)}, u32[]{:S(2)}) copy-start(bf16[8192,128]{1,0:T(8,128)(2,1)} %get-tuple-element.130) | copy-start | bytes 6291460
  258.8 1.9 copy-start.2
  270.0 1.9 copy-start.2
  292.5 1.9 copy-start.2
  303.7 1.9 copy-start.2
  315.0 1.9 copy-start.2
  326.2 1.9 copy-start.2
  348.7 1.9 copy-start.2
  360.0 1.9 copy-start.2
  393.7 1.9 copy-start.2
  404.9 1.9 copy-start.2
  427.4 1.9 copy-start.2
  450.3 13.5 %copy-start.8 = (bf16[128,128]{1,0:T(8,128)(2,1)S(1)}, bf16[128,128]{1,0:T(8,128)(2,1)}, u32[]{:S(2)}) copy-start(bf16[128,128]{1,0:T(8,128)(2,1)} %param.17) | copy-start | bytes 98308
  471.1 51.0 %all-to-all-start.1 = ((bf16[32,16,16,128]{3,2,1,0:T(8,128)(2,1)}), bf16[32,16,16,128]{3,2,1,0:T(8,128)(2,1)}, u32[]{:S(2)}, u32[]{:S(2)}) async-start(bf16[32,16,16,128]{3,2,1,0:T(8,128)(2,1)} %bitcast.107), calls=%async_computation.1 | async-start | bytes 4194304 | tf_op jit(solution)/shard_map/all_to_all | solution.py:123
  529.7 3.0 copy-start.9
  529.7 6.1 %copy-start.6 = (bf16[128,64]{0,1:T(8,128)(2,1)S(1)}, bf16[128,64]{0,1:T(8,128)(2,1)}, u32[]{:S(2)}) copy-start(bf16[128,64]{0,1:T(8,128)(2,1)} %param.19) | copy-start | bytes 49156
  571.7 3.0 copy-start.1
  (5 other events, 9.7 us)
Sparse Core Ops, SparseCore 0:
  130.4 20.7 all-gather.3
  169.8 80.4 all-gather.5
where the time goes:
time: 586 us; the launch traced here: 582 us
  blocking collectives  166 us (28%)
  matrix products  164 us (28%)
  local copies, waits for them, and re-layouts  139 us (24%)
  waiting for transfers between devices  53.6 us (9%)
  other arithmetic  41.8 us (7%)
  between operations  13.8 us (2%)
    dot_general x16, matrix products, one_block(): jnp.einsum('hki,khd->ihd', weights, value_rows, preferred_element_type=jn...  84.2 us
    all_gather x1, blocking collectives, per_device(): lax.all_gather(coords, ('row', 'col'), axis=1, tiled=True)  68 us
    dot_general x16, matrix products, one_block(): jnp.einsum('khd,ihd->hki', key_rows, query_block, preferred_element_type=...  51.5 us
    all_to_all x1, waiting for transfers between devices, per_device(): lax.all_to_all(flat_pieces, ('row', 'col'), split_axis=0, concat_axis=0,...  47.4 us
    while x4, local copies, waits for them, and re-layouts, per_device(): lax.map(one_column, (jnp.swapaxes(query_all, 0, 1), jnp.swapaxes(key_all,...  40.6 us
    unnamed x1, blocking collectives  38.8 us
    while x32, local copies, waits for them, and re-layouts  31 us
    all_to_all x1, blocking collectives, per_device(): lax.all_to_all(logits_cols.astype(jnp.bfloat16), 'row', split_axis=0, con...  30.2 us
  transfers between devices with their start and end apart: 3, of which 2 were waited for; matrix products, arithmetic and copies ran while one was open for 13% of the time, Pallas kernels for 0%

commit v1 on v0

v1 whole, which is shorter than its diff:
```python
import functools

import jax
import jax.numpy as jnp
from jax import lax
from jax.experimental import pallas as pl
from jax.experimental.pallas import tpu as pltpu
from jax.sharding import PartitionSpec as P

F32 = jnp.float32
BF16 = jnp.bfloat16
NT = (((1,), (1,)), ((), ()))
VMEM_LIMIT = 56 * 1024 * 1024


def normalise(values):
    average = jnp.mean(values, axis=-1, keepdims=True)
    centred = values - average
    variance = jnp.mean(centred * centred, axis=-1, keepdims=True)
    return (centred * lax.rsqrt(variance + 1e-05)).astype(BF16)


def pair_kernel(classes, slab, batch, row_coords, col_coords, low, high, z, w_dist, w_bias, pair, bias, wide, spread):
    rows_dev, cols_dev, width = z.shape
    heads = bias.shape[0]
    for axis in range(3):
        line = jnp.broadcast_to(col_coords[axis : axis + 1, :], (width, cols_dev))
        spread[axis] = jnp.transpose(line)

    def some_rows(step, carry):
        first = step * batch
        hots = []
        for at in range(batch):
            squared = jnp.zeros((cols_dev, width), F32)
            for axis in range(3):
                offset = spread[axis] - row_coords[axis, first + at].astype(F32)
                squared = squared + offset * offset
            inside = (squared > low[...]) & (squared <= high[...])
            hots.append(jnp.where(inside, 1.0, 0.0).astype(BF16))
        embedded = jnp.dot(jnp.concatenate(hots, axis=0), w_dist[...], preferred_element_type=F32)
        values = z[pl.ds(first, batch)].reshape(batch * cols_dev, width).astype(F32)
        rounded = (values + embedded).astype(BF16).astype(F32)
        wide[pl.ds(first * cols_dev, batch * cols_dev), :] = rounded
        normed = normalise(rounded)
        found = lax.dot_general(w_bias[...], normed, NT, preferred_element_type=F32)
        for at in range(batch):
            for head in range(heads):
                bias[head, pl.ds(first + at, 1), :] = found[head : head + 1, at * cols_dev : (at + 1) * cols_dev]
        return carry

    lax.fori_loop(0, rows_dev // batch, some_rows, 0)

    def some_cols(step, carry):
        for at in range(slab):
            column = wide[pl.ds(step * slab + at, rows_dev, stride=cols_dev), :]
            pair[step, at] = column.astype(BF16)
        return carry

    lax.fori_loop(0, cols_dev // slab, some_cols, 0)


def attention_kernel(heads, chunk, pair, bias, key_bias, w_key, w_rest, w_out, updated, biased):
    n_rows, _, rows_dev, width = pair.shape
    n_cols = bias.shape[1]
    cols_dev = bias.shape[4]
    total = n_rows * rows_dev
    head_dim = width // heads

    @pl.when(pl.program_id(0) == 0)
    def _():
        for head in range(heads):
            for block in range(n_cols):
                biased[head, :, block * cols_dev : (block + 1) * cols_dev] = (
                    bias[:, block, head].reshape(total, cols_dev) + key_bias[...]
                )

    values = pair[:, 0].reshape(total, width).astype(F32)
    normed = normalise(values)
    key = jnp.dot(normed, w_key[...], preferred_element_type=F32).astype(BF16)
    rest = lax.dot_general(w_rest[...], normed, NT, preferred_element_type=F32)
    query = (rest[:width] * head_dim ** (-0.5)).astype(BF16)
    value = rest[width : 2 * width].astype(BF16)
    gate = jax.nn.sigmoid(rest[2 * width :].astype(BF16).astype(F32))
    ones = jnp.ones((16, total), BF16)
    parts = []
    for head in range(heads):
        lo, hi = head * head_dim, (head + 1) * head_dim
        pieces = []
        if lo:
            pieces.append(jnp.zeros((lo, total), BF16))
        pieces.append(query[lo:hi])
        if hi < width:
            pieces.append(jnp.zeros((width - hi, total), BF16))
        own_query = jnp.concatenate(pieces, axis=0)
        own_value = jnp.concatenate([value[lo:hi], ones], axis=0)
        lanes = []
        for first in range(0, total, chunk):
            score = jnp.dot(key, own_query[:, first : first + chunk], preferred_element_type=F32)
            score = score + biased[head, :, first : first + chunk]
            highest = jnp.max(score, axis=0, keepdims=True)
            raised = jnp.exp(score - highest).astype(BF16)
            summed = jnp.dot(own_value, raised, preferred_element_type=F32)
            lanes.append(summed[:head_dim] / summed[head_dim : head_dim + 1])
        parts.append(jnp.concatenate(lanes, axis=1))
    attended = jnp.concatenate(parts, axis=0)
    gated = (gate * attended).astype(BF16)
    update = jnp.dot(w_out[...], gated, preferred_element_type=F32)
    result = (values + jnp.transpose(update)).astype(BF16)
    updated[:, 0] = result.reshape(n_rows, rows_dev, width)


def logits_kernel(spots, own, mirrored, w_both, logits, wide):
    slab = mirrored.shape[2]
    rows_dev, width = mirrored.shape[3], mirrored.shape[4]
    cols_dev = logits.shape[1]
    pieces = cols_dev // rows_dev
    block = pl.program_id(0)

    @pl.when(block == 0)
    def _():
        wide[...] = own[...].reshape(cols_dev * rows_dev, width).astype(F32)

    first = spots[block] * slab
    for at in range(slab):
        mine = wide[pl.ds(first + at, cols_dev, stride=rows_dev), :]
        other = mirrored[0, :, at].reshape(cols_dev, width).astype(F32)
        both = jnp.concatenate([normalise(mine), normalise(mine + other)], axis=1)
        logits[at] = jnp.dot(both, w_both[...], preferred_element_type=F32)


def per_device(z_trunk, coords, token_mask, w_dist, w_attn, w_bias, w_out, w_pae, w_pde):
    rows_dev, cols_dev, width = z_trunk.shape
    n_rows, n_cols = lax.axis_size("row"), lax.axis_size("col")
    devices = n_rows * n_cols
    total = rows_dev * n_rows
    slab = rows_dev // n_cols
    heads = w_bias.shape[1]
    classes = w_dist.shape[0]
    share = coords.shape[1]
    both_axes = ("row", "col")
    row_at, col_at = lax.axis_index("row"), lax.axis_index("col")

    tokens = jnp.concatenate([coords, token_mask[None, :]], axis=0)
    copies = jnp.broadcast_to(tokens[None], (devices,) + tokens.shape)
    spread = lax.all_to_all(copies, both_axes, split_axis=0, concat_axis=0, tiled=True)
    tokens = spread.transpose(1, 0, 2).reshape(4, total)
    row_coords = lax.dynamic_slice_in_dim(tokens, row_at * rows_dev, rows_dev, 1)
    col_coords = lax.dynamic_slice_in_dim(tokens, col_at * cols_dev, cols_dev, 1).astype(F32)
    key_bias = jnp.broadcast_to(
        ((tokens[3].astype(F32) - 1.0) * 30000.0)[:, None], (total, cols_dev)
    )

    edges = (27.0 + 4.0 * jnp.arange(classes - 1, dtype=F32)) ** 2
    low = jnp.concatenate([jnp.full((1,), -1.0, F32), edges, jnp.full((width - classes,), 1e9, F32)])
    high = jnp.concatenate([edges, jnp.full((width - classes + 1,), 1e9, F32)])
    w_dist_full = jnp.pad(w_dist, ((0, width - classes), (0, 0)))
    w_bias_t = jnp.pad(w_bias.T, ((0, 16 - heads), (0, 0)))

    vmem = pl.BlockSpec(memory_space=pltpu.VMEM)
    smem = pl.BlockSpec(memory_space=pltpu.SMEM)
    pair, bias = pl.pallas_call(
        functools.partial(pair_kernel, classes, slab, 4),
        out_shape=(
            jax.ShapeDtypeStruct((n_rows, slab, rows_dev, width), BF16),
            jax.ShapeDtypeStruct((heads, rows_dev, cols_dev), F32),
        ),
        in_specs=[smem] + [vmem] * 6,
        out_specs=(vmem, vmem),
        scratch_shapes=[
            pltpu.VMEM((rows_dev * cols_dev, width), F32),
            pltpu.VMEM((3, cols_dev, width), F32),
        ],
        compiler_params=pltpu.CompilerParams(vmem_limit_bytes=VMEM_LIMIT),
        name="pair_kernel",
    )(row_coords, col_coords, low[None], high[None], z_trunk, w_dist_full, w_bias_t)

    bias = lax.all_gather(bias, "col", axis=0, tiled=False)
    bias = lax.all_gather(bias, "row", axis=0, tiled=False)
    pair = lax.all_to_all(pair, "row", split_axis=0, concat_axis=0, tiled=True)

    w_key = w_attn[:, width : 2 * width]
    w_rest = jnp.concatenate(
        [w_attn[:, :width], w_attn[:, 2 * width : 3 * width], w_attn[:, 3 * width :]], axis=1
    ).T
    whole = lambda shape: pl.BlockSpec(shape, lambda j: (0,) * len(shape))
    column = pl.BlockSpec((n_rows, 1, rows_dev, width), lambda j: (0, j, 0, 0))
    updated = pl.pallas_call(
        functools.partial(attention_kernel, heads, 2 * cols_dev),
        out_shape=jax.ShapeDtypeStruct(pair.shape, BF16),
        grid=(slab,),
        in_specs=[
            column,
            whole(bias.shape),
            whole(key_bias.shape),
            whole(w_key.shape),
            whole(w_rest.shape),
            whole(w_out.shape),
        ],
        out_specs=column,
        scratch_shapes=[pltpu.VMEM((heads, total, total), F32)],
        compiler_params=pltpu.CompilerParams(vmem_limit_bytes=VMEM_LIMIT),
        name="attention_kernel",
    )(pair, bias, key_bias, w_key, w_rest, w_out.T)

    per_tile = n_rows // n_cols
    got = []
    for shift in range(n_cols):
        hops = []
        for r in range(n_rows):
            for c in range(n_cols):
                to = (per_tile * c + r // n_cols) * n_cols + (r % n_cols + shift) % n_cols
                hops.append((r * n_cols + c, to))
        part = lax.dynamic_slice_in_dim(
            updated, per_tile * ((row_at % n_cols + shift) % n_cols), per_tile, 0
        )
        got.append(lax.ppermute(part, both_axes, hops))
    mirrored = jnp.stack(got)
    spots = (col_at - jnp.arange(n_cols, dtype=jnp.int32)) % n_cols
    own = lax.all_to_all(updated, "row", split_axis=0, concat_axis=0, tiled=True)

    bins = w_pae.shape[1]
    w_both = jnp.concatenate(
        [jnp.pad(w_pae, ((0, 0), (0, bins))), jnp.pad(w_pde, ((0, 0), (bins, 0)))], axis=0
    )
    logits = pl.pallas_call(
        logits_kernel,
        out_shape=jax.ShapeDtypeStruct((rows_dev, cols_dev, 2 * bins), F32),
        grid_spec=pltpu.PrefetchScalarGridSpec(
            num_scalar_prefetch=1,
            grid=(n_cols,),
            in_specs=[
                pl.BlockSpec(own.shape, lambda b, at: (0, 0, 0, 0)),
                pl.BlockSpec((1,) + mirrored.shape[1:], lambda b, at: (b, 0, 0, 0, 0)),
                pl.BlockSpec(w_both.shape, lambda b, at: (0, 0)),
            ],
            out_specs=pl.BlockSpec((slab, cols_dev, 2 * bins), lambda b, at: (at[b], 0, 0)),
            scratch_shapes=[pltpu.VMEM((cols_dev * rows_dev, width), F32)],
        ),
        compiler_params=pltpu.CompilerParams(vmem_limit_bytes=VMEM_LIMIT),
        name="logits_kernel",
    )(spots, own, mirrored, w_both)
    return logits


def solution(mesh):
    in_specs = (
        P("row", "col", None),
        P(None, ("row", "col")),
        P(("row", "col")),
        P(),
        P(),
        P(),
        P(),
        P(),
        P(),
    )
    out_specs = P("row", "col", None)
    return jax.shard_map(
        per_device, mesh=mesh, in_specs=in_specs, out_specs=out_specs, check_vma=False
    )
```

time: 586 us -> 255 us (0.44)
  matrix products: 164 us -> 0 us
  blocking collectives: 166 us -> 16.4 us
  local copies, waits for them, and re-layouts: 139 us -> 7.95 us
  Pallas kernels: 0 us -> 92.1 us
  waiting for transfers between devices: 53.6 us -> 89.9 us
  other arithmetic: 41.8 us -> 5.53 us
  starting transfers between devices: 3.6 us -> 26.9 us
    dot_general x38 -> x0, matrix products: 164 us -> none  [the longest x16 84.2 us: one_block(): jnp.einsum('hki,khd->ihd', weights, value_rows, preferred_element_type=jn...]
    pallas_call x0 -> x3, Pallas kernels: none -> 92.1 us  [the longest x1 62 us: per_device(): pl.pallas_call(functools.partial(attention_kernel, heads, 2 * cols_dev),...]
    while x36 -> x0, local copies, waits for them, and re-layouts: 71.7 us -> none  [the longest x4 40.6 us: per_device(): lax.map(one_column, (jnp.swapaxes(query_all, 0, 1), jnp.swapaxes(key_all,...]
    all_to_all x2 -> x0, blocking collectives: 59.3 us -> none  [the longest x1 30.2 us: per_device(): lax.all_to_all(logits_cols.astype(jnp.bfloat16), 'row', split_axis=0, con...]
    all_gather x1, blocking collectives: 68 us -> 16.4 us  [per_device(): bias = lax.all_gather(bias, 'col', axis=0, tiled=False)]
    ppermute x0 -> x4, waiting for transfers between devices: none -> 45.5 us  [per_device(): got.append(lax.ppermute(part, both_axes, hops))]
    unnamed x1 -> x0, blocking collectives: 38.8 us -> none
    reshape x4 -> x1, local copies, waits for them, and re-layouts: 31.8 us -> 0.1 us  [per_device(): tokens = spread.transpose(1, 0, 2).reshape(4, total)]
  transfers between devices with their start and end apart: 3 -> 8, of which waited for: 2 -> 7; matrix products, arithmetic and copies ran while one was open for 13% -> 4% of each run, Pallas kernels for 0% -> 0%
where the time goes in v1:
time: 255 us; the launch traced here: 252 us
  Pallas kernels  92.1 us (36%)
  waiting for transfers between devices  89.9 us (35%)
  starting transfers between devices  26.9 us (11%)
  blocking collectives  16.4 us (6%)
  between operations  13.5 us (5%)
  local copies, waits for them, and re-layouts  7.95 us (3%)
  other arithmetic  5.53 us (2%)
    pallas_call x1, Pallas kernels, per_device(): pl.pallas_call(functools.partial(attention_kernel, heads, 2 * cols_dev),...  62 us
    ppermute x4, waiting for transfers between devices, per_device(): got.append(lax.ppermute(part, both_axes, hops))  45.5 us
    all_to_all x1, waiting for transfers between devices, per_device(): pair = lax.all_to_all(pair, 'row', split_axis=0, concat_axis=0, tiled=True)  29.5 us
    all_gather x1, blocking collectives, per_device(): bias = lax.all_gather(bias, 'col', axis=0, tiled=False)  16.4 us
    pallas_call x1, Pallas kernels, per_device(): pl.pallas_call(logits_kernel, out_shape=jax.ShapeDtypeStruct((rows_dev, c...  15.8 us
    pallas_call x1, Pallas kernels, per_device(): pl.pallas_call(functools.partial(pair_kernel, classes, slab, 4), out_shap...  14.3 us
    all_gather x1, waiting for transfers between devices, per_device(): bias = lax.all_gather(bias, 'row', axis=0, tiled=False)  11.8 us
    ppermute x4, starting transfers between devices, per_device(): got.append(lax.ppermute(part, both_axes, hops))  10.2 us
  transfers between devices with their start and end apart: 8, of which 7 were waited for; matrix products, arithmetic and copies ran while one was open for 4% of the time, Pallas kernels for 0%

profile of v1, /device:TPU:4, one launch (start us, length us, event | category | flops | bytes accessed | tf_op | source)
XLA Modules:
  0.0 252.3 jit_solution(14582049213016702835)
XLA Ops:
  6.5 0.7 pad_add_fusion
  7.9 6.1 %all-to-all-start = ((s32[32,4,16]{2,1,0:T(4,128)}), s32[32,4,16]{2,1,0:T(4,128)S(1)}, u32[]{:S(2)}, u32[]{:S(2)}) async-start(s32[32,4,16]{2,1,0:T(4,128)} %broadcast_in_dim.26), calls=%async_computation | async-start | bytes 131072 | tf_op jit(solution)/shard_map/all_to_all | solution.py:145
  14.7 1.3 pad.17.w_dist
  16.0 1.3 pad.18.w_bias
  17.3 3.1 %all-to-all-done = s32[32,4,16]{2,1,0:T(4,128)S(1)} async-done(((s32[32,4,16]{2,1,0:T(4,128)}), s32[32,4,16]{2,1,0:T(4,128)S(1)}, u32[]{:S(2)}, u32[]{:S(2)}) %all-to-all-start) | async-done | bytes 8224 | tf_op jit(solution)/shard_map/all_to_all | solution.py:145
  21.7 14.3 %pair_kernel.1 = (bf16[8,16,64,128]{3,2,1,0:T(8,128)(2,1)}, f32[4,64,128]{2,1,0:T(8,128)}) custom-call(s32[4,64]{1,0:T(4,128)} %constant_dynamic-slice_fusion.4.row_coords, f32[4,128]{1,0:T(4,128)} %dynamic-slice_convert_fusion.col_coords, f32[1,128]{1,0:T(1,128)} %get-tuple-element.16.low, f32[1,128]{1,0:T(1,128)} %get-tuple-element.15.high, ...), custom_call_target="tpu_custom_call" | custom-call | tf_op jit(solution)/shard_map/pair_kernel/pallas_call | solution.py:161
  36.0 16.4 %all-gather = f32[16,64,128]{2,1,0:T(8,128)} all-gather(f32[4,64,128]{2,1,0:T(8,128)} %get-tuple-element.8), channel_id=2, replica_groups=mesh['row'=8,'col'=4] {'col'}, dimensions={0}, use_global_device_ids=true | all-gather | bytes 655360 | tf_op jit(solution)/shard_map/all_gather | solution.py:177
  52.4 4.7 %all-to-all-start.1 = ((bf16[8,16,64,128]{3,2,1,0:T(8,128)(2,1)}), bf16[8,16,64,128]{3,2,1,0:T(8,128)(2,1)S(1)}, u32[]{:S(2)}, u32[]{:S(2)}) async-start(bf16[8,16,64,128]{3,2,1,0:T(8,128)(2,1)} %get-tuple-element.7), calls=%async_computation.1 | async-start | bytes 4194304 | tf_op jit(solution)/shard_map/all_to_all | solution.py:179
  58.0 0.7 copy.23
  59.5 29.5 %all-to-all-done.1.pair = bf16[8,16,64,128]{3,2,1,0:T(8,128)(2,1)S(1)} async-done(((bf16[8,16,64,128]{3,2,1,0:T(8,128)(2,1)}), bf16[8,16,64,128]{3,2,1,0:T(8,128)(2,1)S(1)}, u32[]{:S(2)}, u32[]{:S(2)}) %all-to-all-start.1) | async-done | bytes 2097184 | tf_op jit(solution)/shard_map/all_to_all | solution.py:179
  89.0 11.8 %all-gather.4.cloned.1.call-done = f32[32,4,64,128]{3,2,1,0:T(8,128)} async-done(((f32[4,4,64,128]{3,2,1,0:T(8,128)}), f32[32,4,64,128]{3,2,1,0:T(8,128)}) %all-gather.4.cloned.1.call-update) | async-done | bytes 4194320 | tf_op jit(solution)/shard_map/all_gather | solution.py:178
  100.8 0.9 broadcast_in_dim.30.key_bias
  101.7 62.0 %attention_kernel.1 = bf16[8,16,64,128]{3,2,1,0:T(8,128)(2,1)} custom-call(bf16[8,16,64,128]{3,2,1,0:T(8,128)(2,1)} %copy-done.1, f32[8,4,4,64,128]{4,3,2,1,0:T(8,128)} %bitcast.16, f32[512,128]{1,0:T(8,128)} %broadcast_in_dim.30.key_bias, bf16[128,128]{1,0:T(8,128)(2,1)} %get-tuple-element.14.w_key, bf16[384,128]{1,0:T(8,128)(2,1)} %maximum_bitcast_fusion.w_rest, ...), custom_call_target="tpu_custom_call" | custom-call | tf_op jit(solution)/shard_map/attention_kernel/pallas_call | solution.py:187
  163.7 5.9 %all-to-all-start.2 = ((bf16[8,16,64,128]{3,2,1,0:T(8,128)(2,1)}), bf16[8,16,64,128]{3,2,1,0:T(8,128)(2,1)}, u32[]{:S(2)}, u32[]{:S(2)}) async-start(bf16[8,16,64,128]{3,2,1,0:T(8,128)(2,1)} %attention_kernel.1), calls=%async_computation.2 | async-start | bytes 4194304 | tf_op jit(solution)/shard_map/all_to_all | solution.py:219
  169.6 1.2 constant_dynamic-slice_fusion.3
  170.8 3.2 %collective-permute-start.3 = (bf16[2,16,64,128]{3,2,1,0:T(8,128)(2,1)}, bf16[2,16,64,128]{3,2,1,0:T(8,128)(2,1)S(1)}, u32[]{:S(2)}, u32[]{:S(2)}) collective-permute-start(bf16[2,16,64,128]{3,2,1,0:T(8,128)(2,1)} %get-tuple-element.10), channel_id=1, source_target_pairs={{0,3},{1,11},{2,19},{3,27},{4,0},{5,8},{6,16},{7,24},{8,1},{9,9},{... | collective-permute-start | bytes 1572872 | tf_op jit(solution)/shard_map/ppermute | solution.py:216
  174.1 2.3 collective-permute-start.2
  176.3 2.6 %collective-permute-start.1 = (bf16[2,16,64,128]{3,2,1,0:T(8,128)(2,1)S(1)}, bf16[2,16,64,128]{3,2,1,0:T(8,128)(2,1)S(1)}, u32[]{:S(2)}, u32[]{:S(2)}) collective-permute-start(bf16[2,16,64,128]{3,2,1,0:T(8,128)(2,1)S(1)} %get-tuple-element.12), channel_id=1, source_target_pairs={{0,1},{1,9},{2,17},{3,25},{4,2},{5,10},{6,18},{7,26},{8,3},{9,11},... | collective-permute-start | bytes 1572872 | tf_op jit(solution)/shard_map/ppermute | solution.py:216
  179.0 2.1 collective-permute-start
  182.6 13.8 %collective-permute-done.3 = bf16[2,16,64,128]{3,2,1,0:T(8,128)(2,1)S(1)} collective-permute-done((bf16[2,16,64,128]{3,2,1,0:T(8,128)(2,1)}, bf16[2,16,64,128]{3,2,1,0:T(8,128)(2,1)S(1)}, u32[]{:S(2)}, u32[]{:S(2)}) %collective-permute-start.3) | collective-permute-done | bytes 524320 | tf_op jit(solution)/shard_map/ppermute | solution.py:216
  196.5 27.7 %collective-permute-done.2 = bf16[2,16,64,128]{3,2,1,0:T(8,128)(2,1)S(1)} collective-permute-done((bf16[2,16,64,128]{3,2,1,0:T(8,128)(2,1)}, bf16[2,16,64,128]{3,2,1,0:T(8,128)(2,1)S(1)}, u32[]{:S(2)}, u32[]{:S(2)}) %collective-permute-start.2) | collective-permute-done | bytes 524320 | tf_op jit(solution)/shard_map/ppermute | solution.py:216
  224.2 3.4 %collective-permute-done.1 = bf16[2,16,64,128]{3,2,1,0:T(8,128)(2,1)S(1)} collective-permute-done((bf16[2,16,64,128]{3,2,1,0:T(8,128)(2,1)S(1)}, bf16[2,16,64,128]{3,2,1,0:T(8,128)(2,1)S(1)}, u32[]{:S(2)}, u32[]{:S(2)}) %collective-permute-start.1) | collective-permute-done | bytes 524320 | tf_op jit(solution)/shard_map/ppermute | solution.py:216
  228.1 1.6 pad_maximum_fusion.mirrored
  229.7 15.8 %logits_kernel.1 = f32[64,128,128]{2,1,0:T(8,128)} custom-call(s32[4]{0:T(128)} %and_select_fusion.spots, bf16[8,16,64,128]{3,2,1,0:T(8,128)(2,1)} %all-to-all-done.2.own, bf16[4,2,16,64,128]{4,3,2,1,0:T(8,128)(2,1)} %pad_maximum_fusion.mirrored, bf16[256,128]{1,0:T(8,128)(2,1)} %fusion.2.w_both), custom_call_target="tpu_custom_call" | custom-call | tf_op jit(solution)/shard_map/logits_kernel/pallas_call | solution.py:225
  (36 shorter events, 6.4 us)
Async XLA Ops:
  7.9 12.5 %all-to-all-start = ((s32[32,4,16]{2,1,0:T(4,128)}), s32[32,4,16]{2,1,0:T(4,128)S(1)}, u32[]{:S(2)}, u32[]{:S(2)}) async-start(s32[32,4,16]{2,1,0:T(4,128)} %broadcast_in_dim.26), calls=%async_computation | async-start | bytes 131072 | tf_op jit(solution)/shard_map/all_to_all | solution.py:145
  14.0 86.9 %all-gather.4.cloned.1.call-start = ((), (), s32[]{:S(2)}) async-start(), calls=%async_computation.3 | async-start | bytes 4718592 | tf_op jit(solution)/shard_map/all_gather | solution.py:178
  52.4 4.8 %slice-start = ((bf16[128,512]{1,0:T(8,128)(2,1)}), bf16[128,256]{1,0:T(8,128)(2,1)S(1)}, s32[]{:S(2)}) async-start(bf16[128,512]{1,0:T(8,128)(2,1)} %param.13), calls=%async_computation.4 | async-start | bytes 131072 | tf_op jit(solution)/shard_map/slice | solution.py:183
  52.4 4.9 %copy-start.2 = (bf16[128,512]{1,0:T(8,128)(2,1)S(1)}, bf16[128,512]{1,0:T(8,128)(2,1)}, u32[]{:S(2)}) copy-start(bf16[128,512]{1,0:T(8,128)(2,1)} %param.13) | copy-start | bytes 393220
  52.4 5.6 %copy-start.3 = (bf16[128,128]{1,0:T(8,128)(2,1)S(1)}, bf16[128,128]{1,0:T(8,128)(2,1)}, u32[]{:S(2)}) copy-start(bf16[128,128]{1,0:T(8,128)(2,1)} %param.15) | copy-start | bytes 98308
  52.4 36.6 %all-to-all-start.1 = ((bf16[8,16,64,128]{3,2,1,0:T(8,128)(2,1)}), bf16[8,16,64,128]{3,2,1,0:T(8,128)(2,1)S(1)}, u32[]{:S(2)}, u32[]{:S(2)}) async-start(bf16[8,16,64,128]{3,2,1,0:T(8,128)(2,1)} %get-tuple-element.7), calls=%async_computation.1 | async-start | bytes 4194304 | tf_op jit(solution)/shard_map/all_to_all | solution.py:179
  89.0 12.7 %copy-start.1 = (bf16[8,16,64,128]{3,2,1,0:T(8,128)(2,1)}, bf16[8,16,64,128]{3,2,1,0:T(8,128)(2,1)S(1)}, u32[]{:S(2)}) copy-start(bf16[8,16,64,128]{3,2,1,0:T(8,128)(2,1)S(1)} %all-to-all-done.1.pair) | copy-start | bytes 6291460
  163.7 5.9 %copy-start = (bf16[8,16,64,128]{3,2,1,0:T(8,128)(2,1)S(1)}, bf16[8,16,64,128]{3,2,1,0:T(8,128)(2,1)}, u32[]{:S(2)}) copy-start(bf16[8,16,64,128]{3,2,1,0:T(8,128)(2,1)} %attention_kernel.1) | copy-start | bytes 6291460
  163.7 65.9 %all-to-all-start.2 = ((bf16[8,16,64,128]{3,2,1,0:T(8,128)(2,1)}), bf16[8,16,64,128]{3,2,1,0:T(8,128)(2,1)}, u32[]{:S(2)}, u32[]{:S(2)}) async-start(bf16[8,16,64,128]{3,2,1,0:T(8,128)(2,1)} %attention_kernel.1), calls=%async_computation.2 | async-start | bytes 4194304 | tf_op jit(solution)/shard_map/all_to_all | solution.py:219
  169.6 11.5 %copy-start.4 = (bf16[128,64]{0,1:T(8,128)(2,1)S(1)}, bf16[128,64]{0,1:T(8,128)(2,1)}, u32[]{:S(2)}) copy-start(bf16[128,64]{0,1:T(8,128)(2,1)} %param.17) | copy-start | bytes 49156
  169.6 11.6 %copy-start.5 = (bf16[128,64]{0,1:T(8,128)(2,1)S(1)}, bf16[128,64]{0,1:T(8,128)(2,1)}, u32[]{:S(2)}) copy-start(bf16[128,64]{0,1:T(8,128)(2,1)} %param.16) | copy-start | bytes 49156
  170.8 25.6 %collective-permute-start.3 = (bf16[2,16,64,128]{3,2,1,0:T(8,128)(2,1)}, bf16[2,16,64,128]{3,2,1,0:T(8,128)(2,1)S(1)}, u32[]{:S(2)}, u32[]{:S(2)}) collective-permute-start(bf16[2,16,64,128]{3,2,1,0:T(8,128)(2,1)} %get-tuple-element.10), channel_id=1, source_target_pairs={{0,3},{1,11},{2,19},{3,27},{4,0},{5,8},{6,16},{7,24},{8,1},{9,9},{... | collective-permute-start | bytes 1572872 | tf_op jit(solution)/shard_map/ppermute | solution.py:216
  174.1 50.1 %collective-permute-start.2 = (bf16[2,16,64,128]{3,2,1,0:T(8,128)(2,1)}, bf16[2,16,64,128]{3,2,1,0:T(8,128)(2,1)S(1)}, u32[]{:S(2)}, u32[]{:S(2)}) collective-permute-start(bf16[2,16,64,128]{3,2,1,0:T(8,128)(2,1)} %get-tuple-element.11), channel_id=1, source_target_pairs={{0,2},{1,10},{2,18},{3,26},{4,3},{5,11},{6,19},{7,27},{8,0},{9,8},... | collective-permute-start | bytes 1572872 | tf_op jit(solution)/shard_map/ppermute | solution.py:216
  176.3 51.3 %collective-permute-start.1 = (bf16[2,16,64,128]{3,2,1,0:T(8,128)(2,1)S(1)}, bf16[2,16,64,128]{3,2,1,0:T(8,128)(2,1)S(1)}, u32[]{:S(2)}, u32[]{:S(2)}) collective-permute-start(bf16[2,16,64,128]{3,2,1,0:T(8,128)(2,1)S(1)} %get-tuple-element.12), channel_id=1, source_target_pairs={{0,1},{1,9},{2,17},{3,25},{4,2},{5,10},{6,18},{7,26},{8,3},{9,11},... | collective-permute-start | bytes 1572872 | tf_op jit(solution)/shard_map/ppermute | solution.py:216
  179.0 49.1 %collective-permute-start = (bf16[2,16,64,128]{3,2,1,0:T(8,128)(2,1)S(1)}, bf16[2,16,64,128]{3,2,1,0:T(8,128)(2,1)S(1)}, u32[]{:S(2)}, u32[]{:S(2)}) collective-permute-start(bf16[2,16,64,128]{3,2,1,0:T(8,128)(2,1)S(1)} %get-tuple-element.9), channel_id=1, source_target_pairs={{0,0},{1,8},{2,16},{3,24},{4,1},{5,9},{6,17},{7,25},{8,2},{9,10},{... | collective-permute-start | bytes 1572872 | tf_op jit(solution)/shard_map/ppermute | solution.py:216
Sparse Core Ops, SparseCore 0:
  52.5 48.3 all-gather.3

commit v2 on v0

v2 whole, which is shorter than its diff:
```python
import functools

import jax
import jax.numpy as jnp
from jax import lax
from jax.experimental import pallas as pl
from jax.experimental.pallas import tpu as pltpu
from jax.sharding import PartitionSpec as P

F32 = jnp.float32
BF16 = jnp.bfloat16
NT = (((1,), (1,)), ((), ()))
VMEM_LIMIT = 56 * 1024 * 1024
AXES = ("row", "col")


def means(parts):
    width = parts[0].shape[-1]
    stacked = jnp.concatenate(parts, axis=1) if len(parts) > 1 else parts[0]
    return jnp.dot(stacked, jnp.full((stacked.shape[1], width), 1.0 / width, BF16), preferred_element_type=F32)


def normalise(values, parts):
    centred = values - means(parts)
    squares = centred * centred
    high = squares.astype(BF16)
    variance = means([high, (squares - high.astype(F32)).astype(BF16)])
    return (centred * lax.rsqrt(variance + 1e-05)).astype(BF16)


def embed(squares, low, high, w_dist, values):
    hots = []
    for squared in squares:
        inside = (squared > low[...]) & (squared <= high[...])
        hots.append(jnp.where(inside, 1.0, 0.0).astype(BF16))
    hot = jnp.concatenate(hots, axis=0) if len(hots) > 1 else hots[0]
    embedded = jnp.dot(hot, w_dist[...], preferred_element_type=F32)
    return (values + embedded).astype(BF16)


def squared_distance(spread, scalars, token):
    squared = None
    for axis in range(3):
        offset = spread[axis] - scalars[axis, token].astype(F32)
        squared = offset * offset if squared is None else squared + offset * offset
    return squared


def spread_lines(lines, spread):
    length, width = spread.shape[1:]
    for axis in range(3):
        for first in range(0, length, width):
            line = lines[axis : axis + 1, first : first + width].astype(F32)
            spread[axis, first : first + width] = jnp.transpose(jnp.broadcast_to(line, (width, width)))


def bias_kernel(batch, scalars, tokens, low, high, z, w_dist, w_bias, bias, found, spread):
    rows_dev, cols_dev, width = z.shape
    heads = found.shape[0]
    row_at, col_at = lax.axis_index("row"), lax.axis_index("col")
    spread_lines(tokens[:, pl.ds(pl.multiple_of(col_at * cols_dev, cols_dev), cols_dev)], spread)

    def some_rows(step, carry):
        first = step * batch
        values = z[pl.ds(first, batch)].reshape(batch * cols_dev, width).astype(F32)
        squares = [squared_distance(spread, scalars, row_at * rows_dev + first + at) for at in range(batch)]
        pair = embed(squares, low, high, w_dist, values)
        normed = normalise(pair.astype(F32), [pair])
        lines = lax.dot_general(w_bias[...], normed, NT, preferred_element_type=F32)
        for at in range(batch):
            for head in range(heads):
                found[head, pl.ds(first + at, 1), :] = lines[head : head + 1, at * cols_dev : (at + 1) * cols_dev]
        return carry

    lax.fori_loop(0, rows_dev // batch, some_rows, 0)
    swap = row_at % 2 == 1
    for duo in range(heads // 2):
        even, odd = found[2 * duo], found[2 * duo + 1]
        lines = jnp.concatenate([jnp.where(swap, odd, even), jnp.where(swap, even, odd)], axis=0)
        bias[duo] = jnp.transpose(lines)


def project_kernel(
    head_dim, batch, scalars, tokens, low, high, z, w_dist, w_key, w_rest, pair, key, query, value, gate, wide, spread
):
    total, slab, width = z.shape
    row_at, col_at = lax.axis_index("row"), lax.axis_index("col")
    cols_dev = spread.shape[2]
    half = cols_dev // 2

    @pl.when(pl.program_id(0) == 0)
    def _():
        spread_lines(tokens, spread)
        wide[...] = z[...].reshape(total * slab, width).astype(F32)

    first = pl.program_id(0) * batch
    own = col_at * cols_dev + row_at * slab + first
    values = jnp.concatenate([wide[pl.ds(first + at, total, stride=slab), :] for at in range(batch)], axis=0)
    squares = [squared_distance(spread, scalars, own + at) for at in range(batch)]
    rounded = embed(squares, low, high, w_dist, values)
    normed = normalise(rounded.astype(F32), [rounded])
    rest = jnp.dot(normed, w_rest[...], preferred_element_type=F32)
    odd_lane = lax.broadcasted_iota(jnp.int32, (1, width), 1) // head_dim % 2 == 1
    odd_row = lax.broadcasted_iota(jnp.int32, (width, 1), 0) // head_dim % 2 == 1
    for at in range(batch):
        rows = slice(at * total, (at + 1) * total)
        pair[at] = rounded[rows]
        query[at] = (rest[rows, :width] * head_dim ** (-0.5)).astype(BF16)
        gate[at] = rest[rows, 2 * width :].astype(BF16)
        values = rest[rows, width : 2 * width]
        swapped = []
        for start in range(0, total, 2 * half):
            swapped += [values[start + half : start + 2 * half], values[start : start + half]]
        value[at] = jnp.where(odd_lane, jnp.concatenate(swapped, axis=0), values).astype(BF16)
        lines = lax.dot_general(w_key[...], normed[rows], NT, preferred_element_type=F32)
        for start in range(0, total, 2 * half):
            block = lines[:, start : start + 2 * half]
            key[at, :, start : start + 2 * half] = jnp.where(odd_row, pltpu.roll(block, half, 1), block).astype(BF16)


def attention_kernel(heads, n_rows, tokens, key, query, value, gate, pair, w_out, *refs):
    bias = refs[:n_rows]
    updated, mirrored, biased, result = refs[n_rows], refs[n_rows + 1 : -2], refs[-2], refs[-1]
    width, total = key.shape[1:]
    n_cols, _, cols_dev, _ = bias[0].shape
    rows_dev = updated.shape[2]
    halves = n_rows // n_cols
    head_dim = width // heads
    row_at, col_at = lax.axis_index("row"), lax.axis_index("col")
    lane = lax.broadcasted_iota(jnp.int32, (1, width), 1)

    @pl.when(pl.program_id(0) == 0)
    def _():
        from_own = (lane < rows_dev) != (row_at % 2 == 1)
        for step in range(0, n_rows, 2):
            spot = (row_at ^ step) // 2
            start = pl.multiple_of(spot * cols_dev, cols_dev)
            mask = (tokens[3:4, pl.ds(start, cols_dev)].astype(F32) - 1.0) * 30000.0
            for duo in range(heads // 2):
                masks = [mask, jnp.concatenate([mask[:, rows_dev:], mask[:, :rows_dev]], axis=1)]
                for block in range(n_cols):
                    tiles = bias[step][block, duo], bias[step + 1][block, duo]
                    rows = pl.ds(pl.multiple_of((col_at ^ block) * cols_dev, cols_dev), cols_dev)
                    biased[spot, 2 * duo, rows] = jnp.where(from_own, tiles[0], tiles[1]) + masks[0]
                    biased[spot, 2 * duo + 1, rows] = jnp.where(from_own, tiles[1], tiles[0]) + masks[1]

    own_key, own_query = key[0], query[0]
    own_value = jnp.concatenate([value[0], jnp.ones((total, width), BF16)], axis=1)
    attended = jnp.zeros((total, width), F32)
    for head in range(heads):
        inside = lane // head_dim == head
        score = jnp.dot(jnp.where(inside, own_query, jnp.zeros((), BF16)), own_key, preferred_element_type=F32)
        score = score + jnp.concatenate([biased[spot, head] for spot in range(biased.shape[0])], axis=1)
        highest = jnp.max(score, axis=1, keepdims=True)
        raised = jnp.exp(score - highest).astype(BF16)
        summed = jnp.dot(raised, own_value, preferred_element_type=F32)
        attended = jnp.where(inside, summed[:, :width] / summed[:, width:], attended)
    gated = (jax.nn.sigmoid(gate[0].astype(F32)) * attended).astype(BF16)
    update = jnp.dot(gated, w_out[...], preferred_element_type=F32)
    result[...] = (pair[0].astype(F32) + update).astype(BF16).reshape(result.shape)
    updated[:, 0] = result[...]
    for shift in range(n_cols):
        block = (row_at % n_cols) ^ shift
        mirrored[shift][:, 0] = result[pl.ds(block * halves, halves)]


def logits_kernel(n_cols, rounds, *refs):
    own = refs[1 : 1 + rounds]
    mirrored = refs[1 + rounds : 1 + rounds + rounds * n_cols]
    w_both, logits, wide = refs[1 + rounds + rounds * n_cols :]
    n_rows, part, rows_dev, width = own[0].shape
    halves = n_rows // n_cols
    cols_dev = halves * rows_dev
    slab = rounds * part
    at_shift = pl.program_id(0)

    @pl.when(at_shift == 0)
    def _():
        size = part * rows_dev
        for row in range(n_rows):
            for step in range(rounds):
                first = (row * rounds + step) * size
                wide[first : first + size, :] = own[step][row].reshape(size, width).astype(F32)

    first = refs[0][at_shift] * slab
    for shift in range(n_cols):

        @pl.when(at_shift == shift)
        def _():
            for step in range(rounds):
                mine, other = [], []
                for at in range(part):
                    mine.append(wide[pl.ds(first + step * part + at, cols_dev, stride=rows_dev), :])
                    other += [mirrored[step * n_cols + shift][half, at] for half in range(halves)]
                mine, other = jnp.concatenate(mine, axis=0), jnp.concatenate(other, axis=0)
                mine_short = mine.astype(BF16)
                both = jnp.concatenate(
                    [normalise(mine, [mine_short]), normalise(mine + other.astype(F32), [mine_short, other])], axis=1
                )
                found = jnp.dot(both, w_both[...], preferred_element_type=F32)
                logits[step * part : (step + 1) * part] = found.reshape(part, cols_dev, found.shape[1])


def swap_over(array, axis, step, count):
    return lax.ppermute(array, axis, [(at, at ^ step) for at in range(count)])


def per_device(z_trunk, coords, token_mask, w_dist, w_attn, w_bias, w_out, w_pae, w_pde):
    rows_dev, cols_dev, width = z_trunk.shape
    n_rows, n_cols = lax.axis_size("row"), lax.axis_size("col")
    devices = n_rows * n_cols
    total = rows_dev * n_rows
    slab = rows_dev // n_cols
    halves = cols_dev // rows_dev
    heads = w_bias.shape[1]
    head_dim = width // heads
    classes = w_dist.shape[0]
    row_at, col_at = lax.axis_index("row"), lax.axis_index("col")
    params = pltpu.CompilerParams(vmem_limit_bytes=VMEM_LIMIT)
    vmem = pl.BlockSpec(memory_space=pltpu.VMEM)
    smem = pl.BlockSpec(memory_space=pltpu.SMEM)
    once = pl.Buffered(1)
    whole = lambda array: pl.BlockSpec(array.shape, lambda *at: (0,) * array.ndim, pipeline_mode=once)

    edges = (27.0 + 4.0 * jnp.arange(classes - 1, dtype=F32)) ** 2
    low = jnp.concatenate([jnp.full((1,), -1.0, F32), edges, jnp.full((width - classes,), 1e9, F32)])[None]
    high = jnp.concatenate([edges, jnp.full((width - classes + 1,), 1e9, F32)])[None]
    w_dist_full = jnp.pad(w_dist, ((0, width - classes), (0, 0)))
    w_bias_t = jnp.pad(w_bias.T, ((0, 16 - heads), (0, 0)))

    tokens = jnp.concatenate([coords, token_mask[None, :]], axis=0)
    copies = jnp.broadcast_to(tokens[None], (devices,) + tokens.shape)
    tokens = lax.all_to_all(copies, AXES, split_axis=0, concat_axis=0, tiled=True)
    tokens = tokens.transpose(1, 0, 2).reshape(4, total)
    z_parts = z_trunk.reshape(rows_dev, n_rows, slab, width).swapaxes(0, 1)
    z_parts, w_dist_full, w_bias_t = lax.optimization_barrier((z_parts, w_dist_full, w_bias_t))
    z_cols = lax.all_to_all(z_parts, "row", split_axis=0, concat_axis=0, tiled=True)
    z_cols = z_cols.reshape(total, slab, width)

    bias = pl.pallas_call(
        functools.partial(bias_kernel, 16),
        out_shape=jax.ShapeDtypeStruct((heads // 2, cols_dev, 2 * rows_dev), F32),
        in_specs=[smem] + [vmem] * 6,
        out_specs=vmem,
        scratch_shapes=[pltpu.VMEM((heads, rows_dev, cols_dev), F32), pltpu.VMEM((3, cols_dev, width), F32)],
        compiler_params=params,
        cost_estimate=pl.CostEstimate(flops=rows_dev * cols_dev * width * 300, bytes_accessed=1 << 22, transcendentals=0),
        name="bias_kernel",
    )(tokens, tokens, low, high, z_trunk, w_dist_full, w_bias_t)

    plane = jnp.stack([bias] + [swap_over(bias, "col", step, n_cols) for step in range(1, n_cols)])
    plane, z_cols = lax.optimization_barrier((plane, z_cols))
    held = {0: plane}
    for step in range(2, n_rows, 2):
        held[step] = swap_over(plane, "row", step, n_rows)

    w_key = w_attn[:, width : 2 * width].T
    w_rest = jnp.concatenate([w_attn[:, :width], w_attn[:, 2 * width :]], axis=1)
    batch = 4
    by_rows = pl.BlockSpec((batch, total, width), lambda j: (j, 0, 0))
    by_lanes = pl.BlockSpec((batch, width, total), lambda j: (j, 0, 0))
    rows_shape = jax.ShapeDtypeStruct((slab, total, width), BF16)
    lanes_shape = jax.ShapeDtypeStruct((slab, width, total), BF16)
    projected = pl.pallas_call(
        functools.partial(project_kernel, head_dim, batch),
        out_shape=(rows_shape, lanes_shape, rows_shape, rows_shape, rows_shape),
        grid=(slab // batch,),
        in_specs=[smem, whole(tokens), vmem, vmem, whole(z_cols), vmem, vmem, vmem],
        out_specs=(by_rows, by_lanes, by_rows, by_rows, by_rows),
        scratch_shapes=[pltpu.VMEM((total * slab, width), F32), pltpu.VMEM((3, total, width), F32)],
        compiler_params=params,
        cost_estimate=pl.CostEstimate(flops=total * slab * width * 2000, bytes_accessed=1 << 24, transcendentals=0),
        name="project_kernel",
    )(tokens, tokens, low, high, z_cols, w_dist_full, w_key, w_rest)
    far = [held[step] for step in range(2, n_rows, 2)]
    far, projected = lax.optimization_barrier((far, projected))
    for step, tile in zip(range(2, n_rows, 2), far):
        held[step] = tile
    for step in range(0, n_rows, 2):
        held[step + 1] = swap_over(held[step], "row", 1, n_rows)
    pair, key, query, value, gate = projected

    rounds = 2
    part = slab // rounds
    own, mirrored = [], []
    for step in range(rounds):
        rows_spec = pl.BlockSpec((1, total, width), lambda j, step=step: (j + step * part, 0, 0))
        lanes_spec = pl.BlockSpec((1, width, total), lambda j, step=step: (j + step * part, 0, 0))
        out_spec = lambda count: pl.BlockSpec((count, 1, rows_dev, width), lambda j: (0, j, 0, 0))
        out_shape = lambda count: jax.ShapeDtypeStruct((count, part, rows_dev, width), BF16)
        updated, *turned = pl.pallas_call(
            functools.partial(attention_kernel, heads, n_rows),
            out_shape=(out_shape(n_rows),) + (out_shape(halves),) * n_cols,
            grid=(part,),
            in_specs=[whole(tokens), lanes_spec, rows_spec, rows_spec, rows_spec, rows_spec, whole(w_out)]
            + [whole(plane)] * n_rows,
            out_specs=(out_spec(n_rows),) + (out_spec(halves),) * n_cols,
            scratch_shapes=[
                pltpu.VMEM((total // cols_dev, heads, total, cols_dev), F32),
                pltpu.VMEM((n_rows, rows_dev, width), BF16),
            ],
            compiler_params=params,
            cost_estimate=pl.CostEstimate(
                flops=4 * part * total * total * heads * 256,
                bytes_accessed=1 << 24,
                transcendentals=part * heads * total * total,
            ),
            name="attention_kernel",
        )(tokens, key, query, value, gate, pair, w_out, *[held[at] for at in range(n_rows)])
        if step:
            updated, turned, own, mirrored = lax.optimization_barrier((updated, turned, own, mirrored))
        own.append(lax.all_to_all(updated, "row", split_axis=0, concat_axis=0, tiled=True))
        for shift in range(n_cols):
            hops = []
            for r in range(n_rows):
                for c in range(n_cols):
                    to = (halves * c + r // n_cols) * n_cols + (r % n_cols ^ shift)
                    hops.append((r * n_cols + c, to))
            mirrored.append(lax.ppermute(turned[shift], AXES, hops))

    spots = jnp.stack([col_at ^ shift for shift in range(n_cols)]).astype(jnp.int32)
    bins = w_pae.shape[1]
    w_both = jnp.concatenate(
        [jnp.pad(w_pae, ((0, 0), (0, bins))), jnp.pad(w_pde, ((0, 0), (bins, 0)))], axis=0
    )
    return pl.pallas_call(
        functools.partial(logits_kernel, n_cols, rounds),
        out_shape=jax.ShapeDtypeStruct((rows_dev, cols_dev, 2 * bins), F32),
        grid_spec=pltpu.PrefetchScalarGridSpec(
            num_scalar_prefetch=1,
            grid=(n_cols,),
            in_specs=[whole(array) for array in own + mirrored + [w_both]],
            out_specs=pl.BlockSpec((slab, cols_dev, 2 * bins), lambda b, at: (at[b], 0, 0)),
            scratch_shapes=[pltpu.VMEM((cols_dev * rows_dev, width), F32)],
        ),
        compiler_params=params,
        name="logits_kernel",
    )(spots, *own, *mirrored, w_both)


def solution(mesh):
    in_specs = (
        P("row", "col", None),
        P(None, ("row", "col")),
        P(("row", "col")),
        P(),
        P(),
        P(),
        P(),
        P(),
        P(),
    )
    out_specs = P("row", "col", None)
    return jax.shard_map(
        per_device, mesh=mesh, in_specs=in_specs, out_specs=out_specs, check_vma=False
    )
```

time: 586 us -> 180 us (0.31)
  blocking collectives: 166 us -> 0 us
  matrix products: 164 us -> 0 us
  local copies, waits for them, and re-layouts: 139 us -> 8.65 us
  Pallas kernels: 0 us -> 69 us
  starting transfers between devices: 3.6 us -> 48.8 us
  other arithmetic: 41.8 us -> 4.3 us
  between operations: 13.8 us -> 0.33 us
    dot_general x38 -> x0, matrix products: 164 us -> none  [the longest x16 84.2 us: one_block(): jnp.einsum('hki,khd->ihd', weights, value_rows, preferred_element_type=jn...]
    while x36 -> x0, local copies, waits for them, and re-layouts: 71.7 us -> none  [the longest x4 40.6 us: per_device(): lax.map(one_column, (jnp.swapaxes(query_all, 0, 1), jnp.swapaxes(key_all,...]
    pallas_call x0 -> x5, Pallas kernels: none -> 69 us  [the longest x2 37.5 us: per_device(): pl.pallas_call(functools.partial(attention_kernel, heads, n_rows), out_sh...]
    all_gather x1 -> x0, blocking collectives: 68 us -> none  [per_device(): lax.all_gather(coords, ('row', 'col'), axis=1, tiled=True)]
    all_to_all x2 -> x0, blocking collectives: 59.3 us -> none  [the longest x1 30.2 us: per_device(): lax.all_to_all(logits_cols.astype(jnp.bfloat16), 'row', split_axis=0, con...]
    ppermute x0 -> x18, waiting for transfers between devices: none -> 44.6 us  [the longest x8 23 us: per_device(): mirrored.append(lax.ppermute(turned[shift], AXES, hops))]
    all_to_all x1 -> x4, waiting for transfers between devices: 47.4 us -> 3.57 us  [the longest x1 1.88 us: per_device(): lax.all_to_all(copies, AXES, split_axis=0, concat_axis=0, tiled=True)]
    unnamed x1 -> x0, blocking collectives: 38.8 us -> none
  transfers between devices with their start and end apart: 3 -> 22, of which waited for: 2 -> 12; matrix products, arithmetic and copies ran while one was open for 13% -> 5% of each run, Pallas kernels for 0% -> 21%
where the time goes in v2:
time: 180 us; the launch traced here: 179 us
  Pallas kernels  69 us (38%)
  starting transfers between devices  48.8 us (27%)
  waiting for transfers between devices  48.1 us (27%)
  local copies, waits for them, and re-layouts  8.65 us (5%)
  other arithmetic  4.3 us (2%)
    pallas_call x2, Pallas kernels, per_device(): pl.pallas_call(functools.partial(attention_kernel, heads, n_rows), out_sh...  37.5 us
    ppermute x8, waiting for transfers between devices, per_device(): mirrored.append(lax.ppermute(turned[shift], AXES, hops))  23 us
    ppermute x10, waiting for transfers between devices, swap_over(): return lax.ppermute(array, axis, [(at, at ^ step) for at in range(count)])  21.5 us
    ppermute x8, starting transfers between devices, per_device(): mirrored.append(lax.ppermute(turned[shift], AXES, hops))  20.6 us
    pallas_call x1, Pallas kernels, per_device(): pl.pallas_call(functools.partial(logits_kernel, n_cols, rounds), out_shap...  12.9 us
    pallas_call x1, Pallas kernels, per_device(): pl.pallas_call(functools.partial(project_kernel, head_dim, batch), out_sh...  10.9 us
    all_to_all x2, starting transfers between devices, per_device(): lax.all_to_all(updated, 'row', split_axis=0, concat_axis=0, tiled=True)  8.82 us
    ppermute x10, starting transfers between devices, swap_over(): return lax.ppermute(array, axis, [(at, at ^ step) for at in range(count)])  8.39 us
  transfers between devices with their start and end apart: 22, of which 12 were waited for; matrix products, arithmetic and copies ran while one was open for 5% of the time, Pallas kernels for 21%

profile of v2, /device:TPU:4, one launch (start us, length us, event | category | flops | bytes accessed | tf_op | source)
XLA Modules:
  0.0 179.2 jit_solution(1120959006063233651)
XLA Ops:
  1.3 6.1 %all-to-all-start = ((s32[32,4,16]{2,1,0:T(4,128)}), s32[32,4,16]{2,1,0:T(4,128)S(1)}, u32[]{:S(2)}, u32[]{:S(2)}) async-start(s32[32,4,16]{2,1,0:T(4,128)} %broadcast_in_dim.20), calls=%async_computation | async-start | bytes 131072 | tf_op jit(solution)/shard_map/all_to_all | solution.py:233
  7.5 3.3 %copy.25 = bf16[64,8,16,128]{3,2,0,1:T(8,128)(2,1)} copy(bf16[64,8,16,128]{3,2,1,0:T(8,128)(2,1)} %bitcast.21) | data formatting | bytes 4194304 | tf_op jit(solution)/shard_map/reshape | solution.py:235
  13.8 4.9 %all-to-all-start.1 = ((bf16[8,64,16,128]{3,2,1,0:T(8,128)(2,1)}), bf16[8,64,16,128]{3,2,1,0:T(8,128)(2,1)S(1)}, u32[]{:S(2)}, u32[]{:S(2)}) async-start(bf16[8,64,16,128]{3,2,1,0:T(8,128)(2,1)} %bitcast.20), calls=%async_computation.1 | async-start | bytes 4194304 | tf_op jit(solution)/shard_map/all_to_all | solution.py:237
  20.1 7.8 %bias_kernel.1 = f32[2,128,128]{2,1,0:T(8,128)} custom-call(s32[4,512]{1,0:T(4,128)} %reshape.10.scalars.tokens, s32[4,512]{1,0:T(4,128)} %reshape.10.scalars.tokens, f32[1,128]{1,0:T(1,128)} %get-tuple-element.84.low, f32[1,128]{1,0:T(1,128)} %get-tuple-element.83.high, bf16[64,128,128]{2,1,0:T(8,128)(2,1)} %z.1, bf16[128,128]{1,0:T(8,128)(2,1)} %pad.17.w_dist, ...), custom_call_target="tpu_custom_call" | custom-call | flops 314572800 | bytes 4194304 | tf_op jit(solution)/shard_map/bias_kernel/pallas_call | solution.py:240
  29.3 3.0 %collective-permute-start.2 = (f32[2,128,128]{2,1,0:T(8,128)}, f32[2,128,128]{2,1,0:T(8,128)S(1)}, u32[]{:S(2)}, u32[]{:S(2)}) collective-permute-start(f32[2,128,128]{2,1,0:T(8,128)} %bias_kernel.1), channel_id=1, source_target_pairs={{0,3},{1,2},{2,1},{3,0},{4,7},{5,6},{6,5},{7,4},{8,11},{9,10},{10,... | collective-permute-start | bytes 393224 | tf_op jit(solution)/shard_map/ppermute | solution.py:205
  32.3 3.2 %collective-permute-done = f32[2,128,128]{2,1,0:T(8,128)S(1)} collective-permute-done((f32[2,128,128]{2,1,0:T(8,128)}, f32[2,128,128]{2,1,0:T(8,128)S(1)}, u32[]{:S(2)}, u32[]{:S(2)}) %collective-permute-start) | collective-permute-done | bytes 131104 | tf_op jit(solution)/shard_map/ppermute | solution.py:205
  35.5 5.7 %collective-permute-done.1 = f32[2,128,128]{2,1,0:T(8,128)S(1)} collective-permute-done((f32[2,128,128]{2,1,0:T(8,128)}, f32[2,128,128]{2,1,0:T(8,128)S(1)}, u32[]{:S(2)}, u32[]{:S(2)}) %collective-permute-start.1) | collective-permute-done | bytes 131104 | tf_op jit(solution)/shard_map/ppermute | solution.py:205
  48.8 10.9 %project_kernel.1 = (bf16[16,512,128]{2,1,0:T(8,128)(2,1)}, bf16[16,128,512]{2,1,0:T(8,128)(2,1)}, bf16[16,512,128]{2,1,0:T(8,128)(2,1)}, bf16[16,512,128]{2,1,0:T(8,128)(2,1)}, bf16[16,512,128]{2,1,0:T(8,128)(2,1)}) custom-call(s32[4,512]{1,0:T(4,128)} %reshape.10.scalars.tokens, s32[4,512]{1,0:T(4,128)} %reshape.10.scalars.tokens, ...), custom_call_target="tpu_custom_call" | custom-call | flops 2097152000 | bytes 16777216 | tf_op jit(solution)/shard_map/project_kernel/pallas_call | solution.py:264
  59.7 9.5 %collective-permute-done.4.refs_4_ = f32[4,2,128,128]{3,2,1,0:T(8,128)} collective-permute-done((f32[4,2,128,128]{3,2,1,0:T(8,128)S(1)}, f32[4,2,128,128]{3,2,1,0:T(8,128)}, u32[]{:S(2)}, u32[]{:S(2)}) %collective-permute-start.4) | collective-permute-done | bytes 524320 | tf_op jit(solution)/shard_map/ppermute | solution.py:205
  69.7 2.1 %collective-permute-done.7.refs_3_ = f32[4,2,128,128]{3,2,1,0:T(8,128)S(1)} collective-permute-done((f32[4,2,128,128]{3,2,1,0:T(8,128)S(1)}, f32[4,2,128,128]{3,2,1,0:T(8,128)S(1)}, u32[]{:S(2)}, u32[]{:S(2)}) %collective-permute-start.7) | collective-permute-done | bytes 524320 | tf_op jit(solution)/shard_map/ppermute | solution.py:205
  73.7 18.7 %attention_kernel.3 = (bf16[8,8,64,128]{3,2,1,0:T(8,128)(2,1)}, bf16[2,8,64,128]{3,2,1,0:T(8,128)(2,1)}, bf16[2,8,64,128]{3,2,1,0:T(8,128)(2,1)}, bf16[2,8,64,128]{3,2,1,0:T(8,128)(2,1)}, bf16[2,8,64,128]{3,2,1,0:T(8,128)(2,1)}) custom-call(s32[4,512]{1,0:T(4,128)} %reshape.10.scalars.tokens, bf16[16,128,512]{2,1,0:T(8,128)(2,1)} %get-tuple-element.53.key, ...), custom_call_target="tpu_custom_call" | custom-call | flops 8589934592 | bytes 16777216 | tf_op jit(solution)/shard_map/attention_kernel/pallas_call | solution.py:291
  92.4 5.3 %all-to-all-start.2 = ((bf16[8,8,64,128]{3,2,1,0:T(8,128)(2,1)}), bf16[8,8,64,128]{3,2,1,0:T(8,128)(2,1)S(1)}, u32[]{:S(2)}, u32[]{:S(2)}) async-start(bf16[8,8,64,128]{3,2,1,0:T(8,128)(2,1)} %get-tuple-element.66), calls=%async_computation.2 | async-start | bytes 2097152 | tf_op jit(solution)/shard_map/all_to_all | solution.py:312
  97.7 2.0 %collective-permute-start.10 = (bf16[2,8,64,128]{3,2,1,0:T(8,128)(2,1)S(1)}, bf16[2,8,64,128]{3,2,1,0:T(8,128)(2,1)S(1)}, u32[]{:S(2)}, u32[]{:S(2)}) collective-permute-start(bf16[2,8,64,128]{3,2,1,0:T(8,128)(2,1)S(1)} %copy-done.22), channel_id=1, source_target_pairs={{0,0},{1,8},{2,16},{3,24},{4,1},{5,9},{6,17},{7,25},{8,2},{9,10},{... | collective-permute-start | bytes 786440 | tf_op jit(solution)/shard_map/ppermute | solution.py:319
  101.1 2.2 %collective-permute-start.12 = (bf16[2,8,64,128]{3,2,1,0:T(8,128)(2,1)S(1)}, bf16[2,8,64,128]{3,2,1,0:T(8,128)(2,1)S(1)}, u32[]{:S(2)}, u32[]{:S(2)}) collective-permute-start(bf16[2,8,64,128]{3,2,1,0:T(8,128)(2,1)S(1)} %copy-done.20), channel_id=1, source_target_pairs={{0,2},{1,10},{2,18},{3,26},{4,3},{5,11},{6,19},{7,27},{8,0},{9,8},... | collective-permute-start | bytes 786440 | tf_op jit(solution)/shard_map/ppermute | solution.py:319
  103.3 3.6 %collective-permute-start.13 = (bf16[2,8,64,128]{3,2,1,0:T(8,128)(2,1)S(1)}, bf16[2,8,64,128]{3,2,1,0:T(8,128)(2,1)S(1)}, u32[]{:S(2)}, u32[]{:S(2)}) collective-permute-start(bf16[2,8,64,128]{3,2,1,0:T(8,128)(2,1)S(1)} %copy-done.19), channel_id=1, source_target_pairs={{0,3},{1,11},{2,19},{3,27},{4,2},{5,10},{6,18},{7,26},{8,1},{9,9},... | collective-permute-start | bytes 786440 | tf_op jit(solution)/shard_map/ppermute | solution.py:319
  106.9 18.8 %attention_kernel.2 = (bf16[8,8,64,128]{3,2,1,0:T(8,128)(2,1)}, bf16[2,8,64,128]{3,2,1,0:T(8,128)(2,1)}, bf16[2,8,64,128]{3,2,1,0:T(8,128)(2,1)}, bf16[2,8,64,128]{3,2,1,0:T(8,128)(2,1)}, bf16[2,8,64,128]{3,2,1,0:T(8,128)(2,1)}) custom-call(s32[4,512]{1,0:T(4,128)} %reshape.10.scalars.tokens, bf16[16,128,512]{2,1,0:T(8,128)(2,1)} %get-tuple-element.53.key, ...), custom_call_target="tpu_custom_call" | custom-call | flops 8589934592 | bytes 16777216 | tf_op jit(solution)/shard_map/attention_kernel/pallas_call | solution.py:291
  125.8 2.2 %collective-permute-done.13.refs_6_ = bf16[2,8,64,128]{3,2,1,0:T(8,128)(2,1)S(1)} collective-permute-done((bf16[2,8,64,128]{3,2,1,0:T(8,128)(2,1)S(1)}, bf16[2,8,64,128]{3,2,1,0:T(8,128)(2,1)S(1)}, u32[]{:S(2)}, u32[]{:S(2)}) %collective-permute-start.13) | collective-permute-done | bytes 262176 | tf_op jit(solution)/shard_map/ppermute | solution.py:319
  128.0 3.5 %all-to-all-start.3 = ((bf16[8,8,64,128]{3,2,1,0:T(8,128)(2,1)}), bf16[8,8,64,128]{3,2,1,0:T(8,128)(2,1)S(1)}, u32[]{:S(2)}, u32[]{:S(2)}) async-start(bf16[8,8,64,128]{3,2,1,0:T(8,128)(2,1)} %get-tuple-element.72), calls=%async_computation.3 | async-start | bytes 2097152 | tf_op jit(solution)/shard_map/all_to_all | solution.py:312
  131.5 1.9 %collective-permute-start.14 = (bf16[2,8,64,128]{3,2,1,0:T(8,128)(2,1)}, bf16[2,8,64,128]{3,2,1,0:T(8,128)(2,1)S(1)}, u32[]{:S(2)}, u32[]{:S(2)}) collective-permute-start(bf16[2,8,64,128]{3,2,1,0:T(8,128)(2,1)} %get-tuple-element.77), channel_id=1, source_target_pairs={{0,0},{1,8},{2,16},{3,24},{4,1},{5,9},{6,17},{7,25},{8,2},{9,10},{... | collective-permute-start | bytes 786440 | tf_op jit(solution)/shard_map/ppermute | solution.py:319
  133.5 4.5 %collective-permute-start.15 = (bf16[2,8,64,128]{3,2,1,0:T(8,128)(2,1)}, bf16[2,8,64,128]{3,2,1,0:T(8,128)(2,1)}, u32[]{:S(2)}, u32[]{:S(2)}) collective-permute-start(bf16[2,8,64,128]{3,2,1,0:T(8,128)(2,1)} %get-tuple-element.78), channel_id=1, source_target_pairs={{0,1},{1,9},{2,17},{3,25},{4,0},{5,8},{6,16},{7,24},{8,3},{9,11},{... | collective-permute-start | bytes 786440 | tf_op jit(solution)/shard_map/ppermute | solution.py:319
  139.0 3.9 %collective-permute-start.17 = (bf16[2,8,64,128]{3,2,1,0:T(8,128)(2,1)}, bf16[2,8,64,128]{3,2,1,0:T(8,128)(2,1)}, u32[]{:S(2)}, u32[]{:S(2)}) collective-permute-start(bf16[2,8,64,128]{3,2,1,0:T(8,128)(2,1)} %get-tuple-element.80), channel_id=1, source_target_pairs={{0,3},{1,11},{2,19},{3,27},{4,2},{5,10},{6,18},{7,26},{8,1},{9,9},... | collective-permute-start | bytes 786440 | tf_op jit(solution)/shard_map/ppermute | solution.py:319
  144.5 10.3 %collective-permute-done.14.refs_7_ = bf16[2,8,64,128]{3,2,1,0:T(8,128)(2,1)S(1)} collective-permute-done((bf16[2,8,64,128]{3,2,1,0:T(8,128)(2,1)}, bf16[2,8,64,128]{3,2,1,0:T(8,128)(2,1)S(1)}, u32[]{:S(2)}, u32[]{:S(2)}) %collective-permute-start.14) | collective-permute-done | bytes 262176 | tf_op jit(solution)/shard_map/ppermute | solution.py:319
  154.8 10.0 %collective-permute-done.15.refs_8_ = bf16[2,8,64,128]{3,2,1,0:T(8,128)(2,1)} collective-permute-done((bf16[2,8,64,128]{3,2,1,0:T(8,128)(2,1)}, bf16[2,8,64,128]{3,2,1,0:T(8,128)(2,1)}, u32[]{:S(2)}, u32[]{:S(2)}) %collective-permute-start.15) | collective-permute-done | bytes 262176 | tf_op jit(solution)/shard_map/ppermute | solution.py:319
  166.3 12.9 %logits_kernel.1 = f32[64,128,128]{2,1,0:T(8,128)} custom-call(s32[4]{0:T(128)} %pad_add_fusion.1.refs_0_, bf16[8,8,64,128]{3,2,1,0:T(8,128)(2,1)} %copy-done, bf16[8,8,64,128]{3,2,1,0:T(8,128)(2,1)} %copy-done.1, bf16[2,8,64,128]{3,2,1,0:T(8,128)(2,1)} %copy-done.4, bf16[2,8,64,128]{3,2,1,0:T(8,128)(2,1)} %copy-done.5, bf16[2,8,64,128]{3,2,1,0:T(8,128)(2,1)} %copy-done.6, ...), custom_call_target="tpu_custom_call" | custom-call | tf_op jit(solution)/shard_map/logits_kernel/pallas_call | solution.py:326
  (91 shorter events, 22.5 us)
Async XLA Ops:
  1.3 12.5 %all-to-all-start = ((s32[32,4,16]{2,1,0:T(4,128)}), s32[32,4,16]{2,1,0:T(4,128)S(1)}, u32[]{:S(2)}, u32[]{:S(2)}) async-start(s32[32,4,16]{2,1,0:T(4,128)} %broadcast_in_dim.20), calls=%async_computation | async-start | bytes 131072 | tf_op jit(solution)/shard_map/all_to_all | solution.py:233
  13.8 30.1 %all-to-all-start.1 = ((bf16[8,64,16,128]{3,2,1,0:T(8,128)(2,1)}), bf16[8,64,16,128]{3,2,1,0:T(8,128)(2,1)S(1)}, u32[]{:S(2)}, u32[]{:S(2)}) async-start(bf16[8,64,16,128]{3,2,1,0:T(8,128)(2,1)} %bitcast.20), calls=%async_computation.1 | async-start | bytes 4194304 | tf_op jit(solution)/shard_map/all_to_all | solution.py:237
  27.9 7.6 %collective-permute-start = (f32[2,128,128]{2,1,0:T(8,128)}, f32[2,128,128]{2,1,0:T(8,128)S(1)}, u32[]{:S(2)}, u32[]{:S(2)}) collective-permute-start(f32[2,128,128]{2,1,0:T(8,128)} %bias_kernel.1), channel_id=1, source_target_pairs={{0,1},{1,0},{2,3},{3,2},{4,5},{5,4},{6,7},{7,6},{8,9},{9,8},{10,11... | collective-permute-start | bytes 393224 | tf_op jit(solution)/shard_map/ppermute | solution.py:205
  28.2 13.1 %collective-permute-start.1 = (f32[2,128,128]{2,1,0:T(8,128)}, f32[2,128,128]{2,1,0:T(8,128)S(1)}, u32[]{:S(2)}, u32[]{:S(2)}) collective-permute-start(f32[2,128,128]{2,1,0:T(8,128)} %bias_kernel.1), channel_id=1, source_target_pairs={{0,2},{1,3},{2,0},{3,1},{4,6},{5,7},{6,4},{7,5},{8,10},{9,11},{10,... | collective-permute-start | bytes 393224 | tf_op jit(solution)/shard_map/ppermute | solution.py:205
  29.3 12.0 %collective-permute-start.2 = (f32[2,128,128]{2,1,0:T(8,128)}, f32[2,128,128]{2,1,0:T(8,128)S(1)}, u32[]{:S(2)}, u32[]{:S(2)}) collective-permute-start(f32[2,128,128]{2,1,0:T(8,128)} %bias_kernel.1), channel_id=1, source_target_pairs={{0,3},{1,2},{2,1},{3,0},{4,7},{5,6},{6,5},{7,4},{8,11},{9,10},{10,... | collective-permute-start | bytes 393224 | tf_op jit(solution)/shard_map/ppermute | solution.py:205
  43.9 15.8 %collective-permute-start.3 = (f32[4,2,128,128]{3,2,1,0:T(8,128)S(1)}, f32[4,2,128,128]{3,2,1,0:T(8,128)S(1)}, u32[]{:S(2)}, u32[]{:S(2)}) collective-permute-start(f32[4,2,128,128]{3,2,1,0:T(8,128)S(1)} %pad_maximum_fusion.refs_0_), channel_id=1, source_target_pairs={{0,8},{4,12},{8,0},{12,4},{16,24},{20,28},{24,16},{28,20},{1,9},{5... | collective-permute-start | bytes 1572872 | tf_op jit(solution)/shard_map/ppermute | solution.py:205
  44.5 24.6 %collective-permute-start.4 = (f32[4,2,128,128]{3,2,1,0:T(8,128)S(1)}, f32[4,2,128,128]{3,2,1,0:T(8,128)}, u32[]{:S(2)}, u32[]{:S(2)}) collective-permute-start(f32[4,2,128,128]{3,2,1,0:T(8,128)S(1)} %pad_maximum_fusion.refs_0_), channel_id=1, source_target_pairs={{0,16},{4,20},{8,24},{12,28},{16,0},{20,4},{24,8},{28,12},{1,17},{... | collective-permute-start | bytes 1572872 | tf_op jit(solution)/shard_map/ppermute | solution.py:205
  45.9 23.3 %collective-permute-start.5 = (f32[4,2,128,128]{3,2,1,0:T(8,128)S(1)}, f32[4,2,128,128]{3,2,1,0:T(8,128)}, u32[]{:S(2)}, u32[]{:S(2)}) collective-permute-start(f32[4,2,128,128]{3,2,1,0:T(8,128)S(1)} %pad_maximum_fusion.refs_0_), channel_id=1, source_target_pairs={{0,24},{4,28},{8,16},{12,20},{16,8},{20,12},{24,0},{28,4},{1,25},{... | collective-permute-start | bytes 1572872 | tf_op jit(solution)/shard_map/ppermute | solution.py:205
  48.8 20.9 %collective-permute-start.6 = (f32[4,2,128,128]{3,2,1,0:T(8,128)S(1)}, f32[4,2,128,128]{3,2,1,0:T(8,128)S(1)}, u32[]{:S(2)}, u32[]{:S(2)}) collective-permute-start(f32[4,2,128,128]{3,2,1,0:T(8,128)S(1)} %pad_maximum_fusion.refs_0_), channel_id=1, source_target_pairs={{0,4},{4,0},{8,12},{12,8},{16,20},{20,16},{24,28},{28,24},{1,5},{5... | collective-permute-start | bytes 1572872 | tf_op jit(solution)/shard_map/ppermute | solution.py:205
  69.2 2.6 %collective-permute-start.7 = (f32[4,2,128,128]{3,2,1,0:T(8,128)S(1)}, f32[4,2,128,128]{3,2,1,0:T(8,128)S(1)}, u32[]{:S(2)}, u32[]{:S(2)}) collective-permute-start(f32[4,2,128,128]{3,2,1,0:T(8,128)S(1)} %collective-permute-done.3.refs_2_), channel_id=1, source_target_pairs={{0,4},{4,0},{8,12},{12,8},{16,20},{20,16},{24,28},{28,24},{1,5},{5... | collective-permute-start | bytes 1572872 | tf_op jit(solution)/shard_map/ppermute | solution.py:205
  69.2 2.9 %collective-permute-start.8 = (f32[4,2,128,128]{3,2,1,0:T(8,128)}, f32[4,2,128,128]{3,2,1,0:T(8,128)S(1)}, u32[]{:S(2)}, u32[]{:S(2)}) collective-permute-start(f32[4,2,128,128]{3,2,1,0:T(8,128)} %collective-permute-done.4.refs_4_), channel_id=1, source_target_pairs={{0,4},{4,0},{8,12},{12,8},{16,20},{20,16},{24,28},{28,24},{1,5},{5... | collective-permute-start | bytes 1572872 | tf_op jit(solution)/shard_map/ppermute | solution.py:205
  69.7 3.1 %collective-permute-start.9 = (f32[4,2,128,128]{3,2,1,0:T(8,128)}, f32[4,2,128,128]{3,2,1,0:T(8,128)S(1)}, u32[]{:S(2)}, u32[]{:S(2)}) collective-permute-start(f32[4,2,128,128]{3,2,1,0:T(8,128)} %collective-permute-done.5.refs_6_), channel_id=1, source_target_pairs={{0,4},{4,0},{8,12},{12,8},{16,20},{20,16},{24,28},{28,24},{1,5},{5... | collective-permute-start | bytes 1572872 | tf_op jit(solution)/shard_map/ppermute | solution.py:205
  92.4 35.7 %all-to-all-start.2 = ((bf16[8,8,64,128]{3,2,1,0:T(8,128)(2,1)}), bf16[8,8,64,128]{3,2,1,0:T(8,128)(2,1)S(1)}, u32[]{:S(2)}, u32[]{:S(2)}) async-start(bf16[8,8,64,128]{3,2,1,0:T(8,128)(2,1)} %get-tuple-element.66), calls=%async_computation.2 | async-start | bytes 2097152 | tf_op jit(solution)/shard_map/all_to_all | solution.py:312
  97.7 28.1 %collective-permute-start.10 = (bf16[2,8,64,128]{3,2,1,0:T(8,128)(2,1)S(1)}, bf16[2,8,64,128]{3,2,1,0:T(8,128)(2,1)S(1)}, u32[]{:S(2)}, u32[]{:S(2)}) collective-permute-start(bf16[2,8,64,128]{3,2,1,0:T(8,128)(2,1)S(1)} %copy-done.22), channel_id=1, source_target_pairs={{0,0},{1,8},{2,16},{3,24},{4,1},{5,9},{6,17},{7,25},{8,2},{9,10},{... | collective-permute-start | bytes 786440 | tf_op jit(solution)/shard_map/ppermute | solution.py:319
  99.7 26.1 %collective-permute-start.11 = (bf16[2,8,64,128]{3,2,1,0:T(8,128)(2,1)S(1)}, bf16[2,8,64,128]{3,2,1,0:T(8,128)(2,1)S(1)}, u32[]{:S(2)}, u32[]{:S(2)}) collective-permute-start(bf16[2,8,64,128]{3,2,1,0:T(8,128)(2,1)S(1)} %copy-done.21), channel_id=1, source_target_pairs={{0,1},{1,9},{2,17},{3,25},{4,0},{5,8},{6,16},{7,24},{8,3},{9,11},{... | collective-permute-start | bytes 786440 | tf_op jit(solution)/shard_map/ppermute | solution.py:319
  101.1 24.7 %collective-permute-start.12 = (bf16[2,8,64,128]{3,2,1,0:T(8,128)(2,1)S(1)}, bf16[2,8,64,128]{3,2,1,0:T(8,128)(2,1)S(1)}, u32[]{:S(2)}, u32[]{:S(2)}) collective-permute-start(bf16[2,8,64,128]{3,2,1,0:T(8,128)(2,1)S(1)} %copy-done.20), channel_id=1, source_target_pairs={{0,2},{1,10},{2,18},{3,26},{4,3},{5,11},{6,19},{7,27},{8,0},{9,8},... | collective-permute-start | bytes 786440 | tf_op jit(solution)/shard_map/ppermute | solution.py:319
  103.3 24.7 %collective-permute-start.13 = (bf16[2,8,64,128]{3,2,1,0:T(8,128)(2,1)S(1)}, bf16[2,8,64,128]{3,2,1,0:T(8,128)(2,1)S(1)}, u32[]{:S(2)}, u32[]{:S(2)}) collective-permute-start(bf16[2,8,64,128]{3,2,1,0:T(8,128)(2,1)S(1)} %copy-done.19), channel_id=1, source_target_pairs={{0,3},{1,11},{2,19},{3,27},{4,2},{5,10},{6,18},{7,26},{8,1},{9,9},... | collective-permute-start | bytes 786440 | tf_op jit(solution)/shard_map/ppermute | solution.py:319
  125.8 39.6 %copy-start.4 = (bf16[2,8,64,128]{3,2,1,0:T(8,128)(2,1)}, bf16[2,8,64,128]{3,2,1,0:T(8,128)(2,1)S(1)}, u32[]{:S(2)}) copy-start(bf16[2,8,64,128]{3,2,1,0:T(8,128)(2,1)S(1)} %collective-permute-done.10.refs_3_) | copy-start | bytes 786436
  125.8 39.5 %copy-start.5 = (bf16[2,8,64,128]{3,2,1,0:T(8,128)(2,1)}, bf16[2,8,64,128]{3,2,1,0:T(8,128)(2,1)S(1)}, u32[]{:S(2)}) copy-start(bf16[2,8,64,128]{3,2,1,0:T(8,128)(2,1)S(1)} %collective-permute-done.11.refs_4_) | copy-start | bytes 786436
  128.0 37.3 %all-to-all-start.3 = ((bf16[8,8,64,128]{3,2,1,0:T(8,128)(2,1)}), bf16[8,8,64,128]{3,2,1,0:T(8,128)(2,1)S(1)}, u32[]{:S(2)}, u32[]{:S(2)}) async-start(bf16[8,8,64,128]{3,2,1,0:T(8,128)(2,1)} %get-tuple-element.72), calls=%async_computation.3 | async-start | bytes 2097152 | tf_op jit(solution)/shard_map/all_to_all | solution.py:312
  131.5 23.2 %collective-permute-start.14 = (bf16[2,8,64,128]{3,2,1,0:T(8,128)(2,1)}, bf16[2,8,64,128]{3,2,1,0:T(8,128)(2,1)S(1)}, u32[]{:S(2)}, u32[]{:S(2)}) collective-permute-start(bf16[2,8,64,128]{3,2,1,0:T(8,128)(2,1)} %get-tuple-element.77), channel_id=1, source_target_pairs={{0,0},{1,8},{2,16},{3,24},{4,1},{5,9},{6,17},{7,25},{8,2},{9,10},{... | collective-permute-start | bytes 786440 | tf_op jit(solution)/shard_map/ppermute | solution.py:319
  133.5 31.3 %collective-permute-start.15 = (bf16[2,8,64,128]{3,2,1,0:T(8,128)(2,1)}, bf16[2,8,64,128]{3,2,1,0:T(8,128)(2,1)}, u32[]{:S(2)}, u32[]{:S(2)}) collective-permute-start(bf16[2,8,64,128]{3,2,1,0:T(8,128)(2,1)} %get-tuple-element.78), channel_id=1, source_target_pairs={{0,1},{1,9},{2,17},{3,25},{4,0},{5,8},{6,16},{7,24},{8,3},{9,11},{... | collective-permute-start | bytes 786440 | tf_op jit(solution)/shard_map/ppermute | solution.py:319
  138.0 26.8 %collective-permute-start.16 = (bf16[2,8,64,128]{3,2,1,0:T(8,128)(2,1)}, bf16[2,8,64,128]{3,2,1,0:T(8,128)(2,1)}, u32[]{:S(2)}, u32[]{:S(2)}) collective-permute-start(bf16[2,8,64,128]{3,2,1,0:T(8,128)(2,1)} %get-tuple-element.79), channel_id=1, source_target_pairs={{0,2},{1,10},{2,18},{3,26},{4,3},{5,11},{6,19},{7,27},{8,0},{9,8},... | collective-permute-start | bytes 786440 | tf_op jit(solution)/shard_map/ppermute | solution.py:319
  139.0 26.4 %collective-permute-start.17 = (bf16[2,8,64,128]{3,2,1,0:T(8,128)(2,1)}, bf16[2,8,64,128]{3,2,1,0:T(8,128)(2,1)}, u32[]{:S(2)}, u32[]{:S(2)}) collective-permute-start(bf16[2,8,64,128]{3,2,1,0:T(8,128)(2,1)} %get-tuple-element.80), channel_id=1, source_target_pairs={{0,3},{1,11},{2,19},{3,27},{4,2},{5,10},{6,18},{7,26},{8,1},{9,9},... | collective-permute-start | bytes 786440 | tf_op jit(solution)/shard_map/ppermute | solution.py:319
  (22 other events, 312.1 us)

commit v3 on v2

--- a/solution.py
+++ b/solution.py
@@ -25,6 +25,21 @@
     squares = centred * centred
     high = squares.astype(BF16)
     variance = means([high, (squares - high.astype(F32)).astype(BF16)])
+    return (centred * lax.rsqrt(variance + 1e-05)).astype(BF16)
+
+
+def normalise_pair(mine, other):
+    width = mine.shape[1]
+    row = lax.broadcasted_iota(jnp.int32, (2 * width, 2 * width), 0) < width
+    lane = lax.broadcasted_iota(jnp.int32, (2 * width, 2 * width), 1) < width
+    both_ways = jnp.where(jnp.logical_or(row, jnp.logical_not(lane)), 1.0 / width, 0.0).astype(BF16)
+    each_way = jnp.where(row == lane, 1.0 / width, 0.0).astype(BF16)
+    average = jnp.dot(jnp.concatenate([mine.astype(BF16), other], axis=1), both_ways, preferred_element_type=F32)
+    centred = jnp.concatenate([mine, mine + other.astype(F32)], axis=1) - average
+    squares = centred * centred
+    high = squares.astype(BF16)
+    rest = (squares - high.astype(F32)).astype(BF16)
+    variance = jnp.dot(high, each_way, preferred_element_type=F32) + jnp.dot(rest, each_way, preferred_element_type=F32)
     return (centred * lax.rsqrt(variance + 1e-05)).astype(BF16)
 
 
@@ -118,11 +133,12 @@
             key[at, :, start : start + 2 * half] = jnp.where(odd_row, pltpu.roll(block, half, 1), block).astype(BF16)
 
 
-def attention_kernel(heads, n_rows, tokens, key, query, value, gate, pair, w_out, *refs):
-    bias = refs[:n_rows]
-    updated, mirrored, biased, result = refs[n_rows], refs[n_rows + 1 : -2], refs[-2], refs[-1]
+def attention_kernel(heads, n_cols, splits, tokens, key, query, value, gate, pair, w_out, *refs):
+    n_rows, count = len(splits), sum(splits)
+    bias = [refs[sum(splits[:step]) : sum(splits[: step + 1])] for step in range(n_rows)]
+    updated, mirrored, biased, result = refs[count], refs[count + 1 : -2], refs[-2], refs[-1]
     width, total = key.shape[1:]
-    n_cols, _, cols_dev, _ = bias[0].shape
+    cols_dev = bias[0][0].shape[2]
     rows_dev = updated.shape[2]
     halves = n_rows // n_cols
     head_dim = width // heads
@@ -139,22 +155,27 @@
             for duo in range(heads // 2):
                 masks = [mask, jnp.concatenate([mask[:, rows_dev:], mask[:, :rows_dev]], axis=1)]
                 for block in range(n_cols):
-                    tiles = bias[step][block, duo], bias[step + 1][block, duo]
+                    piece, spot_in = divmod(block, n_cols // splits[step])
+                    tiles = bias[step][piece][spot_in, duo], bias[step + 1][piece][spot_in, duo]
                     rows = pl.ds(pl.multiple_of((col_at ^ block) * cols_dev, cols_dev), cols_dev)
                     biased[spot, 2 * duo, rows] = jnp.where(from_own, tiles[0], tiles[1]) + masks[0]
                     biased[spot, 2 * duo + 1, rows] = jnp.where(from_own, tiles[1], tiles[0]) + masks[1]
 
     own_key, own_query = key[0], query[0]
     own_value = jnp.concatenate([value[0], jnp.ones((total, width), BF16)], axis=1)
-    attended = jnp.zeros((total, width), F32)
+    blocks = [jnp.zeros((cols_dev, width), F32)] * (total // cols_dev)
     for head in range(heads):
         inside = lane // head_dim == head
-        score = jnp.dot(jnp.where(inside, own_query, jnp.zeros((), BF16)), own_key, preferred_element_type=F32)
-        score = score + jnp.concatenate([biased[spot, head] for spot in range(biased.shape[0])], axis=1)
-        highest = jnp.max(score, axis=1, keepdims=True)
-        raised = jnp.exp(score - highest).astype(BF16)
-        summed = jnp.dot(raised, own_value, preferred_element_type=F32)
-        attended = jnp.where(inside, summed[:, :width] / summed[:, width:], attended)
+        for at in range(len(blocks)):
+            rows = slice(at * cols_dev, (at + 1) * cols_dev)
+            own = jnp.where(inside, own_query[rows], jnp.zeros((), BF16))
+            score = jnp.dot(own, own_key, preferred_element_type=F32)
+            score = score + jnp.concatenate([biased[spot, head, rows] for spot in range(biased.shape[0])], axis=1)
+            highest = jnp.max(score, axis=1, keepdims=True)
+            raised = jnp.exp(score - highest).astype(BF16)
+            summed = jnp.dot(raised, own_value, preferred_element_type=F32)
+            blocks[at] = jnp.where(inside, summed[:, :width] / summed[:, width:], blocks[at])
+    attended = jnp.concatenate(blocks, axis=0)
     gated = (jax.nn.sigmoid(gate[0].astype(F32)) * attended).astype(BF16)
     update = jnp.dot(gated, w_out[...], preferred_element_type=F32)
     result[...] = (pair[0].astype(F32) + update).astype(BF16).reshape(result.shape)
@@ -193,10 +214,7 @@
                     mine.append(wide[pl.ds(first + step * part + at, cols_dev, stride=rows_dev), :])
                     other += [mirrored[step * n_cols + shift][half, at] for half in range(halves)]
                 mine, other = jnp.concatenate(mine, axis=0), jnp.concatenate(other, axis=0)
-                mine_short = mine.astype(BF16)
-                both = jnp.concatenate(
-                    [normalise(mine, [mine_short]), normalise(mine + other.astype(F32), [mine_short, other])], axis=1
-                )
+                both = normalise_pair(mine, other)
                 found = jnp.dot(both, w_both[...], preferred_element_type=F32)
                 logits[step * part : (step + 1) * part] = found.reshape(part, cols_dev, found.shape[1])
 
@@ -208,7 +226,6 @@
 def per_device(z_trunk, coords, token_mask, w_dist, w_attn, w_bias, w_out, w_pae, w_pde):
     rows_dev, cols_dev, width = z_trunk.shape
     n_rows, n_cols = lax.axis_size("row"), lax.axis_size("col")
-    devices = n_rows * n_cols
     total = rows_dev * n_rows
     slab = rows_dev // n_cols
     halves = cols_dev // rows_dev
@@ -229,7 +246,7 @@
     w_bias_t = jnp.pad(w_bias.T, ((0, 16 - heads), (0, 0)))
 
     tokens = jnp.concatenate([coords, token_mask[None, :]], axis=0)
-    copies = jnp.broadcast_to(tokens[None], (devices,) + tokens.shape)
+    copies = jnp.broadcast_to(tokens[None], (n_rows * n_cols,) + tokens.shape)
     tokens = lax.all_to_all(copies, AXES, split_axis=0, concat_axis=0, tiled=True)
     tokens = tokens.transpose(1, 0, 2).reshape(4, total)
     z_parts = z_trunk.reshape(rows_dev, n_rows, slab, width).swapaxes(0, 1)
@@ -249,10 +266,10 @@
     )(tokens, tokens, low, high, z_trunk, w_dist_full, w_bias_t)
 
     plane = jnp.stack([bias] + [swap_over(bias, "col", step, n_cols) for step in range(1, n_cols)])
-    plane, z_cols = lax.optimization_barrier((plane, z_cols))
-    held = {0: plane}
+    held = {0: [plane]}
     for step in range(2, n_rows, 2):
-        held[step] = swap_over(plane, "row", step, n_rows)
+        if step & (step - 1) == 0:
+            held[step] = [swap_over(plane, "row", step, n_rows)]
 
     w_key = w_attn[:, width : 2 * width].T
     w_rest = jnp.concatenate([w_attn[:, :width], w_attn[:, 2 * width :]], axis=1)
@@ -272,12 +289,19 @@
         cost_estimate=pl.CostEstimate(flops=total * slab * width * 2000, bytes_accessed=1 << 24, transcendentals=0),
         name="project_kernel",
     )(tokens, tokens, low, high, z_cols, w_dist_full, w_key, w_rest)
-    far = [held[step] for step in range(2, n_rows, 2)]
-    far, projected = lax.optimization_barrier((far, projected))
-    for step, tile in zip(range(2, n_rows, 2), far):
-        held[step] = tile
+    held, projected = lax.optimization_barrier((held, projected))
+    for step in range(2, n_rows, 2):
+        one = step & -step
+        if step != one:
+            cut = n_cols // 2
+            first, second = held[step ^ one], held[one]
+            first = first[0] if len(first) == 2 else first[0][:cut]
+            second = second[1] if len(second) == 2 else second[0][cut:]
+            held[step] = [swap_over(first, "row", one, n_rows), swap_over(second, "row", step ^ one, n_rows)]
     for step in range(0, n_rows, 2):
-        held[step + 1] = swap_over(held[step], "row", 1, n_rows)
+        held[step + 1] = [swap_over(tile, "row", 1, n_rows) for tile in held[step]]
+    splits = tuple(len(held[step]) for step in range(n_rows))
+    tiles = [tile for step in range(n_rows) for tile in held[step]]
     pair, key, query, value, gate = projected
 
     rounds = 2
@@ -289,11 +313,11 @@
         out_spec = lambda count: pl.BlockSpec((count, 1, rows_dev, width), lambda j: (0, j, 0, 0))
         out_shape = lambda count: jax.ShapeDtypeStruct((count, part, rows_dev, width), BF16)
         updated, *turned = pl.pallas_call(
-            functools.partial(attention_kernel, heads, n_rows),
+            functools.partial(attention_kernel, heads, n_cols, splits),
             out_shape=(out_shape(n_rows),) + (out_shape(halves),) * n_cols,
             grid=(part,),
             in_specs=[whole(tokens), lanes_spec, rows_spec, rows_spec, rows_spec, rows_spec, whole(w_out)]
-            + [whole(plane)] * n_rows,
+            + [whole(tile) for tile in tiles],
             out_specs=(out_spec(n_rows),) + (out_spec(halves),) * n_cols,
             scratch_shapes=[
                 pltpu.VMEM((total // cols_dev, heads, total, cols_dev), F32),
@@ -306,7 +330,7 @@
                 transcendentals=part * heads * total * total,
             ),
             name="attention_kernel",
-        )(tokens, key, query, value, gate, pair, w_out, *[held[at] for at in range(n_rows)])
+        )(tokens, key, query, value, gate, pair, w_out, *tiles)
         if step:
             updated, turned, own, mirrored = lax.optimization_barrier((updated, turned, own, mirrored))
         own.append(lax.all_to_all(updated, "row", split_axis=0, concat_axis=0, tiled=True))

time: 180 us -> 176 us (0.978)
  waiting for transfers between devices: 48.1 us -> 39.3 us
  local copies, waits for them, and re-layouts: 8.65 us -> 12.2 us
  starting transfers between devices: 48.8 us -> 52.1 us
  Pallas kernels: 69 us -> 66.9 us
    ppermute x10 -> x12, waiting for transfers between devices: 21.5 us -> 14.3 us  [swap_over(): return lax.ppermute(array, axis, [(at, at ^ step) for at in range(count)])]
    pallas_call x2, Pallas kernels: 37.5 us -> 35 us  [per_device(): pl.pallas_call(functools.partial(attention_kernel, heads, n_cols, splits)...]
    ppermute x8, starting transfers between devices: 20.6 us -> 22.9 us  [per_device(): mirrored.append(lax.ppermute(turned[shift], AXES, hops))]
    unnamed x49 -> x55, local copies, waits for them, and re-layouts: 2.82 us -> 5.11 us
    ppermute x10 -> x12, starting transfers between devices: 8.39 us -> 9.42 us  [swap_over(): return lax.ppermute(array, axis, [(at, at ^ step) for at in range(count)])]
  transfers between devices with their start and end apart: 22 -> 24, of which waited for: 12 -> 12; matrix products, arithmetic and copies ran while one was open for 5% -> 6% of each run, Pallas kernels for 21% -> 21%
where the time goes in v3:
time: 176 us; the launch traced here: 175 us
  Pallas kernels  66.9 us (38%)
  starting transfers between devices  52.1 us (30%)
  waiting for transfers between devices  39.3 us (22%)
  local copies, waits for them, and re-layouts  12.2 us (7%)
  other arithmetic  4.34 us (2%)
    pallas_call x2, Pallas kernels, per_device(): pl.pallas_call(functools.partial(attention_kernel, heads, n_cols, splits)...  35 us
    ppermute x8, waiting for transfers between devices, per_device(): mirrored.append(lax.ppermute(turned[shift], AXES, hops))  23.1 us
    ppermute x8, starting transfers between devices, per_device(): mirrored.append(lax.ppermute(turned[shift], AXES, hops))  22.9 us
    ppermute x12, waiting for transfers between devices, swap_over(): return lax.ppermute(array, axis, [(at, at ^ step) for at in range(count)])  14.3 us
    pallas_call x1, Pallas kernels, per_device(): pl.pallas_call(functools.partial(logits_kernel, n_cols, rounds), out_shap...  13.2 us
    pallas_call x1, Pallas kernels, per_device(): pl.pallas_call(functools.partial(project_kernel, head_dim, batch), out_sh...  10.9 us
    ppermute x12, starting transfers between devices, swap_over(): return lax.ppermute(array, axis, [(at, at ^ step) for at in range(count)])  9.42 us
    all_to_all x2, starting transfers between devices, per_device(): lax.all_to_all(updated, 'row', split_axis=0, concat_axis=0, tiled=True)  8.89 us
  transfers between devices with their start and end apart: 24, of which 12 were waited for; matrix products, arithmetic and copies ran while one was open for 6% of the time, Pallas kernels for 21%

profile of v3, /device:TPU:4, one launch (start us, length us, event | category | flops | bytes accessed | tf_op | source)
XLA Modules:
  0.0 175.2 jit_solution(10495225650694271327)
XLA Ops:
  1.4 6.1 %all-to-all-start = ((s32[32,4,16]{2,1,0:T(4,128)}), s32[32,4,16]{2,1,0:T(4,128)S(1)}, u32[]{:S(2)}, u32[]{:S(2)}) async-start(s32[32,4,16]{2,1,0:T(4,128)} %broadcast_in_dim.20), calls=%async_computation | async-start | bytes 131072 | tf_op jit(solution)/shard_map/all_to_all | solution.py:250
  7.5 3.3 %copy.25 = bf16[64,8,16,128]{3,2,0,1:T(8,128)(2,1)} copy(bf16[64,8,16,128]{3,2,1,0:T(8,128)(2,1)} %bitcast.21) | data formatting | bytes 4194304 | tf_op jit(solution)/shard_map/reshape | solution.py:252
  12.0 1.9 %all-to-all-done = s32[32,4,16]{2,1,0:T(4,128)S(1)} async-done(((s32[32,4,16]{2,1,0:T(4,128)}), s32[32,4,16]{2,1,0:T(4,128)S(1)}, u32[]{:S(2)}, u32[]{:S(2)}) %all-to-all-start) | async-done | bytes 8224 | tf_op jit(solution)/shard_map/all_to_all | solution.py:250
  13.9 4.9 %all-to-all-start.1 = ((bf16[8,64,16,128]{3,2,1,0:T(8,128)(2,1)}), bf16[8,64,16,128]{3,2,1,0:T(8,128)(2,1)S(1)}, u32[]{:S(2)}, u32[]{:S(2)}) async-start(bf16[8,64,16,128]{3,2,1,0:T(8,128)(2,1)} %bitcast.20), calls=%async_computation.1 | async-start | bytes 4194304 | tf_op jit(solution)/shard_map/all_to_all | solution.py:254
  20.1 7.8 %bias_kernel.1 = f32[2,128,128]{2,1,0:T(8,128)} custom-call(s32[4,512]{1,0:T(4,128)} %reshape.10.scalars.tokens, s32[4,512]{1,0:T(4,128)} %reshape.10.scalars.tokens, f32[1,128]{1,0:T(1,128)} %get-tuple-element.80.low, f32[1,128]{1,0:T(1,128)} %get-tuple-element.79.high, bf16[64,128,128]{2,1,0:T(8,128)(2,1)} %z.1, bf16[128,128]{1,0:T(8,128)(2,1)} %pad.17.w_dist, ...), custom_call_target="tpu_custom_call" | custom-call | flops 314572800 | bytes 4194304 | tf_op jit(solution)/shard_map/bias_kernel/pallas_call | solution.py:257
  29.3 3.0 %collective-permute-start.2 = (f32[2,128,128]{2,1,0:T(8,128)}, f32[2,128,128]{2,1,0:T(8,128)S(1)}, u32[]{:S(2)}, u32[]{:S(2)}) collective-permute-start(f32[2,128,128]{2,1,0:T(8,128)} %bias_kernel.1), channel_id=1, source_target_pairs={{0,3},{1,2},{2,1},{3,0},{4,7},{5,6},{6,5},{7,4},{8,11},{9,10},{10,... | collective-permute-start | bytes 393224 | tf_op jit(solution)/shard_map/ppermute | solution.py:223
  32.3 3.2 %collective-permute-done = f32[2,128,128]{2,1,0:T(8,128)S(1)} collective-permute-done((f32[2,128,128]{2,1,0:T(8,128)}, f32[2,128,128]{2,1,0:T(8,128)S(1)}, u32[]{:S(2)}, u32[]{:S(2)}) %collective-permute-start) | collective-permute-done | bytes 131104 | tf_op jit(solution)/shard_map/ppermute | solution.py:223
  35.5 5.7 %collective-permute-done.1 = f32[2,128,128]{2,1,0:T(8,128)S(1)} collective-permute-done((f32[2,128,128]{2,1,0:T(8,128)}, f32[2,128,128]{2,1,0:T(8,128)S(1)}, u32[]{:S(2)}, u32[]{:S(2)}) %collective-permute-start.1) | collective-permute-done | bytes 131104 | tf_op jit(solution)/shard_map/ppermute | solution.py:223
  47.0 10.9 %project_kernel.1 = (bf16[16,512,128]{2,1,0:T(8,128)(2,1)}, bf16[16,128,512]{2,1,0:T(8,128)(2,1)}, bf16[16,512,128]{2,1,0:T(8,128)(2,1)}, bf16[16,512,128]{2,1,0:T(8,128)(2,1)}, bf16[16,512,128]{2,1,0:T(8,128)(2,1)}) custom-call(s32[4,512]{1,0:T(4,128)} %reshape.10.scalars.tokens, s32[4,512]{1,0:T(4,128)} %reshape.10.scalars.tokens, ...), custom_call_target="tpu_custom_call" | custom-call | flops 2097152000 | bytes 16777216 | tf_op jit(solution)/shard_map/project_kernel/pallas_call | solution.py:281
  59.3 1.9 %collective-permute-start.9 = (f32[2,2,128,128]{3,2,1,0:T(8,128)S(1)}, f32[2,2,128,128]{3,2,1,0:T(8,128)S(1)}, u32[]{:S(2)}, u32[]{:S(2)}) collective-permute-start(f32[2,2,128,128]{3,2,1,0:T(8,128)S(1)} %slice.19), channel_id=1, source_target_pairs={{0,16},{4,20},{8,24},{12,28},{16,0},{20,4},{24,8},{28,12},{1,17},{... | collective-permute-start | bytes 786440 | tf_op jit(solution)/shard_map/ppermute | solution.py:223
  61.8 3.7 %collective-permute-done.8.refs_6_ = f32[2,2,128,128]{3,2,1,0:T(8,128)S(1)} collective-permute-done((f32[2,2,128,128]{3,2,1,0:T(8,128)S(1)}, f32[2,2,128,128]{3,2,1,0:T(8,128)S(1)}, u32[]{:S(2)}, u32[]{:S(2)}) %collective-permute-start.8) | collective-permute-done | bytes 262176 | tf_op jit(solution)/shard_map/ppermute | solution.py:223
  69.3 17.4 %attention_kernel.3 = (bf16[8,8,64,128]{3,2,1,0:T(8,128)(2,1)}, bf16[2,8,64,128]{3,2,1,0:T(8,128)(2,1)}, bf16[2,8,64,128]{3,2,1,0:T(8,128)(2,1)}, bf16[2,8,64,128]{3,2,1,0:T(8,128)(2,1)}, bf16[2,8,64,128]{3,2,1,0:T(8,128)(2,1)}) custom-call(s32[4,512]{1,0:T(4,128)} %reshape.10.scalars.tokens, bf16[16,128,512]{2,1,0:T(8,128)(2,1)} %get-tuple-element.49.key, ...), custom_call_target="tpu_custom_call" | custom-call | flops 8589934592 | bytes 16777216 | tf_op jit(solution)/shard_map/attention_kernel/pallas_call | solution.py:315
  86.8 5.4 %all-to-all-start.2 = ((bf16[8,8,64,128]{3,2,1,0:T(8,128)(2,1)}), bf16[8,8,64,128]{3,2,1,0:T(8,128)(2,1)S(1)}, u32[]{:S(2)}, u32[]{:S(2)}) async-start(bf16[8,8,64,128]{3,2,1,0:T(8,128)(2,1)} %get-tuple-element.62), calls=%async_computation.2 | async-start | bytes 2097152 | tf_op jit(solution)/shard_map/all_to_all | solution.py:336
  92.2 2.0 %collective-permute-start.12 = (bf16[2,8,64,128]{3,2,1,0:T(8,128)(2,1)S(1)}, bf16[2,8,64,128]{3,2,1,0:T(8,128)(2,1)S(1)}, u32[]{:S(2)}, u32[]{:S(2)}) collective-permute-start(bf16[2,8,64,128]{3,2,1,0:T(8,128)(2,1)S(1)} %copy-done.25), channel_id=1, source_target_pairs={{0,0},{1,8},{2,16},{3,24},{4,1},{5,9},{6,17},{7,25},{8,2},{9,10},{... | collective-permute-start | bytes 786440 | tf_op jit(solution)/shard_map/ppermute | solution.py:343
  94.2 3.6 %collective-permute-start.13 = (bf16[2,8,64,128]{3,2,1,0:T(8,128)(2,1)S(1)}, bf16[2,8,64,128]{3,2,1,0:T(8,128)(2,1)S(1)}, u32[]{:S(2)}, u32[]{:S(2)}) collective-permute-start(bf16[2,8,64,128]{3,2,1,0:T(8,128)(2,1)S(1)} %copy-done.24), channel_id=1, source_target_pairs={{0,1},{1,9},{2,17},{3,25},{4,0},{5,8},{6,16},{7,24},{8,3},{9,11},{... | collective-permute-start | bytes 786440 | tf_op jit(solution)/shard_map/ppermute | solution.py:343
  98.8 4.7 %collective-permute-start.15 = (bf16[2,8,64,128]{3,2,1,0:T(8,128)(2,1)S(1)}, bf16[2,8,64,128]{3,2,1,0:T(8,128)(2,1)S(1)}, u32[]{:S(2)}, u32[]{:S(2)}) collective-permute-start(bf16[2,8,64,128]{3,2,1,0:T(8,128)(2,1)S(1)} %copy-done.22), channel_id=1, source_target_pairs={{0,3},{1,11},{2,19},{3,27},{4,2},{5,10},{6,18},{7,26},{8,1},{9,9},... | collective-permute-start | bytes 786440 | tf_op jit(solution)/shard_map/ppermute | solution.py:343
  103.5 17.5 %attention_kernel.2 = (bf16[8,8,64,128]{3,2,1,0:T(8,128)(2,1)}, bf16[2,8,64,128]{3,2,1,0:T(8,128)(2,1)}, bf16[2,8,64,128]{3,2,1,0:T(8,128)(2,1)}, bf16[2,8,64,128]{3,2,1,0:T(8,128)(2,1)}, bf16[2,8,64,128]{3,2,1,0:T(8,128)(2,1)}) custom-call(s32[4,512]{1,0:T(4,128)} %reshape.10.scalars.tokens, bf16[16,128,512]{2,1,0:T(8,128)(2,1)} %get-tuple-element.49.key, ...), custom_call_target="tpu_custom_call" | custom-call | flops 8589934592 | bytes 16777216 | tf_op jit(solution)/shard_map/attention_kernel/pallas_call | solution.py:315
  123.3 3.5 %all-to-all-start.3 = ((bf16[8,8,64,128]{3,2,1,0:T(8,128)(2,1)}), bf16[8,8,64,128]{3,2,1,0:T(8,128)(2,1)S(1)}, u32[]{:S(2)}, u32[]{:S(2)}) async-start(bf16[8,8,64,128]{3,2,1,0:T(8,128)(2,1)} %get-tuple-element.68), calls=%async_computation.3 | async-start | bytes 2097152 | tf_op jit(solution)/shard_map/all_to_all | solution.py:336
  126.8 2.0 %collective-permute-start.16 = (bf16[2,8,64,128]{3,2,1,0:T(8,128)(2,1)}, bf16[2,8,64,128]{3,2,1,0:T(8,128)(2,1)S(1)}, u32[]{:S(2)}, u32[]{:S(2)}) collective-permute-start(bf16[2,8,64,128]{3,2,1,0:T(8,128)(2,1)} %get-tuple-element.73), channel_id=1, source_target_pairs={{0,0},{1,8},{2,16},{3,24},{4,1},{5,9},{6,17},{7,25},{8,2},{9,10},{... | collective-permute-start | bytes 786440 | tf_op jit(solution)/shard_map/ppermute | solution.py:343
  128.8 4.6 %collective-permute-start.17 = (bf16[2,8,64,128]{3,2,1,0:T(8,128)(2,1)}, bf16[2,8,64,128]{3,2,1,0:T(8,128)(2,1)}, u32[]{:S(2)}, u32[]{:S(2)}) collective-permute-start(bf16[2,8,64,128]{3,2,1,0:T(8,128)(2,1)} %get-tuple-element.74), channel_id=1, source_target_pairs={{0,1},{1,9},{2,17},{3,25},{4,0},{5,8},{6,16},{7,24},{8,3},{9,11},{... | collective-permute-start | bytes 786440 | tf_op jit(solution)/shard_map/ppermute | solution.py:343
  134.4 3.9 %collective-permute-start.19 = (bf16[2,8,64,128]{3,2,1,0:T(8,128)(2,1)}, bf16[2,8,64,128]{3,2,1,0:T(8,128)(2,1)}, u32[]{:S(2)}, u32[]{:S(2)}) collective-permute-start(bf16[2,8,64,128]{3,2,1,0:T(8,128)(2,1)} %get-tuple-element.76), channel_id=1, source_target_pairs={{0,3},{1,11},{2,19},{3,27},{4,2},{5,10},{6,18},{7,26},{8,1},{9,9},... | collective-permute-start | bytes 786440 | tf_op jit(solution)/shard_map/ppermute | solution.py:343
  140.0 10.1 %collective-permute-done.16.refs_7_ = bf16[2,8,64,128]{3,2,1,0:T(8,128)(2,1)S(1)} collective-permute-done((bf16[2,8,64,128]{3,2,1,0:T(8,128)(2,1)}, bf16[2,8,64,128]{3,2,1,0:T(8,128)(2,1)S(1)}, u32[]{:S(2)}, u32[]{:S(2)}) %collective-permute-start.16) | collective-permute-done | bytes 262176 | tf_op jit(solution)/shard_map/ppermute | solution.py:343
  150.1 9.5 %collective-permute-done.17.refs_8_ = bf16[2,8,64,128]{3,2,1,0:T(8,128)(2,1)} collective-permute-done((bf16[2,8,64,128]{3,2,1,0:T(8,128)(2,1)}, bf16[2,8,64,128]{3,2,1,0:T(8,128)(2,1)}, u32[]{:S(2)}, u32[]{:S(2)}) %collective-permute-start.17) | collective-permute-done | bytes 262176 | tf_op jit(solution)/shard_map/ppermute | solution.py:343
  162.0 13.2 %logits_kernel.1 = f32[64,128,128]{2,1,0:T(8,128)} custom-call(s32[4]{0:T(128)} %pad_add_fusion.1.refs_0_, bf16[8,8,64,128]{3,2,1,0:T(8,128)(2,1)} %copy-done, bf16[8,8,64,128]{3,2,1,0:T(8,128)(2,1)} %copy-done.1, bf16[2,8,64,128]{3,2,1,0:T(8,128)(2,1)} %copy-done.4, bf16[2,8,64,128]{3,2,1,0:T(8,128)(2,1)} %copy-done.5, bf16[2,8,64,128]{3,2,1,0:T(8,128)(2,1)} %copy-done.6, ...), custom_call_target="tpu_custom_call" | custom-call | tf_op jit(solution)/shard_map/logits_kernel/pallas_call | solution.py:350
  (103 shorter events, 24.7 us)
Async XLA Ops:
  1.4 12.5 %all-to-all-start = ((s32[32,4,16]{2,1,0:T(4,128)}), s32[32,4,16]{2,1,0:T(4,128)S(1)}, u32[]{:S(2)}, u32[]{:S(2)}) async-start(s32[32,4,16]{2,1,0:T(4,128)} %broadcast_in_dim.20), calls=%async_computation | async-start | bytes 131072 | tf_op jit(solution)/shard_map/all_to_all | solution.py:250
  13.9 31.8 %all-to-all-start.1 = ((bf16[8,64,16,128]{3,2,1,0:T(8,128)(2,1)}), bf16[8,64,16,128]{3,2,1,0:T(8,128)(2,1)S(1)}, u32[]{:S(2)}, u32[]{:S(2)}) async-start(bf16[8,64,16,128]{3,2,1,0:T(8,128)(2,1)} %bitcast.20), calls=%async_computation.1 | async-start | bytes 4194304 | tf_op jit(solution)/shard_map/all_to_all | solution.py:254
  27.9 7.6 %collective-permute-start = (f32[2,128,128]{2,1,0:T(8,128)}, f32[2,128,128]{2,1,0:T(8,128)S(1)}, u32[]{:S(2)}, u32[]{:S(2)}) collective-permute-start(f32[2,128,128]{2,1,0:T(8,128)} %bias_kernel.1), channel_id=1, source_target_pairs={{0,1},{1,0},{2,3},{3,2},{4,5},{5,4},{6,7},{7,6},{8,9},{9,8},{10,11... | collective-permute-start | bytes 393224 | tf_op jit(solution)/shard_map/ppermute | solution.py:223
  28.2 13.1 %collective-permute-start.1 = (f32[2,128,128]{2,1,0:T(8,128)}, f32[2,128,128]{2,1,0:T(8,128)S(1)}, u32[]{:S(2)}, u32[]{:S(2)}) collective-permute-start(f32[2,128,128]{2,1,0:T(8,128)} %bias_kernel.1), channel_id=1, source_target_pairs={{0,2},{1,3},{2,0},{3,1},{4,6},{5,7},{6,4},{7,5},{8,10},{9,11},{10,... | collective-permute-start | bytes 393224 | tf_op jit(solution)/shard_map/ppermute | solution.py:223
  29.3 11.9 %collective-permute-start.2 = (f32[2,128,128]{2,1,0:T(8,128)}, f32[2,128,128]{2,1,0:T(8,128)S(1)}, u32[]{:S(2)}, u32[]{:S(2)}) collective-permute-start(f32[2,128,128]{2,1,0:T(8,128)} %bias_kernel.1), channel_id=1, source_target_pairs={{0,3},{1,2},{2,1},{3,0},{4,7},{5,6},{6,5},{7,4},{8,11},{9,10},{10,... | collective-permute-start | bytes 393224 | tf_op jit(solution)/shard_map/ppermute | solution.py:223
  42.2 15.7 %collective-permute-start.3 = (f32[4,2,128,128]{3,2,1,0:T(8,128)S(1)}, f32[4,2,128,128]{3,2,1,0:T(8,128)S(1)}, u32[]{:S(2)}, u32[]{:S(2)}) collective-permute-start(f32[4,2,128,128]{3,2,1,0:T(8,128)S(1)} %pad_maximum_fusion.refs_0_), channel_id=1, source_target_pairs={{0,8},{4,12},{8,0},{12,4},{16,24},{20,28},{24,16},{28,20},{1,9},{5... | collective-permute-start | bytes 1572872 | tf_op jit(solution)/shard_map/ppermute | solution.py:223
  43.8 14.1 %collective-permute-start.4 = (f32[4,2,128,128]{3,2,1,0:T(8,128)S(1)}, f32[4,2,128,128]{3,2,1,0:T(8,128)}, u32[]{:S(2)}, u32[]{:S(2)}) collective-permute-start(f32[4,2,128,128]{3,2,1,0:T(8,128)S(1)} %pad_maximum_fusion.refs_0_), channel_id=1, source_target_pairs={{0,16},{4,20},{8,24},{12,28},{16,0},{20,4},{24,8},{28,12},{1,17},{... | collective-permute-start | bytes 1572872 | tf_op jit(solution)/shard_map/ppermute | solution.py:223
  59.1 6.4 %collective-permute-start.8 = (f32[2,2,128,128]{3,2,1,0:T(8,128)S(1)}, f32[2,2,128,128]{3,2,1,0:T(8,128)S(1)}, u32[]{:S(2)}, u32[]{:S(2)}) collective-permute-start(f32[2,2,128,128]{3,2,1,0:T(8,128)S(1)} %slice.18), channel_id=1, source_target_pairs={{0,8},{4,12},{8,0},{12,4},{16,24},{20,28},{24,16},{28,20},{1,9},{5... | collective-permute-start | bytes 786440 | tf_op jit(solution)/shard_map/ppermute | solution.py:223
  59.3 6.4 %collective-permute-start.9 = (f32[2,2,128,128]{3,2,1,0:T(8,128)S(1)}, f32[2,2,128,128]{3,2,1,0:T(8,128)S(1)}, u32[]{:S(2)}, u32[]{:S(2)}) collective-permute-start(f32[2,2,128,128]{3,2,1,0:T(8,128)S(1)} %slice.19), channel_id=1, source_target_pairs={{0,16},{4,20},{8,24},{12,28},{16,0},{20,4},{24,8},{28,12},{1,17},{... | collective-permute-start | bytes 786440 | tf_op jit(solution)/shard_map/ppermute | solution.py:223
  61.3 6.2 %collective-permute-start.5 = (f32[4,2,128,128]{3,2,1,0:T(8,128)S(1)}, f32[4,2,128,128]{3,2,1,0:T(8,128)S(1)}, u32[]{:S(2)}, u32[]{:S(2)}) collective-permute-start(f32[4,2,128,128]{3,2,1,0:T(8,128)S(1)} %pad_maximum_fusion.refs_0_), channel_id=1, source_target_pairs={{0,4},{4,0},{8,12},{12,8},{16,20},{20,16},{24,28},{28,24},{1,5},{5... | collective-permute-start | bytes 1572872 | tf_op jit(solution)/shard_map/ppermute | solution.py:223
  61.3 6.2 %collective-permute-start.6 = (f32[4,2,128,128]{3,2,1,0:T(8,128)S(1)}, f32[4,2,128,128]{3,2,1,0:T(8,128)S(1)}, u32[]{:S(2)}, u32[]{:S(2)}) collective-permute-start(f32[4,2,128,128]{3,2,1,0:T(8,128)S(1)} %collective-permute-done.3.refs_2_), channel_id=1, source_target_pairs={{0,4},{4,0},{8,12},{12,8},{16,20},{20,16},{24,28},{28,24},{1,5},{5... | collective-permute-start | bytes 1572872 | tf_op jit(solution)/shard_map/ppermute | solution.py:223
  61.8 5.7 %collective-permute-start.7 = (f32[4,2,128,128]{3,2,1,0:T(8,128)}, f32[4,2,128,128]{3,2,1,0:T(8,128)S(1)}, u32[]{:S(2)}, u32[]{:S(2)}) collective-permute-start(f32[4,2,128,128]{3,2,1,0:T(8,128)} %collective-permute-done.4.refs_4_), channel_id=1, source_target_pairs={{0,4},{4,0},{8,12},{12,8},{16,20},{20,16},{24,28},{28,24},{1,5},{5... | collective-permute-start | bytes 1572872 | tf_op jit(solution)/shard_map/ppermute | solution.py:223
  65.5 1.5 collective-permute-start.10
  65.8 1.7 collective-permute-start.11
  86.8 36.5 %all-to-all-start.2 = ((bf16[8,8,64,128]{3,2,1,0:T(8,128)(2,1)}), bf16[8,8,64,128]{3,2,1,0:T(8,128)(2,1)S(1)}, u32[]{:S(2)}, u32[]{:S(2)}) async-start(bf16[8,8,64,128]{3,2,1,0:T(8,128)(2,1)} %get-tuple-element.62), calls=%async_computation.2 | async-start | bytes 2097152 | tf_op jit(solution)/shard_map/all_to_all | solution.py:336
  92.2 28.9 %collective-permute-start.12 = (bf16[2,8,64,128]{3,2,1,0:T(8,128)(2,1)S(1)}, bf16[2,8,64,128]{3,2,1,0:T(8,128)(2,1)S(1)}, u32[]{:S(2)}, u32[]{:S(2)}) collective-permute-start(bf16[2,8,64,128]{3,2,1,0:T(8,128)(2,1)S(1)} %copy-done.25), channel_id=1, source_target_pairs={{0,0},{1,8},{2,16},{3,24},{4,1},{5,9},{6,17},{7,25},{8,2},{9,10},{... | collective-permute-start | bytes 786440 | tf_op jit(solution)/shard_map/ppermute | solution.py:343
  94.2 27.9 %collective-permute-start.13 = (bf16[2,8,64,128]{3,2,1,0:T(8,128)(2,1)S(1)}, bf16[2,8,64,128]{3,2,1,0:T(8,128)(2,1)S(1)}, u32[]{:S(2)}, u32[]{:S(2)}) collective-permute-start(bf16[2,8,64,128]{3,2,1,0:T(8,128)(2,1)S(1)} %copy-done.24), channel_id=1, source_target_pairs={{0,1},{1,9},{2,17},{3,25},{4,0},{5,8},{6,16},{7,24},{8,3},{9,11},{... | collective-permute-start | bytes 786440 | tf_op jit(solution)/shard_map/ppermute | solution.py:343
  97.8 24.3 %collective-permute-start.14 = (bf16[2,8,64,128]{3,2,1,0:T(8,128)(2,1)S(1)}, bf16[2,8,64,128]{3,2,1,0:T(8,128)(2,1)S(1)}, u32[]{:S(2)}, u32[]{:S(2)}) collective-permute-start(bf16[2,8,64,128]{3,2,1,0:T(8,128)(2,1)S(1)} %copy-done.23), channel_id=1, source_target_pairs={{0,2},{1,10},{2,18},{3,26},{4,3},{5,11},{6,19},{7,27},{8,0},{9,8},... | collective-permute-start | bytes 786440 | tf_op jit(solution)/shard_map/ppermute | solution.py:343
  98.8 24.5 %collective-permute-start.15 = (bf16[2,8,64,128]{3,2,1,0:T(8,128)(2,1)S(1)}, bf16[2,8,64,128]{3,2,1,0:T(8,128)(2,1)S(1)}, u32[]{:S(2)}, u32[]{:S(2)}) collective-permute-start(bf16[2,8,64,128]{3,2,1,0:T(8,128)(2,1)S(1)} %copy-done.22), channel_id=1, source_target_pairs={{0,3},{1,11},{2,19},{3,27},{4,2},{5,10},{6,18},{7,26},{8,1},{9,9},... | collective-permute-start | bytes 786440 | tf_op jit(solution)/shard_map/ppermute | solution.py:343
  123.3 37.6 %all-to-all-start.3 = ((bf16[8,8,64,128]{3,2,1,0:T(8,128)(2,1)}), bf16[8,8,64,128]{3,2,1,0:T(8,128)(2,1)S(1)}, u32[]{:S(2)}, u32[]{:S(2)}) async-start(bf16[8,8,64,128]{3,2,1,0:T(8,128)(2,1)} %get-tuple-element.68), calls=%async_computation.3 | async-start | bytes 2097152 | tf_op jit(solution)/shard_map/all_to_all | solution.py:336
  126.8 23.3 %collective-permute-start.16 = (bf16[2,8,64,128]{3,2,1,0:T(8,128)(2,1)}, bf16[2,8,64,128]{3,2,1,0:T(8,128)(2,1)S(1)}, u32[]{:S(2)}, u32[]{:S(2)}) collective-permute-start(bf16[2,8,64,128]{3,2,1,0:T(8,128)(2,1)} %get-tuple-element.73), channel_id=1, source_target_pairs={{0,0},{1,8},{2,16},{3,24},{4,1},{5,9},{6,17},{7,25},{8,2},{9,10},{... | collective-permute-start | bytes 786440 | tf_op jit(solution)/shard_map/ppermute | solution.py:343
  128.8 30.9 %collective-permute-start.17 = (bf16[2,8,64,128]{3,2,1,0:T(8,128)(2,1)}, bf16[2,8,64,128]{3,2,1,0:T(8,128)(2,1)}, u32[]{:S(2)}, u32[]{:S(2)}) collective-permute-start(bf16[2,8,64,128]{3,2,1,0:T(8,128)(2,1)} %get-tuple-element.74), channel_id=1, source_target_pairs={{0,1},{1,9},{2,17},{3,25},{4,0},{5,8},{6,16},{7,24},{8,3},{9,11},{... | collective-permute-start | bytes 786440 | tf_op jit(solution)/shard_map/ppermute | solution.py:343
  133.5 26.2 %collective-permute-start.18 = (bf16[2,8,64,128]{3,2,1,0:T(8,128)(2,1)}, bf16[2,8,64,128]{3,2,1,0:T(8,128)(2,1)}, u32[]{:S(2)}, u32[]{:S(2)}) collective-permute-start(bf16[2,8,64,128]{3,2,1,0:T(8,128)(2,1)} %get-tuple-element.75), channel_id=1, source_target_pairs={{0,2},{1,10},{2,18},{3,26},{4,3},{5,11},{6,19},{7,27},{8,0},{9,8},... | collective-permute-start | bytes 786440 | tf_op jit(solution)/shard_map/ppermute | solution.py:343
  134.4 26.5 %collective-permute-start.19 = (bf16[2,8,64,128]{3,2,1,0:T(8,128)(2,1)}, bf16[2,8,64,128]{3,2,1,0:T(8,128)(2,1)}, u32[]{:S(2)}, u32[]{:S(2)}) collective-permute-start(bf16[2,8,64,128]{3,2,1,0:T(8,128)(2,1)} %get-tuple-element.76), channel_id=1, source_target_pairs={{0,3},{1,11},{2,19},{3,27},{4,2},{5,10},{6,18},{7,26},{8,1},{9,9},... | collective-permute-start | bytes 786440 | tf_op jit(solution)/shard_map/ppermute | solution.py:343
  (27 other events, 378.4 us)

commit v4 on v3

--- a/solution.py
+++ b/solution.py
@@ -14,32 +14,10 @@
 AXES = ("row", "col")
 
 
-def means(parts):
-    width = parts[0].shape[-1]
-    stacked = jnp.concatenate(parts, axis=1) if len(parts) > 1 else parts[0]
-    return jnp.dot(stacked, jnp.full((stacked.shape[1], width), 1.0 / width, BF16), preferred_element_type=F32)
-
-
-def normalise(values, parts):
-    centred = values - means(parts)
-    squares = centred * centred
-    high = squares.astype(BF16)
-    variance = means([high, (squares - high.astype(F32)).astype(BF16)])
-    return (centred * lax.rsqrt(variance + 1e-05)).astype(BF16)
-
-
-def normalise_pair(mine, other):
-    width = mine.shape[1]
-    row = lax.broadcasted_iota(jnp.int32, (2 * width, 2 * width), 0) < width
-    lane = lax.broadcasted_iota(jnp.int32, (2 * width, 2 * width), 1) < width
-    both_ways = jnp.where(jnp.logical_or(row, jnp.logical_not(lane)), 1.0 / width, 0.0).astype(BF16)
-    each_way = jnp.where(row == lane, 1.0 / width, 0.0).astype(BF16)
-    average = jnp.dot(jnp.concatenate([mine.astype(BF16), other], axis=1), both_ways, preferred_element_type=F32)
-    centred = jnp.concatenate([mine, mine + other.astype(F32)], axis=1) - average
-    squares = centred * centred
-    high = squares.astype(BF16)
-    rest = (squares - high.astype(F32)).astype(BF16)
-    variance = jnp.dot(high, each_way, preferred_element_type=F32) + jnp.dot(rest, each_way, preferred_element_type=F32)
+def normalise(values):
+    average = jnp.mean(values, axis=-1, keepdims=True)
+    centred = values - average
+    variance = jnp.mean(centred * centred, axis=-1, keepdims=True)
     return (centred * lax.rsqrt(variance + 1e-05)).astype(BF16)
 
 
@@ -80,7 +58,7 @@
         values = z[pl.ds(first, batch)].reshape(batch * cols_dev, width).astype(F32)
         squares = [squared_distance(spread, scalars, row_at * rows_dev + first + at) for at in range(batch)]
         pair = embed(squares, low, high, w_dist, values)
-        normed = normalise(pair.astype(F32), [pair])
+        normed = normalise(pair.astype(F32))
         lines = lax.dot_general(w_bias[...], normed, NT, preferred_element_type=F32)
         for at in range(batch):
             for head in range(heads):
@@ -96,24 +74,34 @@
 
 
 def project_kernel(
-    head_dim, batch, scalars, tokens, low, high, z, w_dist, w_key, w_rest, pair, key, query, value, gate, wide, spread
+    head_dim, batch, done, part, scalars, tokens, low, high, z, w_dist, w_key, w_rest, pair, key, query, value, gate, wide, spread
 ):
     total, slab, width = z.shape
     row_at, col_at = lax.axis_index("row"), lax.axis_index("col")
     cols_dev = spread.shape[2]
     half = cols_dev // 2
+    pitch = wide.shape[0] // total
+    lowest = done // 8 * 8
 
     @pl.when(pl.program_id(0) == 0)
     def _():
         spread_lines(tokens, spread)
-        wide[...] = z[...].reshape(total * slab, width).astype(F32)
+        lines = 16
+
+        def some_lines(step, carry):
+            for at in range(lines):
+                spot = pl.multiple_of((step * lines + at) * pitch, 8)
+                wide[pl.ds(spot, pitch), :] = z[step * lines + at].astype(F32)[lowest : lowest + pitch]
+            return carry
+
+        lax.fori_loop(0, total // lines, some_lines, 0)
 
     first = pl.program_id(0) * batch
-    own = col_at * cols_dev + row_at * slab + first
-    values = jnp.concatenate([wide[pl.ds(first + at, total, stride=slab), :] for at in range(batch)], axis=0)
+    own = col_at * cols_dev + row_at * slab + done + first
+    values = jnp.concatenate([wide[pl.ds(done - lowest + first + at, total, stride=pitch), :] for at in range(batch)], axis=0)
     squares = [squared_distance(spread, scalars, own + at) for at in range(batch)]
     rounded = embed(squares, low, high, w_dist, values)
-    normed = normalise(rounded.astype(F32), [rounded])
+    normed = normalise(rounded.astype(F32))
     rest = jnp.dot(normed, w_rest[...], preferred_element_type=F32)
     odd_lane = lax.broadcasted_iota(jnp.int32, (1, width), 1) // head_dim % 2 == 1
     odd_row = lax.broadcasted_iota(jnp.int32, (width, 1), 0) // head_dim % 2 == 1
@@ -185,23 +173,25 @@
         mirrored[shift][:, 0] = result[pl.ds(block * halves, halves)]
 
 
-def logits_kernel(n_cols, rounds, *refs):
+def logits_kernel(n_cols, parts, *refs):
+    rounds = len(parts)
     own = refs[1 : 1 + rounds]
     mirrored = refs[1 + rounds : 1 + rounds + rounds * n_cols]
     w_both, logits, wide = refs[1 + rounds + rounds * n_cols :]
-    n_rows, part, rows_dev, width = own[0].shape
+    n_rows, _, rows_dev, width = own[0].shape
     halves = n_rows // n_cols
     cols_dev = halves * rows_dev
-    slab = rounds * part
+    slab = sum(parts)
+    pitch = wide.shape[0] // cols_dev
     at_shift = pl.program_id(0)
 
     @pl.when(at_shift == 0)
     def _():
-        size = part * rows_dev
         for row in range(n_rows):
             for step in range(rounds):
-                first = (row * rounds + step) * size
-                wide[first : first + size, :] = own[step][row].reshape(size, width).astype(F32)
+                for at in range(parts[step]):
+                    first = (row * slab + sum(parts[:step]) + at) * pitch
+                    wide[first : first + rows_dev, :] = own[step][row, at].astype(F32)
 
     first = refs[0][at_shift] * slab
     for shift in range(n_cols):
@@ -209,14 +199,15 @@
         @pl.when(at_shift == shift)
         def _():
             for step in range(rounds):
+                done = sum(parts[:step])
                 mine, other = [], []
-                for at in range(part):
-                    mine.append(wide[pl.ds(first + step * part + at, cols_dev, stride=rows_dev), :])
+                for at in range(parts[step]):
+                    mine.append(wide[pl.ds(first + done + at, cols_dev, stride=pitch), :])
                     other += [mirrored[step * n_cols + shift][half, at] for half in range(halves)]
-                mine, other = jnp.concatenate(mine, axis=0), jnp.concatenate(other, axis=0)
-                both = normalise_pair(mine, other)
+                mine, other = jnp.concatenate(mine, axis=0), jnp.concatenate(other, axis=0).astype(F32)
+                both = jnp.concatenate([normalise(mine), normalise(mine + other)], axis=1)
                 found = jnp.dot(both, w_both[...], preferred_element_type=F32)
-                logits[step * part : (step + 1) * part] = found.reshape(part, cols_dev, found.shape[1])
+                logits[done : done + parts[step]] = found.reshape(parts[step], cols_dev, found.shape[1])
 
 
 def swap_over(array, axis, step, count):
@@ -255,7 +246,7 @@
     z_cols = z_cols.reshape(total, slab, width)
 
     bias = pl.pallas_call(
-        functools.partial(bias_kernel, 16),
+        functools.partial(bias_kernel, 32),
         out_shape=jax.ShapeDtypeStruct((heads // 2, cols_dev, 2 * rows_dev), F32),
         in_specs=[smem] + [vmem] * 6,
         out_specs=vmem,
@@ -273,22 +264,32 @@
 
     w_key = w_attn[:, width : 2 * width].T
     w_rest = jnp.concatenate([w_attn[:, :width], w_attn[:, 2 * width :]], axis=1)
-    batch = 4
-    by_rows = pl.BlockSpec((batch, total, width), lambda j: (j, 0, 0))
-    by_lanes = pl.BlockSpec((batch, width, total), lambda j: (j, 0, 0))
-    rows_shape = jax.ShapeDtypeStruct((slab, total, width), BF16)
-    lanes_shape = jax.ShapeDtypeStruct((slab, width, total), BF16)
-    projected = pl.pallas_call(
-        functools.partial(project_kernel, head_dim, batch),
-        out_shape=(rows_shape, lanes_shape, rows_shape, rows_shape, rows_shape),
-        grid=(slab // batch,),
-        in_specs=[smem, whole(tokens), vmem, vmem, whole(z_cols), vmem, vmem, vmem],
-        out_specs=(by_rows, by_lanes, by_rows, by_rows, by_rows),
-        scratch_shapes=[pltpu.VMEM((total * slab, width), F32), pltpu.VMEM((3, total, width), F32)],
-        compiler_params=params,
-        cost_estimate=pl.CostEstimate(flops=total * slab * width * 2000, bytes_accessed=1 << 24, transcendentals=0),
-        name="project_kernel",
-    )(tokens, tokens, low, high, z_cols, w_dist_full, w_key, w_rest)
+    rounds = 2
+    parts = tuple((slab + rounds - 1 - step) // rounds for step in range(rounds))
+
+    def project(step):
+        done, part = sum(parts[:step]), parts[step]
+        batch = min(4, part)
+        spread_rows = -(-(done + part) // 8) * 8 - done // 8 * 8
+        by_rows = pl.BlockSpec((batch, total, width), lambda j: (j, 0, 0))
+        by_lanes = pl.BlockSpec((batch, width, total), lambda j: (j, 0, 0))
+        rows_shape = jax.ShapeDtypeStruct((part, total, width), BF16)
+        lanes_shape = jax.ShapeDtypeStruct((part, width, total), BF16)
+        return pl.pallas_call(
+            functools.partial(project_kernel, head_dim, batch, done, part),
+            out_shape=(rows_shape, lanes_shape, rows_shape, rows_shape, rows_shape),
+            grid=(part // batch,),
+            in_specs=[smem, whole(tokens), vmem, vmem, whole(z_cols), vmem, vmem, vmem],
+            out_specs=(by_rows, by_lanes, by_rows, by_rows, by_rows),
+            scratch_shapes=[pltpu.VMEM((total * spread_rows, width), F32), pltpu.VMEM((3, total, width), F32)],
+            compiler_params=params,
+            cost_estimate=pl.CostEstimate(
+                flops=total * part * width * 2000, bytes_accessed=1 << 23, transcendentals=0
+            ),
+            name="project_kernel",
+        )(tokens, tokens, low, high, z_cols, w_dist_full, w_key, w_rest)
+
+    projected = [project(0)]
     held, projected = lax.optimization_barrier((held, projected))
     for step in range(2, n_rows, 2):
         one = step & -step
@@ -298,18 +299,20 @@
             first = first[0] if len(first) == 2 else first[0][:cut]
             second = second[1] if len(second) == 2 else second[0][cut:]
             held[step] = [swap_over(first, "row", one, n_rows), swap_over(second, "row", step ^ one, n_rows)]
+    projected.append(project(1))
+    passed_on = {step: held[step] for step in range(2, n_rows, 2) if step & (step - 1)}
+    passed_on, projected = lax.optimization_barrier((passed_on, projected))
+    held |= passed_on
     for step in range(0, n_rows, 2):
         held[step + 1] = [swap_over(tile, "row", 1, n_rows) for tile in held[step]]
     splits = tuple(len(held[step]) for step in range(n_rows))
     tiles = [tile for step in range(n_rows) for tile in held[step]]
-    pair, key, query, value, gate = projected
-
-    rounds = 2
-    part = slab // rounds
+
     own, mirrored = [], []
-    for step in range(rounds):
-        rows_spec = pl.BlockSpec((1, total, width), lambda j, step=step: (j + step * part, 0, 0))
-        lanes_spec = pl.BlockSpec((1, width, total), lambda j, step=step: (j + step * part, 0, 0))
+    for step, part in enumerate(parts):
+        pair, key, query, value, gate = projected[step]
+        rows_spec = pl.BlockSpec((1, total, width), lambda j: (j, 0, 0))
+        lanes_spec = pl.BlockSpec((1, width, total), lambda j: (j, 0, 0))
         out_spec = lambda count: pl.BlockSpec((count, 1, rows_dev, width), lambda j: (0, j, 0, 0))
         out_shape = lambda count: jax.ShapeDtypeStruct((count, part, rows_dev, width), BF16)
         updated, *turned = pl.pallas_call(
@@ -348,14 +351,14 @@
         [jnp.pad(w_pae, ((0, 0), (0, bins))), jnp.pad(w_pde, ((0, 0), (bins, 0)))], axis=0
     )
     return pl.pallas_call(
-        functools.partial(logits_kernel, n_cols, rounds),
+        functools.partial(logits_kernel, n_cols, parts),
         out_shape=jax.ShapeDtypeStruct((rows_dev, cols_dev, 2 * bins), F32),
         grid_spec=pltpu.PrefetchScalarGridSpec(
             num_scalar_prefetch=1,
             grid=(n_cols,),
             in_specs=[whole(array) for array in own + mirrored + [w_both]],
             out_specs=pl.BlockSpec((slab, cols_dev, 2 * bins), lambda b, at: (at[b], 0, 0)),
-            scratch_shapes=[pltpu.VMEM((cols_dev * rows_dev, width), F32)],
+            scratch_shapes=[pltpu.VMEM((cols_dev * (rows_dev + 8), width), F32)],
         ),
         compiler_params=params,
         name="logits_kernel",

time: 176 us -> 173 us (0.983)
    ppermute x12, waiting for transfers between devices: 14.3 us -> 12.6 us  [swap_over(): return lax.ppermute(array, axis, [(at, at ^ step) for at in range(count)])]
    pallas_call x3 -> x4, Pallas kernels: 31.9 us -> 31.1 us  [the longest x2 14.8 us: project(): pl.pallas_call(functools.partial(project_kernel, head_dim, batch, done, p...]
  transfers between devices with their start and end apart: 24 -> 24, of which waited for: 12 -> 12; matrix products, arithmetic and copies ran while one was open for 6% -> 6% of each run, Pallas kernels for 21% -> 22%
where the time goes in v4:
time: 173 us
  Pallas kernels  66.1 us (38%)
  starting transfers between devices  50.6 us (29%)
  waiting for transfers between devices  39 us (23%)
  local copies, waits for them, and re-layouts  12.2 us (7%)
  other arithmetic  4.3 us (2%)
    pallas_call x2, Pallas kernels, per_device(): pl.pallas_call(functools.partial(attention_kernel, heads, n_cols, splits)...  35 us
    ppermute x8, waiting for transfers between devices, per_device(): mirrored.append(lax.ppermute(turned[shift], AXES, hops))  24.4 us
    ppermute x8, starting transfers between devices, per_device(): mirrored.append(lax.ppermute(turned[shift], AXES, hops))  22.2 us
    pallas_call x2, Pallas kernels, project(): pl.pallas_call(functools.partial(project_kernel, head_dim, batch, done, p...  14.8 us
    ppermute x12, waiting for transfers between devices, swap_over(): return lax.ppermute(array, axis, [(at, at ^ step) for at in range(count)])  12.6 us
    pallas_call x1, Pallas kernels, per_device(): pl.pallas_call(functools.partial(logits_kernel, n_cols, parts), out_shape...  9.97 us
    ppermute x12, starting transfers between devices, swap_over(): return lax.ppermute(array, axis, [(at, at ^ step) for at in range(count)])  9.53 us
    all_to_all x2, starting transfers between devices, per_device(): lax.all_to_all(updated, 'row', split_axis=0, concat_axis=0, tiled=True)  7.92 us
  transfers between devices with their start and end apart: 24, of which 12 were waited for; matrix products, arithmetic and copies ran while one was open for 6% of the time, Pallas kernels for 22%

profile of v4, /device:TPU:4, one launch (start us, length us, event | category | flops | bytes accessed | tf_op | source)
XLA Modules:
  0.0 172.6 jit_solution(9640032565484884749)
XLA Ops:
  1.3 6.1 %all-to-all-start = ((s32[32,4,16]{2,1,0:T(4,128)}), s32[32,4,16]{2,1,0:T(4,128)S(1)}, u32[]{:S(2)}, u32[]{:S(2)}) async-start(s32[32,4,16]{2,1,0:T(4,128)} %broadcast_in_dim.20), calls=%async_computation | async-start | bytes 131072 | tf_op jit(solution)/shard_map/all_to_all | solution.py:241
  7.5 3.3 %copy.25 = bf16[64,8,16,128]{3,2,0,1:T(8,128)(2,1)} copy(bf16[64,8,16,128]{3,2,1,0:T(8,128)(2,1)} %bitcast.21) | data formatting | bytes 4194304 | tf_op jit(solution)/shard_map/reshape | solution.py:243
  13.8 4.9 %all-to-all-start.1 = ((bf16[8,64,16,128]{3,2,1,0:T(8,128)(2,1)}), bf16[8,64,16,128]{3,2,1,0:T(8,128)(2,1)S(1)}, u32[]{:S(2)}, u32[]{:S(2)}) async-start(bf16[8,64,16,128]{3,2,1,0:T(8,128)(2,1)} %bitcast.20), calls=%async_computation.1 | async-start | bytes 4194304 | tf_op jit(solution)/shard_map/all_to_all | solution.py:245
  20.1 6.3 %bias_kernel.1 = f32[2,128,128]{2,1,0:T(8,128)} custom-call(s32[4,512]{1,0:T(4,128)} %reshape.10.scalars.tokens, s32[4,512]{1,0:T(4,128)} %reshape.10.scalars.tokens, f32[1,128]{1,0:T(1,128)} %get-tuple-element.114.low, f32[1,128]{1,0:T(1,128)} %get-tuple-element.113.high, bf16[64,128,128]{2,1,0:T(8,128)(2,1)} %z.1, bf16[128,128]{1,0:T(8,128)(2,1)} %pad.17.w_dist, ...), custom_call_target="tpu_custom_call" | custom-call | flops 314572800 | bytes 4194304 | tf_op jit(solution)/shard_map/bias_kernel/pallas_call | solution.py:248
  27.8 3.0 %collective-permute-start.2 = (f32[2,128,128]{2,1,0:T(8,128)}, f32[2,128,128]{2,1,0:T(8,128)S(1)}, u32[]{:S(2)}, u32[]{:S(2)}) collective-permute-start(f32[2,128,128]{2,1,0:T(8,128)} %bias_kernel.1), channel_id=1, source_target_pairs={{0,3},{1,2},{2,1},{3,0},{4,7},{5,6},{6,5},{7,4},{8,11},{9,10},{10,... | collective-permute-start | bytes 393224 | tf_op jit(solution)/shard_map/ppermute | solution.py:214
  30.8 3.2 %collective-permute-done = f32[2,128,128]{2,1,0:T(8,128)S(1)} collective-permute-done((f32[2,128,128]{2,1,0:T(8,128)}, f32[2,128,128]{2,1,0:T(8,128)S(1)}, u32[]{:S(2)}, u32[]{:S(2)}) %collective-permute-start) | collective-permute-done | bytes 131104 | tf_op jit(solution)/shard_map/ppermute | solution.py:214
  34.0 5.7 %collective-permute-done.1 = f32[2,128,128]{2,1,0:T(8,128)S(1)} collective-permute-done((f32[2,128,128]{2,1,0:T(8,128)}, f32[2,128,128]{2,1,0:T(8,128)S(1)}, u32[]{:S(2)}, u32[]{:S(2)}) %collective-permute-start.1) | collective-permute-done | bytes 131104 | tf_op jit(solution)/shard_map/ppermute | solution.py:214
  45.7 7.4 %project_kernel.2 = (bf16[8,512,128]{2,1,0:T(8,128)(2,1)}, bf16[8,128,512]{2,1,0:T(8,128)(2,1)}, bf16[8,512,128]{2,1,0:T(8,128)(2,1)}, bf16[8,512,128]{2,1,0:T(8,128)(2,1)}, bf16[8,512,128]{2,1,0:T(8,128)(2,1)}) custom-call(s32[4,512]{1,0:T(4,128)} %reshape.10.scalars.tokens, s32[4,512]{1,0:T(4,128)} %reshape.10.scalars.tokens, ...), custom_call_target="tpu_custom_call" | custom-call | flops 1048576000 | bytes 8388608 | tf_op jit(solution)/shard_map/project_kernel/pallas_call | solution.py:278
  53.1 2.1 %collective-permute-done.3.refs_2_ = f32[4,2,128,128]{3,2,1,0:T(8,128)S(1)} collective-permute-done((f32[4,2,128,128]{3,2,1,0:T(8,128)S(1)}, f32[4,2,128,128]{3,2,1,0:T(8,128)S(1)}, u32[]{:S(2)}, u32[]{:S(2)}) %collective-permute-start.3) | collective-permute-done | bytes 524320 | tf_op jit(solution)/shard_map/ppermute | solution.py:214
  58.9 7.4 %project_kernel.3 = (bf16[8,512,128]{2,1,0:T(8,128)(2,1)}, bf16[8,128,512]{2,1,0:T(8,128)(2,1)}, bf16[8,512,128]{2,1,0:T(8,128)(2,1)}, bf16[8,512,128]{2,1,0:T(8,128)(2,1)}, bf16[8,512,128]{2,1,0:T(8,128)(2,1)}) custom-call(s32[4,512]{1,0:T(4,128)} %reshape.10.scalars.tokens, s32[4,512]{1,0:T(4,128)} %reshape.10.scalars.tokens, ...), custom_call_target="tpu_custom_call" | custom-call | flops 1048576000 | bytes 8388608 | tf_op jit(solution)/shard_map/project_kernel/pallas_call | solution.py:278
  70.3 17.4 %attention_kernel.3 = (bf16[8,8,64,128]{3,2,1,0:T(8,128)(2,1)}, bf16[2,8,64,128]{3,2,1,0:T(8,128)(2,1)}, bf16[2,8,64,128]{3,2,1,0:T(8,128)(2,1)}, bf16[2,8,64,128]{3,2,1,0:T(8,128)(2,1)}, bf16[2,8,64,128]{3,2,1,0:T(8,128)(2,1)}) custom-call(s32[4,512]{1,0:T(4,128)} %reshape.10.scalars.tokens, bf16[8,128,512]{2,1,0:T(8,128)(2,1)} %get-tuple-element.91.key, ...), custom_call_target="tpu_custom_call" | custom-call | flops 8589934592 | bytes 16777216 | tf_op jit(solution)/shard_map/attention_kernel/pallas_call | solution.py:318
  87.8 4.4 %all-to-all-start.2 = ((bf16[8,8,64,128]{3,2,1,0:T(8,128)(2,1)}), bf16[8,8,64,128]{3,2,1,0:T(8,128)(2,1)S(1)}, u32[]{:S(2)}, u32[]{:S(2)}) async-start(bf16[8,8,64,128]{3,2,1,0:T(8,128)(2,1)} %get-tuple-element.96), calls=%async_computation.2 | async-start | bytes 2097152 | tf_op jit(solution)/shard_map/all_to_all | solution.py:339
  92.2 2.0 %collective-permute-start.12 = (bf16[2,8,64,128]{3,2,1,0:T(8,128)(2,1)S(1)}, bf16[2,8,64,128]{3,2,1,0:T(8,128)(2,1)S(1)}, u32[]{:S(2)}, u32[]{:S(2)}) collective-permute-start(bf16[2,8,64,128]{3,2,1,0:T(8,128)(2,1)S(1)} %copy-done.25), channel_id=1, source_target_pairs={{0,0},{1,8},{2,16},{3,24},{4,1},{5,9},{6,17},{7,25},{8,2},{9,10},{... | collective-permute-start | bytes 786440 | tf_op jit(solution)/shard_map/ppermute | solution.py:346
  94.2 3.0 %collective-permute-start.13 = (bf16[2,8,64,128]{3,2,1,0:T(8,128)(2,1)S(1)}, bf16[2,8,64,128]{3,2,1,0:T(8,128)(2,1)S(1)}, u32[]{:S(2)}, u32[]{:S(2)}) collective-permute-start(bf16[2,8,64,128]{3,2,1,0:T(8,128)(2,1)S(1)} %copy-done.24), channel_id=1, source_target_pairs={{0,1},{1,9},{2,17},{3,25},{4,0},{5,8},{6,16},{7,24},{8,3},{9,11},{... | collective-permute-start | bytes 786440 | tf_op jit(solution)/shard_map/ppermute | solution.py:346
  98.3 4.9 %collective-permute-start.15 = (bf16[2,8,64,128]{3,2,1,0:T(8,128)(2,1)S(1)}, bf16[2,8,64,128]{3,2,1,0:T(8,128)(2,1)S(1)}, u32[]{:S(2)}, u32[]{:S(2)}) collective-permute-start(bf16[2,8,64,128]{3,2,1,0:T(8,128)(2,1)S(1)} %copy-done.22), channel_id=1, source_target_pairs={{0,3},{1,11},{2,19},{3,27},{4,2},{5,10},{6,18},{7,26},{8,1},{9,9},... | collective-permute-start | bytes 786440 | tf_op jit(solution)/shard_map/ppermute | solution.py:346
  103.2 17.5 %attention_kernel.2 = (bf16[8,8,64,128]{3,2,1,0:T(8,128)(2,1)}, bf16[2,8,64,128]{3,2,1,0:T(8,128)(2,1)}, bf16[2,8,64,128]{3,2,1,0:T(8,128)(2,1)}, bf16[2,8,64,128]{3,2,1,0:T(8,128)(2,1)}, bf16[2,8,64,128]{3,2,1,0:T(8,128)(2,1)}) custom-call(s32[4,512]{1,0:T(4,128)} %reshape.10.scalars.tokens, bf16[8,128,512]{2,1,0:T(8,128)(2,1)} %get-tuple-element.78.key, ...), custom_call_target="tpu_custom_call" | custom-call | flops 8589934592 | bytes 16777216 | tf_op jit(solution)/shard_map/attention_kernel/pallas_call | solution.py:318
  123.0 3.5 %all-to-all-start.3 = ((bf16[8,8,64,128]{3,2,1,0:T(8,128)(2,1)}), bf16[8,8,64,128]{3,2,1,0:T(8,128)(2,1)S(1)}, u32[]{:S(2)}, u32[]{:S(2)}) async-start(bf16[8,8,64,128]{3,2,1,0:T(8,128)(2,1)} %get-tuple-element.102), calls=%async_computation.3 | async-start | bytes 2097152 | tf_op jit(solution)/shard_map/all_to_all | solution.py:339
  126.6 1.9 %collective-permute-start.16 = (bf16[2,8,64,128]{3,2,1,0:T(8,128)(2,1)}, bf16[2,8,64,128]{3,2,1,0:T(8,128)(2,1)S(1)}, u32[]{:S(2)}, u32[]{:S(2)}) collective-permute-start(bf16[2,8,64,128]{3,2,1,0:T(8,128)(2,1)} %get-tuple-element.107), channel_id=1, source_target_pairs={{0,0},{1,8},{2,16},{3,24},{4,1},{5,9},{6,17},{7,25},{8,2},{9,10},{... | collective-permute-start | bytes 786440 | tf_op jit(solution)/shard_map/ppermute | solution.py:346
  128.5 4.6 %collective-permute-start.17 = (bf16[2,8,64,128]{3,2,1,0:T(8,128)(2,1)}, bf16[2,8,64,128]{3,2,1,0:T(8,128)(2,1)}, u32[]{:S(2)}, u32[]{:S(2)}) collective-permute-start(bf16[2,8,64,128]{3,2,1,0:T(8,128)(2,1)} %get-tuple-element.108), channel_id=1, source_target_pairs={{0,1},{1,9},{2,17},{3,25},{4,0},{5,8},{6,16},{7,24},{8,3},{9,11},{... | collective-permute-start | bytes 786440 | tf_op jit(solution)/shard_map/ppermute | solution.py:346
  134.1 3.7 %collective-permute-start.19 = (bf16[2,8,64,128]{3,2,1,0:T(8,128)(2,1)}, bf16[2,8,64,128]{3,2,1,0:T(8,128)(2,1)}, u32[]{:S(2)}, u32[]{:S(2)}) collective-permute-start(bf16[2,8,64,128]{3,2,1,0:T(8,128)(2,1)} %get-tuple-element.110), channel_id=1, source_target_pairs={{0,3},{1,11},{2,19},{3,27},{4,2},{5,10},{6,18},{7,26},{8,1},{9,9},... | collective-permute-start | bytes 786440 | tf_op jit(solution)/shard_map/ppermute | solution.py:346
  139.5 10.3 %collective-permute-done.16.refs_7_ = bf16[2,8,64,128]{3,2,1,0:T(8,128)(2,1)S(1)} collective-permute-done((bf16[2,8,64,128]{3,2,1,0:T(8,128)(2,1)}, bf16[2,8,64,128]{3,2,1,0:T(8,128)(2,1)S(1)}, u32[]{:S(2)}, u32[]{:S(2)}) %collective-permute-start.16) | collective-permute-done | bytes 262176 | tf_op jit(solution)/shard_map/ppermute | solution.py:346
  149.8 8.5 %collective-permute-done.17.refs_8_ = bf16[2,8,64,128]{3,2,1,0:T(8,128)(2,1)} collective-permute-done((bf16[2,8,64,128]{3,2,1,0:T(8,128)(2,1)}, bf16[2,8,64,128]{3,2,1,0:T(8,128)(2,1)}, u32[]{:S(2)}, u32[]{:S(2)}) %collective-permute-start.17) | collective-permute-done | bytes 262176 | tf_op jit(solution)/shard_map/ppermute | solution.py:346
  158.3 3.3 %collective-permute-done.19.refs_10_ = bf16[2,8,64,128]{3,2,1,0:T(8,128)(2,1)} collective-permute-done((bf16[2,8,64,128]{3,2,1,0:T(8,128)(2,1)}, bf16[2,8,64,128]{3,2,1,0:T(8,128)(2,1)}, u32[]{:S(2)}, u32[]{:S(2)}) %collective-permute-start.19) | collective-permute-done | bytes 262176 | tf_op jit(solution)/shard_map/ppermute | solution.py:346
  162.6 10.0 %logits_kernel.1 = f32[64,128,128]{2,1,0:T(8,128)} custom-call(s32[4]{0:T(128)} %pad_add_fusion.1.refs_0_, bf16[8,8,64,128]{3,2,1,0:T(8,128)(2,1)} %copy-done, bf16[8,8,64,128]{3,2,1,0:T(8,128)(2,1)} %copy-done.1, bf16[2,8,64,128]{3,2,1,0:T(8,128)(2,1)} %copy-done.4, bf16[2,8,64,128]{3,2,1,0:T(8,128)(2,1)} %copy-done.5, bf16[2,8,64,128]{3,2,1,0:T(8,128)(2,1)} %copy-done.6, ...), custom_call_target="tpu_custom_call" | custom-call | tf_op jit(solution)/shard_map/logits_kernel/pallas_call | solution.py:353
  (104 shorter events, 27.5 us)
Async XLA Ops:
  1.3 12.5 %all-to-all-start = ((s32[32,4,16]{2,1,0:T(4,128)}), s32[32,4,16]{2,1,0:T(4,128)S(1)}, u32[]{:S(2)}, u32[]{:S(2)}) async-start(s32[32,4,16]{2,1,0:T(4,128)} %broadcast_in_dim.20), calls=%async_computation | async-start | bytes 131072 | tf_op jit(solution)/shard_map/all_to_all | solution.py:241
  13.8 30.5 %all-to-all-start.1 = ((bf16[8,64,16,128]{3,2,1,0:T(8,128)(2,1)}), bf16[8,64,16,128]{3,2,1,0:T(8,128)(2,1)S(1)}, u32[]{:S(2)}, u32[]{:S(2)}) async-start(bf16[8,64,16,128]{3,2,1,0:T(8,128)(2,1)} %bitcast.20), calls=%async_computation.1 | async-start | bytes 4194304 | tf_op jit(solution)/shard_map/all_to_all | solution.py:245
  26.4 7.6 %collective-permute-start = (f32[2,128,128]{2,1,0:T(8,128)}, f32[2,128,128]{2,1,0:T(8,128)S(1)}, u32[]{:S(2)}, u32[]{:S(2)}) collective-permute-start(f32[2,128,128]{2,1,0:T(8,128)} %bias_kernel.1), channel_id=1, source_target_pairs={{0,1},{1,0},{2,3},{3,2},{4,5},{5,4},{6,7},{7,6},{8,9},{9,8},{10,11... | collective-permute-start | bytes 393224 | tf_op jit(solution)/shard_map/ppermute | solution.py:214
  26.6 13.1 %collective-permute-start.1 = (f32[2,128,128]{2,1,0:T(8,128)}, f32[2,128,128]{2,1,0:T(8,128)S(1)}, u32[]{:S(2)}, u32[]{:S(2)}) collective-permute-start(f32[2,128,128]{2,1,0:T(8,128)} %bias_kernel.1), channel_id=1, source_target_pairs={{0,2},{1,3},{2,0},{3,1},{4,6},{5,7},{6,4},{7,5},{8,10},{9,11},{10,... | collective-permute-start | bytes 393224 | tf_op jit(solution)/shard_map/ppermute | solution.py:214
  27.8 12.0 %collective-permute-start.2 = (f32[2,128,128]{2,1,0:T(8,128)}, f32[2,128,128]{2,1,0:T(8,128)S(1)}, u32[]{:S(2)}, u32[]{:S(2)}) collective-permute-start(f32[2,128,128]{2,1,0:T(8,128)} %bias_kernel.1), channel_id=1, source_target_pairs={{0,3},{1,2},{2,1},{3,0},{4,7},{5,6},{6,5},{7,4},{8,11},{9,10},{10,... | collective-permute-start | bytes 393224 | tf_op jit(solution)/shard_map/ppermute | solution.py:214
  40.7 14.5 %collective-permute-start.3 = (f32[4,2,128,128]{3,2,1,0:T(8,128)S(1)}, f32[4,2,128,128]{3,2,1,0:T(8,128)S(1)}, u32[]{:S(2)}, u32[]{:S(2)}) collective-permute-start(f32[4,2,128,128]{3,2,1,0:T(8,128)S(1)} %pad_maximum_fusion.refs_0_), channel_id=1, source_target_pairs={{0,8},{4,12},{8,0},{12,4},{16,24},{20,28},{24,16},{28,20},{1,9},{5... | collective-permute-start | bytes 1572872 | tf_op jit(solution)/shard_map/ppermute | solution.py:214
  42.2 13.0 %collective-permute-start.4 = (f32[4,2,128,128]{3,2,1,0:T(8,128)S(1)}, f32[4,2,128,128]{3,2,1,0:T(8,128)}, u32[]{:S(2)}, u32[]{:S(2)}) collective-permute-start(f32[4,2,128,128]{3,2,1,0:T(8,128)S(1)} %pad_maximum_fusion.refs_0_), channel_id=1, source_target_pairs={{0,16},{4,20},{8,24},{12,28},{16,0},{20,4},{24,8},{28,12},{1,17},{... | collective-permute-start | bytes 1572872 | tf_op jit(solution)/shard_map/ppermute | solution.py:214
  56.4 9.9 %collective-permute-start.5 = (f32[2,2,128,128]{3,2,1,0:T(8,128)S(1)}, f32[2,2,128,128]{3,2,1,0:T(8,128)S(1)}, u32[]{:S(2)}, u32[]{:S(2)}) collective-permute-start(f32[2,2,128,128]{3,2,1,0:T(8,128)S(1)} %slice.18), channel_id=1, source_target_pairs={{0,8},{4,12},{8,0},{12,4},{16,24},{20,28},{24,16},{28,20},{1,9},{5... | collective-permute-start | bytes 786440 | tf_op jit(solution)/shard_map/ppermute | solution.py:214
  57.0 9.3 %collective-permute-start.6 = (f32[2,2,128,128]{3,2,1,0:T(8,128)S(1)}, f32[2,2,128,128]{3,2,1,0:T(8,128)S(1)}, u32[]{:S(2)}, u32[]{:S(2)}) collective-permute-start(f32[2,2,128,128]{3,2,1,0:T(8,128)S(1)} %slice.19), channel_id=1, source_target_pairs={{0,16},{4,20},{8,24},{12,28},{16,0},{20,4},{24,8},{28,12},{1,17},{... | collective-permute-start | bytes 786440 | tf_op jit(solution)/shard_map/ppermute | solution.py:214
  58.4 10.1 %collective-permute-start.7 = (f32[4,2,128,128]{3,2,1,0:T(8,128)S(1)}, f32[4,2,128,128]{3,2,1,0:T(8,128)S(1)}, u32[]{:S(2)}, u32[]{:S(2)}) collective-permute-start(f32[4,2,128,128]{3,2,1,0:T(8,128)S(1)} %pad_maximum_fusion.refs_0_), channel_id=1, source_target_pairs={{0,4},{4,0},{8,12},{12,8},{16,20},{20,16},{24,28},{28,24},{1,5},{5... | collective-permute-start | bytes 1572872 | tf_op jit(solution)/shard_map/ppermute | solution.py:214
  58.4 10.1 %collective-permute-start.8 = (f32[4,2,128,128]{3,2,1,0:T(8,128)S(1)}, f32[4,2,128,128]{3,2,1,0:T(8,128)S(1)}, u32[]{:S(2)}, u32[]{:S(2)}) collective-permute-start(f32[4,2,128,128]{3,2,1,0:T(8,128)S(1)} %collective-permute-done.3.refs_2_), channel_id=1, source_target_pairs={{0,4},{4,0},{8,12},{12,8},{16,20},{20,16},{24,28},{28,24},{1,5},{5... | collective-permute-start | bytes 1572872 | tf_op jit(solution)/shard_map/ppermute | solution.py:214
  58.9 9.6 %collective-permute-start.9 = (f32[4,2,128,128]{3,2,1,0:T(8,128)}, f32[4,2,128,128]{3,2,1,0:T(8,128)S(1)}, u32[]{:S(2)}, u32[]{:S(2)}) collective-permute-start(f32[4,2,128,128]{3,2,1,0:T(8,128)} %collective-permute-done.4.refs_4_), channel_id=1, source_target_pairs={{0,4},{4,0},{8,12},{12,8},{16,20},{20,16},{24,28},{28,24},{1,5},{5... | collective-permute-start | bytes 1572872 | tf_op jit(solution)/shard_map/ppermute | solution.py:214
  66.3 1.7 collective-permute-start.10
  66.9 1.5 collective-permute-start.11
  87.8 35.2 %all-to-all-start.2 = ((bf16[8,8,64,128]{3,2,1,0:T(8,128)(2,1)}), bf16[8,8,64,128]{3,2,1,0:T(8,128)(2,1)S(1)}, u32[]{:S(2)}, u32[]{:S(2)}) async-start(bf16[8,8,64,128]{3,2,1,0:T(8,128)(2,1)} %get-tuple-element.96), calls=%async_computation.2 | async-start | bytes 2097152 | tf_op jit(solution)/shard_map/all_to_all | solution.py:339
  92.2 28.6 %collective-permute-start.12 = (bf16[2,8,64,128]{3,2,1,0:T(8,128)(2,1)S(1)}, bf16[2,8,64,128]{3,2,1,0:T(8,128)(2,1)S(1)}, u32[]{:S(2)}, u32[]{:S(2)}) collective-permute-start(bf16[2,8,64,128]{3,2,1,0:T(8,128)(2,1)S(1)} %copy-done.25), channel_id=1, source_target_pairs={{0,0},{1,8},{2,16},{3,24},{4,1},{5,9},{6,17},{7,25},{8,2},{9,10},{... | collective-permute-start | bytes 786440 | tf_op jit(solution)/shard_map/ppermute | solution.py:346
  94.2 27.4 %collective-permute-start.13 = (bf16[2,8,64,128]{3,2,1,0:T(8,128)(2,1)S(1)}, bf16[2,8,64,128]{3,2,1,0:T(8,128)(2,1)S(1)}, u32[]{:S(2)}, u32[]{:S(2)}) collective-permute-start(bf16[2,8,64,128]{3,2,1,0:T(8,128)(2,1)S(1)} %copy-done.24), channel_id=1, source_target_pairs={{0,1},{1,9},{2,17},{3,25},{4,0},{5,8},{6,16},{7,24},{8,3},{9,11},{... | collective-permute-start | bytes 786440 | tf_op jit(solution)/shard_map/ppermute | solution.py:346
  97.3 24.4 %collective-permute-start.14 = (bf16[2,8,64,128]{3,2,1,0:T(8,128)(2,1)S(1)}, bf16[2,8,64,128]{3,2,1,0:T(8,128)(2,1)S(1)}, u32[]{:S(2)}, u32[]{:S(2)}) collective-permute-start(bf16[2,8,64,128]{3,2,1,0:T(8,128)(2,1)S(1)} %copy-done.23), channel_id=1, source_target_pairs={{0,2},{1,10},{2,18},{3,26},{4,3},{5,11},{6,19},{7,27},{8,0},{9,8},... | collective-permute-start | bytes 786440 | tf_op jit(solution)/shard_map/ppermute | solution.py:346
  98.3 24.8 %collective-permute-start.15 = (bf16[2,8,64,128]{3,2,1,0:T(8,128)(2,1)S(1)}, bf16[2,8,64,128]{3,2,1,0:T(8,128)(2,1)S(1)}, u32[]{:S(2)}, u32[]{:S(2)}) collective-permute-start(bf16[2,8,64,128]{3,2,1,0:T(8,128)(2,1)S(1)} %copy-done.22), channel_id=1, source_target_pairs={{0,3},{1,11},{2,19},{3,27},{4,2},{5,10},{6,18},{7,26},{8,1},{9,9},... | collective-permute-start | bytes 786440 | tf_op jit(solution)/shard_map/ppermute | solution.py:346
  123.0 38.6 %all-to-all-start.3 = ((bf16[8,8,64,128]{3,2,1,0:T(8,128)(2,1)}), bf16[8,8,64,128]{3,2,1,0:T(8,128)(2,1)S(1)}, u32[]{:S(2)}, u32[]{:S(2)}) async-start(bf16[8,8,64,128]{3,2,1,0:T(8,128)(2,1)} %get-tuple-element.102), calls=%async_computation.3 | async-start | bytes 2097152 | tf_op jit(solution)/shard_map/all_to_all | solution.py:339
  126.6 23.2 %collective-permute-start.16 = (bf16[2,8,64,128]{3,2,1,0:T(8,128)(2,1)}, bf16[2,8,64,128]{3,2,1,0:T(8,128)(2,1)S(1)}, u32[]{:S(2)}, u32[]{:S(2)}) collective-permute-start(bf16[2,8,64,128]{3,2,1,0:T(8,128)(2,1)} %get-tuple-element.107), channel_id=1, source_target_pairs={{0,0},{1,8},{2,16},{3,24},{4,1},{5,9},{6,17},{7,25},{8,2},{9,10},{... | collective-permute-start | bytes 786440 | tf_op jit(solution)/shard_map/ppermute | solution.py:346
  128.5 29.8 %collective-permute-start.17 = (bf16[2,8,64,128]{3,2,1,0:T(8,128)(2,1)}, bf16[2,8,64,128]{3,2,1,0:T(8,128)(2,1)}, u32[]{:S(2)}, u32[]{:S(2)}) collective-permute-start(bf16[2,8,64,128]{3,2,1,0:T(8,128)(2,1)} %get-tuple-element.108), channel_id=1, source_target_pairs={{0,1},{1,9},{2,17},{3,25},{4,0},{5,8},{6,16},{7,24},{8,3},{9,11},{... | collective-permute-start | bytes 786440 | tf_op jit(solution)/shard_map/ppermute | solution.py:346
  133.1 25.1 %collective-permute-start.18 = (bf16[2,8,64,128]{3,2,1,0:T(8,128)(2,1)}, bf16[2,8,64,128]{3,2,1,0:T(8,128)(2,1)}, u32[]{:S(2)}, u32[]{:S(2)}) collective-permute-start(bf16[2,8,64,128]{3,2,1,0:T(8,128)(2,1)} %get-tuple-element.109), channel_id=1, source_target_pairs={{0,2},{1,10},{2,18},{3,26},{4,3},{5,11},{6,19},{7,27},{8,0},{9,8},... | collective-permute-start | bytes 786440 | tf_op jit(solution)/shard_map/ppermute | solution.py:346
  134.1 27.5 %collective-permute-start.19 = (bf16[2,8,64,128]{3,2,1,0:T(8,128)(2,1)}, bf16[2,8,64,128]{3,2,1,0:T(8,128)(2,1)}, u32[]{:S(2)}, u32[]{:S(2)}) collective-permute-start(bf16[2,8,64,128]{3,2,1,0:T(8,128)(2,1)} %get-tuple-element.110), channel_id=1, source_target_pairs={{0,3},{1,11},{2,19},{3,27},{4,2},{5,10},{6,18},{7,26},{8,1},{9,9},... | collective-permute-start | bytes 786440 | tf_op jit(solution)/shard_map/ppermute | solution.py:346
  (27 other events, 370.6 us)

commit v5 on v4

--- a/solution.py
+++ b/solution.py
@@ -14,9 +14,11 @@
 AXES = ("row", "col")
 
 
-def normalise(values):
-    average = jnp.mean(values, axis=-1, keepdims=True)
-    centred = values - average
+def normalise(values, parts):
+    width = values.shape[1]
+    stacked = jnp.concatenate(parts, axis=1) if len(parts) > 1 else parts[0]
+    weight = jnp.full((stacked.shape[1], width), 1.0 / width, BF16)
+    centred = values - jnp.dot(stacked, weight, preferred_element_type=F32)
     variance = jnp.mean(centred * centred, axis=-1, keepdims=True)
     return (centred * lax.rsqrt(variance + 1e-05)).astype(BF16)
 
@@ -58,7 +60,7 @@
         values = z[pl.ds(first, batch)].reshape(batch * cols_dev, width).astype(F32)
         squares = [squared_distance(spread, scalars, row_at * rows_dev + first + at) for at in range(batch)]
         pair = embed(squares, low, high, w_dist, values)
-        normed = normalise(pair.astype(F32))
+        normed = normalise(pair.astype(F32), [pair])
         lines = lax.dot_general(w_bias[...], normed, NT, preferred_element_type=F32)
         for at in range(batch):
             for head in range(heads):
@@ -101,7 +103,7 @@
     values = jnp.concatenate([wide[pl.ds(done - lowest + first + at, total, stride=pitch), :] for at in range(batch)], axis=0)
     squares = [squared_distance(spread, scalars, own + at) for at in range(batch)]
     rounded = embed(squares, low, high, w_dist, values)
-    normed = normalise(rounded.astype(F32))
+    normed = normalise(rounded.astype(F32), [rounded])
     rest = jnp.dot(normed, w_rest[...], preferred_element_type=F32)
     odd_lane = lax.broadcasted_iota(jnp.int32, (1, width), 1) // head_dim % 2 == 1
     odd_row = lax.broadcasted_iota(jnp.int32, (width, 1), 0) // head_dim % 2 == 1
@@ -152,6 +154,7 @@
     own_key, own_query = key[0], query[0]
     own_value = jnp.concatenate([value[0], jnp.ones((total, width), BF16)], axis=1)
     blocks = [jnp.zeros((cols_dev, width), F32)] * (total // cols_dev)
+    wholes = list(blocks)
     for head in range(heads):
         inside = lane // head_dim == head
         for at in range(len(blocks)):
@@ -162,8 +165,9 @@
             highest = jnp.max(score, axis=1, keepdims=True)
             raised = jnp.exp(score - highest).astype(BF16)
             summed = jnp.dot(raised, own_value, preferred_element_type=F32)
-            blocks[at] = jnp.where(inside, summed[:, :width] / summed[:, width:], blocks[at])
-    attended = jnp.concatenate(blocks, axis=0)
+            blocks[at] = jnp.where(inside, summed[:, :width], blocks[at])
+            wholes[at] = jnp.where(inside, summed[:, width:], wholes[at])
+    attended = jnp.concatenate(blocks, axis=0) / jnp.concatenate(wholes, axis=0)
     gated = (jax.nn.sigmoid(gate[0].astype(F32)) * attended).astype(BF16)
     update = jnp.dot(gated, w_out[...], preferred_element_type=F32)
     result[...] = (pair[0].astype(F32) + update).astype(BF16).reshape(result.shape)
@@ -204,8 +208,10 @@
                 for at in range(parts[step]):
                     mine.append(wide[pl.ds(first + done + at, cols_dev, stride=pitch), :])
                     other += [mirrored[step * n_cols + shift][half, at] for half in range(halves)]
-                mine, other = jnp.concatenate(mine, axis=0), jnp.concatenate(other, axis=0).astype(F32)
-                both = jnp.concatenate([normalise(mine), normalise(mine + other)], axis=1)
+                mine, other = jnp.concatenate(mine, axis=0), jnp.concatenate(other, axis=0)
+                short = mine.astype(BF16)
+                summed = mine + other.astype(F32)
+                both = jnp.concatenate([normalise(mine, [short]), normalise(summed, [short, other])], axis=1)
                 found = jnp.dot(both, w_both[...], preferred_element_type=F32)
                 logits[done : done + parts[step]] = found.reshape(parts[step], cols_dev, found.shape[1])
 
@@ -241,7 +247,8 @@
     tokens = lax.all_to_all(copies, AXES, split_axis=0, concat_axis=0, tiled=True)
     tokens = tokens.transpose(1, 0, 2).reshape(4, total)
     z_parts = z_trunk.reshape(rows_dev, n_rows, slab, width).swapaxes(0, 1)
-    z_parts, w_dist_full, w_bias_t = lax.optimization_barrier((z_parts, w_dist_full, w_bias_t))
+    early = (z_parts, w_dist_full, w_bias_t, low, high)
+    z_parts, w_dist_full, w_bias_t, low, high = lax.optimization_barrier(early)
     z_cols = lax.all_to_all(z_parts, "row", split_axis=0, concat_axis=0, tiled=True)
     z_cols = z_cols.reshape(total, slab, width)
 
@@ -281,7 +288,7 @@
             grid=(part // batch,),
             in_specs=[smem, whole(tokens), vmem, vmem, whole(z_cols), vmem, vmem, vmem],
             out_specs=(by_rows, by_lanes, by_rows, by_rows, by_rows),
-            scratch_shapes=[pltpu.VMEM((total * spread_rows, width), F32), pltpu.VMEM((3, total, width), F32)],
+            scratch_shapes=[pltpu.VMEM(((total + 1) * spread_rows, width), F32), pltpu.VMEM((3, total, width), F32)],
             compiler_params=params,
             cost_estimate=pl.CostEstimate(
                 flops=total * part * width * 2000, bytes_accessed=1 << 23, transcendentals=0
@@ -358,7 +365,7 @@
             grid=(n_cols,),
             in_specs=[whole(array) for array in own + mirrored + [w_both]],
             out_specs=pl.BlockSpec((slab, cols_dev, 2 * bins), lambda b, at: (at[b], 0, 0)),
-            scratch_shapes=[pltpu.VMEM((cols_dev * (rows_dev + 8), width), F32)],
+            scratch_shapes=[pltpu.VMEM(((cols_dev + 1) * (rows_dev + 8), width), F32)],
         ),
         compiler_params=params,
         name="logits_kernel",

time: 173 us -> 170 us (0.983)
  Pallas kernels: 66.1 us -> 61.7 us
  waiting for transfers between devices: 39 us -> 42.7 us
  starting transfers between devices: 50.6 us -> 47.9 us
    ppermute x8, starting transfers between devices: 22.2 us -> 19.1 us  [per_device(): mirrored.append(lax.ppermute(turned[shift], AXES, hops))]
    pallas_call x2, Pallas kernels: 14.8 us -> 12.2 us  [project(): pl.pallas_call(functools.partial(project_kernel, head_dim, batch, done, p...]
    ppermute x8, waiting for transfers between devices: 24.4 us -> 26.3 us  [per_device(): mirrored.append(lax.ppermute(turned[shift], AXES, hops))]
  transfers between devices with their start and end apart: 24 -> 24, of which waited for: 12 -> 13; matrix products, arithmetic and copies ran while one was open for 6% -> 6% of each run, Pallas kernels for 22% -> 21%
where the time goes in v5:
time: 170 us; the launch traced here: 169 us
  Pallas kernels  61.7 us (36%)
  starting transfers between devices  47.9 us (28%)
  waiting for transfers between devices  42.7 us (25%)
  local copies, waits for them, and re-layouts  12.2 us (7%)
  other arithmetic  4.3 us (3%)
    pallas_call x2, Pallas kernels, per_device(): pl.pallas_call(functools.partial(attention_kernel, heads, n_cols, splits)...  34.9 us
    ppermute x8, waiting for transfers between devices, per_device(): mirrored.append(lax.ppermute(turned[shift], AXES, hops))  26.3 us
    ppermute x8, starting transfers between devices, per_device(): mirrored.append(lax.ppermute(turned[shift], AXES, hops))  19.1 us
    ppermute x12, waiting for transfers between devices, swap_over(): return lax.ppermute(array, axis, [(at, at ^ step) for at in range(count)])  13.8 us
    pallas_call x2, Pallas kernels, project(): pl.pallas_call(functools.partial(project_kernel, head_dim, batch, done, p...  12.2 us
    ppermute x12, starting transfers between devices, swap_over(): return lax.ppermute(array, axis, [(at, at ^ step) for at in range(count)])  9.53 us
    pallas_call x1, Pallas kernels, per_device(): pl.pallas_call(functools.partial(logits_kernel, n_cols, parts), out_shape...  8.75 us
    all_to_all x2, starting transfers between devices, per_device(): lax.all_to_all(updated, 'row', split_axis=0, concat_axis=0, tiled=True)  8.32 us
  transfers between devices with their start and end apart: 24, of which 13 were waited for; matrix products, arithmetic and copies ran while one was open for 6% of the time, Pallas kernels for 21%

profile of v5, /device:TPU:4, one launch (start us, length us, event | category | flops | bytes accessed | tf_op | source)
XLA Modules:
  0.0 169.1 jit_solution(9017742851306519346)
XLA Ops:
  1.3 6.1 %all-to-all-start = ((s32[32,4,16]{2,1,0:T(4,128)}), s32[32,4,16]{2,1,0:T(4,128)S(1)}, u32[]{:S(2)}, u32[]{:S(2)}) async-start(s32[32,4,16]{2,1,0:T(4,128)} %broadcast_in_dim.20), calls=%async_computation | async-start | bytes 131072 | tf_op jit(solution)/shard_map/all_to_all | solution.py:247
  8.1 3.3 %copy.25 = bf16[64,8,16,128]{3,2,0,1:T(8,128)(2,1)} copy(bf16[64,8,16,128]{3,2,1,0:T(8,128)(2,1)} %bitcast.21) | data formatting | bytes 4194304 | tf_op jit(solution)/shard_map/reshape | solution.py:249
  13.8 4.9 %all-to-all-start.1 = ((bf16[8,64,16,128]{3,2,1,0:T(8,128)(2,1)}), bf16[8,64,16,128]{3,2,1,0:T(8,128)(2,1)S(1)}, u32[]{:S(2)}, u32[]{:S(2)}) async-start(bf16[8,64,16,128]{3,2,1,0:T(8,128)(2,1)} %bitcast.20), calls=%async_computation.1 | async-start | bytes 4194304 | tf_op jit(solution)/shard_map/all_to_all | solution.py:252
  19.4 5.9 %bias_kernel.1 = f32[2,128,128]{2,1,0:T(8,128)} custom-call(s32[4,512]{1,0:T(4,128)} %reshape.10.scalars.tokens, s32[4,512]{1,0:T(4,128)} %reshape.10.scalars.tokens, f32[1,128]{1,0:T(1,128)} %get-tuple-element.60.low, f32[1,128]{1,0:T(1,128)} %get-tuple-element.61.high, bf16[64,128,128]{2,1,0:T(8,128)(2,1)} %z.1, bf16[128,128]{1,0:T(8,128)(2,1)} %pad.17.w_dist, ...), custom_call_target="tpu_custom_call" | custom-call | flops 314572800 | bytes 4194304 | tf_op jit(solution)/shard_map/bias_kernel/pallas_call | solution.py:255
  27.3 2.4 %collective-permute-start.2 = (f32[2,128,128]{2,1,0:T(8,128)}, f32[2,128,128]{2,1,0:T(8,128)S(1)}, u32[]{:S(2)}, u32[]{:S(2)}) collective-permute-start(f32[2,128,128]{2,1,0:T(8,128)} %bias_kernel.1), channel_id=1, source_target_pairs={{0,3},{1,2},{2,1},{3,0},{4,7},{5,6},{6,5},{7,4},{8,11},{9,10},{10,... | collective-permute-start | bytes 393224 | tf_op jit(solution)/shard_map/ppermute | solution.py:220
  29.7 3.2 %collective-permute-done = f32[2,128,128]{2,1,0:T(8,128)S(1)} collective-permute-done((f32[2,128,128]{2,1,0:T(8,128)}, f32[2,128,128]{2,1,0:T(8,128)S(1)}, u32[]{:S(2)}, u32[]{:S(2)}) %collective-permute-start) | collective-permute-done | bytes 131104 | tf_op jit(solution)/shard_map/ppermute | solution.py:220
  32.9 5.7 %collective-permute-done.1 = f32[2,128,128]{2,1,0:T(8,128)S(1)} collective-permute-done((f32[2,128,128]{2,1,0:T(8,128)}, f32[2,128,128]{2,1,0:T(8,128)S(1)}, u32[]{:S(2)}, u32[]{:S(2)}) %collective-permute-start.1) | collective-permute-done | bytes 131104 | tf_op jit(solution)/shard_map/ppermute | solution.py:220
  45.7 6.1 %project_kernel.2 = (bf16[8,512,128]{2,1,0:T(8,128)(2,1)}, bf16[8,128,512]{2,1,0:T(8,128)(2,1)}, bf16[8,512,128]{2,1,0:T(8,128)(2,1)}, bf16[8,512,128]{2,1,0:T(8,128)(2,1)}, bf16[8,512,128]{2,1,0:T(8,128)(2,1)}) custom-call(s32[4,512]{1,0:T(4,128)} %reshape.10.scalars.tokens, s32[4,512]{1,0:T(4,128)} %reshape.10.scalars.tokens, ...), custom_call_target="tpu_custom_call" | custom-call | flops 1048576000 | bytes 8388608 | tf_op jit(solution)/shard_map/project_kernel/pallas_call | solution.py:285
  51.8 3.4 %collective-permute-done.3.refs_2_ = f32[4,2,128,128]{3,2,1,0:T(8,128)S(1)} collective-permute-done((f32[4,2,128,128]{3,2,1,0:T(8,128)S(1)}, f32[4,2,128,128]{3,2,1,0:T(8,128)S(1)}, u32[]{:S(2)}, u32[]{:S(2)}) %collective-permute-start.3) | collective-permute-done | bytes 524320 | tf_op jit(solution)/shard_map/ppermute | solution.py:220
  58.9 6.1 %project_kernel.3 = (bf16[8,512,128]{2,1,0:T(8,128)(2,1)}, bf16[8,128,512]{2,1,0:T(8,128)(2,1)}, bf16[8,512,128]{2,1,0:T(8,128)(2,1)}, bf16[8,512,128]{2,1,0:T(8,128)(2,1)}, bf16[8,512,128]{2,1,0:T(8,128)(2,1)}) custom-call(s32[4,512]{1,0:T(4,128)} %reshape.10.scalars.tokens, s32[4,512]{1,0:T(4,128)} %reshape.10.scalars.tokens, ...), custom_call_target="tpu_custom_call" | custom-call | flops 1048576000 | bytes 8388608 | tf_op jit(solution)/shard_map/project_kernel/pallas_call | solution.py:285
  69.0 17.4 %attention_kernel.3 = (bf16[8,8,64,128]{3,2,1,0:T(8,128)(2,1)}, bf16[2,8,64,128]{3,2,1,0:T(8,128)(2,1)}, bf16[2,8,64,128]{3,2,1,0:T(8,128)(2,1)}, bf16[2,8,64,128]{3,2,1,0:T(8,128)(2,1)}, bf16[2,8,64,128]{3,2,1,0:T(8,128)(2,1)}) custom-call(s32[4,512]{1,0:T(4,128)} %reshape.10.scalars.tokens, bf16[8,128,512]{2,1,0:T(8,128)(2,1)} %get-tuple-element.95.key, ...), custom_call_target="tpu_custom_call" | custom-call | flops 8589934592 | bytes 16777216 | tf_op jit(solution)/shard_map/attention_kernel/pallas_call | solution.py:325
  86.4 4.8 %all-to-all-start.2 = ((bf16[8,8,64,128]{3,2,1,0:T(8,128)(2,1)}), bf16[8,8,64,128]{3,2,1,0:T(8,128)(2,1)S(1)}, u32[]{:S(2)}, u32[]{:S(2)}) async-start(bf16[8,8,64,128]{3,2,1,0:T(8,128)(2,1)} %get-tuple-element.100), calls=%async_computation.2 | async-start | bytes 2097152 | tf_op jit(solution)/shard_map/all_to_all | solution.py:346
  91.2 2.0 %collective-permute-start.12 = (bf16[2,8,64,128]{3,2,1,0:T(8,128)(2,1)S(1)}, bf16[2,8,64,128]{3,2,1,0:T(8,128)(2,1)S(1)}, u32[]{:S(2)}, u32[]{:S(2)}) collective-permute-start(bf16[2,8,64,128]{3,2,1,0:T(8,128)(2,1)S(1)} %copy-done.25), channel_id=1, source_target_pairs={{0,0},{1,8},{2,16},{3,24},{4,1},{5,9},{6,17},{7,25},{8,2},{9,10},{... | collective-permute-start | bytes 786440 | tf_op jit(solution)/shard_map/ppermute | solution.py:353
  94.8 2.0 %collective-permute-start.14 = (bf16[2,8,64,128]{3,2,1,0:T(8,128)(2,1)S(1)}, bf16[2,8,64,128]{3,2,1,0:T(8,128)(2,1)S(1)}, u32[]{:S(2)}, u32[]{:S(2)}) collective-permute-start(bf16[2,8,64,128]{3,2,1,0:T(8,128)(2,1)S(1)} %copy-done.23), channel_id=1, source_target_pairs={{0,2},{1,10},{2,18},{3,26},{4,3},{5,11},{6,19},{7,27},{8,0},{9,8},... | collective-permute-start | bytes 786440 | tf_op jit(solution)/shard_map/ppermute | solution.py:353
  96.8 3.9 %collective-permute-start.15 = (bf16[2,8,64,128]{3,2,1,0:T(8,128)(2,1)S(1)}, bf16[2,8,64,128]{3,2,1,0:T(8,128)(2,1)S(1)}, u32[]{:S(2)}, u32[]{:S(2)}) collective-permute-start(bf16[2,8,64,128]{3,2,1,0:T(8,128)(2,1)S(1)} %copy-done.22), channel_id=1, source_target_pairs={{0,3},{1,11},{2,19},{3,27},{4,2},{5,10},{6,18},{7,26},{8,1},{9,9},... | collective-permute-start | bytes 786440 | tf_op jit(solution)/shard_map/ppermute | solution.py:353
  100.7 17.5 %attention_kernel.2 = (bf16[8,8,64,128]{3,2,1,0:T(8,128)(2,1)}, bf16[2,8,64,128]{3,2,1,0:T(8,128)(2,1)}, bf16[2,8,64,128]{3,2,1,0:T(8,128)(2,1)}, bf16[2,8,64,128]{3,2,1,0:T(8,128)(2,1)}, bf16[2,8,64,128]{3,2,1,0:T(8,128)(2,1)}) custom-call(s32[4,512]{1,0:T(4,128)} %reshape.10.scalars.tokens, bf16[8,128,512]{2,1,0:T(8,128)(2,1)} %get-tuple-element.82.key, ...), custom_call_target="tpu_custom_call" | custom-call | flops 8589934592 | bytes 16777216 | tf_op jit(solution)/shard_map/attention_kernel/pallas_call | solution.py:325
  118.6 3.6 %collective-permute-done.15.refs_6_ = bf16[2,8,64,128]{3,2,1,0:T(8,128)(2,1)S(1)} collective-permute-done((bf16[2,8,64,128]{3,2,1,0:T(8,128)(2,1)S(1)}, bf16[2,8,64,128]{3,2,1,0:T(8,128)(2,1)S(1)}, u32[]{:S(2)}, u32[]{:S(2)}) %collective-permute-start.15) | collective-permute-done | bytes 262176 | tf_op jit(solution)/shard_map/ppermute | solution.py:353
  122.2 3.5 %all-to-all-start.3 = ((bf16[8,8,64,128]{3,2,1,0:T(8,128)(2,1)}), bf16[8,8,64,128]{3,2,1,0:T(8,128)(2,1)S(1)}, u32[]{:S(2)}, u32[]{:S(2)}) async-start(bf16[8,8,64,128]{3,2,1,0:T(8,128)(2,1)} %get-tuple-element.106), calls=%async_computation.3 | async-start | bytes 2097152 | tf_op jit(solution)/shard_map/all_to_all | solution.py:346
  127.7 2.9 %collective-permute-start.17 = (bf16[2,8,64,128]{3,2,1,0:T(8,128)(2,1)}, bf16[2,8,64,128]{3,2,1,0:T(8,128)(2,1)}, u32[]{:S(2)}, u32[]{:S(2)}) collective-permute-start(bf16[2,8,64,128]{3,2,1,0:T(8,128)(2,1)} %get-tuple-element.112), channel_id=1, source_target_pairs={{0,1},{1,9},{2,17},{3,25},{4,0},{5,8},{6,16},{7,24},{8,3},{9,11},{... | collective-permute-start | bytes 786440 | tf_op jit(solution)/shard_map/ppermute | solution.py:353
  131.6 3.7 %collective-permute-start.19 = (bf16[2,8,64,128]{3,2,1,0:T(8,128)(2,1)}, bf16[2,8,64,128]{3,2,1,0:T(8,128)(2,1)}, u32[]{:S(2)}, u32[]{:S(2)}) collective-permute-start(bf16[2,8,64,128]{3,2,1,0:T(8,128)(2,1)} %get-tuple-element.114), channel_id=1, source_target_pairs={{0,3},{1,11},{2,19},{3,27},{4,2},{5,10},{6,18},{7,26},{8,1},{9,9},... | collective-permute-start | bytes 786440 | tf_op jit(solution)/shard_map/ppermute | solution.py:353
  137.0 13.1 %collective-permute-done.16.refs_7_ = bf16[2,8,64,128]{3,2,1,0:T(8,128)(2,1)S(1)} collective-permute-done((bf16[2,8,64,128]{3,2,1,0:T(8,128)(2,1)}, bf16[2,8,64,128]{3,2,1,0:T(8,128)(2,1)S(1)}, u32[]{:S(2)}, u32[]{:S(2)}) %collective-permute-start.16) | collective-permute-done | bytes 262176 | tf_op jit(solution)/shard_map/ppermute | solution.py:353
  150.1 5.2 %collective-permute-done.17.refs_8_ = bf16[2,8,64,128]{3,2,1,0:T(8,128)(2,1)} collective-permute-done((bf16[2,8,64,128]{3,2,1,0:T(8,128)(2,1)}, bf16[2,8,64,128]{3,2,1,0:T(8,128)(2,1)}, u32[]{:S(2)}, u32[]{:S(2)}) %collective-permute-start.17) | collective-permute-done | bytes 262176 | tf_op jit(solution)/shard_map/ppermute | solution.py:353
  155.3 4.0 %collective-permute-done.19.refs_10_ = bf16[2,8,64,128]{3,2,1,0:T(8,128)(2,1)} collective-permute-done((bf16[2,8,64,128]{3,2,1,0:T(8,128)(2,1)}, bf16[2,8,64,128]{3,2,1,0:T(8,128)(2,1)}, u32[]{:S(2)}, u32[]{:S(2)}) %collective-permute-start.19) | collective-permute-done | bytes 262176 | tf_op jit(solution)/shard_map/ppermute | solution.py:353
  160.3 8.7 %logits_kernel.1 = f32[64,128,128]{2,1,0:T(8,128)} custom-call(s32[4]{0:T(128)} %pad_add_fusion.1.refs_0_, bf16[8,8,64,128]{3,2,1,0:T(8,128)(2,1)} %copy-done, bf16[8,8,64,128]{3,2,1,0:T(8,128)(2,1)} %copy-done.1, bf16[2,8,64,128]{3,2,1,0:T(8,128)(2,1)} %copy-done.4, bf16[2,8,64,128]{3,2,1,0:T(8,128)(2,1)} %copy-done.5, bf16[2,8,64,128]{3,2,1,0:T(8,128)(2,1)} %copy-done.6, ...), custom_call_target="tpu_custom_call" | custom-call | tf_op jit(solution)/shard_map/logits_kernel/pallas_call | solution.py:360
  (104 shorter events, 29.3 us)
Async XLA Ops:
  1.3 12.5 %all-to-all-start = ((s32[32,4,16]{2,1,0:T(4,128)}), s32[32,4,16]{2,1,0:T(4,128)S(1)}, u32[]{:S(2)}, u32[]{:S(2)}) async-start(s32[32,4,16]{2,1,0:T(4,128)} %broadcast_in_dim.20), calls=%async_computation | async-start | bytes 131072 | tf_op jit(solution)/shard_map/all_to_all | solution.py:247
  13.8 30.6 %all-to-all-start.1 = ((bf16[8,64,16,128]{3,2,1,0:T(8,128)(2,1)}), bf16[8,64,16,128]{3,2,1,0:T(8,128)(2,1)S(1)}, u32[]{:S(2)}, u32[]{:S(2)}) async-start(bf16[8,64,16,128]{3,2,1,0:T(8,128)(2,1)} %bitcast.20), calls=%async_computation.1 | async-start | bytes 4194304 | tf_op jit(solution)/shard_map/all_to_all | solution.py:252
  25.3 7.6 %collective-permute-start = (f32[2,128,128]{2,1,0:T(8,128)}, f32[2,128,128]{2,1,0:T(8,128)S(1)}, u32[]{:S(2)}, u32[]{:S(2)}) collective-permute-start(f32[2,128,128]{2,1,0:T(8,128)} %bias_kernel.1), channel_id=1, source_target_pairs={{0,1},{1,0},{2,3},{3,2},{4,5},{5,4},{6,7},{7,6},{8,9},{9,8},{10,11... | collective-permute-start | bytes 393224 | tf_op jit(solution)/shard_map/ppermute | solution.py:220
  25.5 13.1 %collective-permute-start.1 = (f32[2,128,128]{2,1,0:T(8,128)}, f32[2,128,128]{2,1,0:T(8,128)S(1)}, u32[]{:S(2)}, u32[]{:S(2)}) collective-permute-start(f32[2,128,128]{2,1,0:T(8,128)} %bias_kernel.1), channel_id=1, source_target_pairs={{0,2},{1,3},{2,0},{3,1},{4,6},{5,7},{6,4},{7,5},{8,10},{9,11},{10,... | collective-permute-start | bytes 393224 | tf_op jit(solution)/shard_map/ppermute | solution.py:220
  27.3 11.3 %collective-permute-start.2 = (f32[2,128,128]{2,1,0:T(8,128)}, f32[2,128,128]{2,1,0:T(8,128)S(1)}, u32[]{:S(2)}, u32[]{:S(2)}) collective-permute-start(f32[2,128,128]{2,1,0:T(8,128)} %bias_kernel.1), channel_id=1, source_target_pairs={{0,3},{1,2},{2,1},{3,0},{4,7},{5,6},{6,5},{7,4},{8,11},{9,10},{10,... | collective-permute-start | bytes 393224 | tf_op jit(solution)/shard_map/ppermute | solution.py:220
  39.6 15.6 %collective-permute-start.3 = (f32[4,2,128,128]{3,2,1,0:T(8,128)S(1)}, f32[4,2,128,128]{3,2,1,0:T(8,128)S(1)}, u32[]{:S(2)}, u32[]{:S(2)}) collective-permute-start(f32[4,2,128,128]{3,2,1,0:T(8,128)S(1)} %pad_maximum_fusion.refs_0_), channel_id=1, source_target_pairs={{0,8},{4,12},{8,0},{12,4},{16,24},{20,28},{24,16},{28,20},{1,9},{5... | collective-permute-start | bytes 1572872 | tf_op jit(solution)/shard_map/ppermute | solution.py:220
  41.1 14.1 %collective-permute-start.4 = (f32[4,2,128,128]{3,2,1,0:T(8,128)S(1)}, f32[4,2,128,128]{3,2,1,0:T(8,128)}, u32[]{:S(2)}, u32[]{:S(2)}) collective-permute-start(f32[4,2,128,128]{3,2,1,0:T(8,128)S(1)} %pad_maximum_fusion.refs_0_), channel_id=1, source_target_pairs={{0,16},{4,20},{8,24},{12,28},{16,0},{20,4},{24,8},{28,12},{1,17},{... | collective-permute-start | bytes 1572872 | tf_op jit(solution)/shard_map/ppermute | solution.py:220
  56.4 8.6 %collective-permute-start.5 = (f32[2,2,128,128]{3,2,1,0:T(8,128)S(1)}, f32[2,2,128,128]{3,2,1,0:T(8,128)S(1)}, u32[]{:S(2)}, u32[]{:S(2)}) collective-permute-start(f32[2,2,128,128]{3,2,1,0:T(8,128)S(1)} %slice.18), channel_id=1, source_target_pairs={{0,8},{4,12},{8,0},{12,4},{16,24},{20,28},{24,16},{28,20},{1,9},{5... | collective-permute-start | bytes 786440 | tf_op jit(solution)/shard_map/ppermute | solution.py:220
  57.0 8.0 %collective-permute-start.6 = (f32[2,2,128,128]{3,2,1,0:T(8,128)S(1)}, f32[2,2,128,128]{3,2,1,0:T(8,128)S(1)}, u32[]{:S(2)}, u32[]{:S(2)}) collective-permute-start(f32[2,2,128,128]{3,2,1,0:T(8,128)S(1)} %slice.19), channel_id=1, source_target_pairs={{0,16},{4,20},{8,24},{12,28},{16,0},{20,4},{24,8},{28,12},{1,17},{... | collective-permute-start | bytes 786440 | tf_op jit(solution)/shard_map/ppermute | solution.py:220
  58.4 8.7 %collective-permute-start.7 = (f32[4,2,128,128]{3,2,1,0:T(8,128)S(1)}, f32[4,2,128,128]{3,2,1,0:T(8,128)S(1)}, u32[]{:S(2)}, u32[]{:S(2)}) collective-permute-start(f32[4,2,128,128]{3,2,1,0:T(8,128)S(1)} %pad_maximum_fusion.refs_0_), channel_id=1, source_target_pairs={{0,4},{4,0},{8,12},{12,8},{16,20},{20,16},{24,28},{28,24},{1,5},{5... | collective-permute-start | bytes 1572872 | tf_op jit(solution)/shard_map/ppermute | solution.py:220
  58.4 8.7 %collective-permute-start.8 = (f32[4,2,128,128]{3,2,1,0:T(8,128)S(1)}, f32[4,2,128,128]{3,2,1,0:T(8,128)S(1)}, u32[]{:S(2)}, u32[]{:S(2)}) collective-permute-start(f32[4,2,128,128]{3,2,1,0:T(8,128)S(1)} %collective-permute-done.3.refs_2_), channel_id=1, source_target_pairs={{0,4},{4,0},{8,12},{12,8},{16,20},{20,16},{24,28},{28,24},{1,5},{5... | collective-permute-start | bytes 1572872 | tf_op jit(solution)/shard_map/ppermute | solution.py:220
  58.9 8.2 %collective-permute-start.9 = (f32[4,2,128,128]{3,2,1,0:T(8,128)}, f32[4,2,128,128]{3,2,1,0:T(8,128)S(1)}, u32[]{:S(2)}, u32[]{:S(2)}) collective-permute-start(f32[4,2,128,128]{3,2,1,0:T(8,128)} %collective-permute-done.4.refs_4_), channel_id=1, source_target_pairs={{0,4},{4,0},{8,12},{12,8},{16,20},{20,16},{24,28},{28,24},{1,5},{5... | collective-permute-start | bytes 1572872 | tf_op jit(solution)/shard_map/ppermute | solution.py:220
  65.0 1.7 %collective-permute-start.10 = (f32[2,2,128,128]{3,2,1,0:T(8,128)S(1)}, f32[2,2,128,128]{3,2,1,0:T(8,128)S(1)}, u32[]{:S(2)}, u32[]{:S(2)}) collective-permute-start(f32[2,2,128,128]{3,2,1,0:T(8,128)S(1)} %collective-permute-done.5.refs_6_), channel_id=1, source_target_pairs={{0,4},{4,0},{8,12},{12,8},{16,20},{20,16},{24,28},{28,24},{1,5},{5... | collective-permute-start | bytes 786440 | tf_op jit(solution)/shard_map/ppermute | solution.py:220
  65.5 1.5 collective-permute-start.11
  86.4 35.8 %all-to-all-start.2 = ((bf16[8,8,64,128]{3,2,1,0:T(8,128)(2,1)}), bf16[8,8,64,128]{3,2,1,0:T(8,128)(2,1)S(1)}, u32[]{:S(2)}, u32[]{:S(2)}) async-start(bf16[8,8,64,128]{3,2,1,0:T(8,128)(2,1)} %get-tuple-element.100), calls=%async_computation.2 | async-start | bytes 2097152 | tf_op jit(solution)/shard_map/all_to_all | solution.py:346
  91.2 27.0 %collective-permute-start.12 = (bf16[2,8,64,128]{3,2,1,0:T(8,128)(2,1)S(1)}, bf16[2,8,64,128]{3,2,1,0:T(8,128)(2,1)S(1)}, u32[]{:S(2)}, u32[]{:S(2)}) collective-permute-start(bf16[2,8,64,128]{3,2,1,0:T(8,128)(2,1)S(1)} %copy-done.25), channel_id=1, source_target_pairs={{0,0},{1,8},{2,16},{3,24},{4,1},{5,9},{6,17},{7,25},{8,2},{9,10},{... | collective-permute-start | bytes 786440 | tf_op jit(solution)/shard_map/ppermute | solution.py:353
  93.2 25.3 %collective-permute-start.13 = (bf16[2,8,64,128]{3,2,1,0:T(8,128)(2,1)S(1)}, bf16[2,8,64,128]{3,2,1,0:T(8,128)(2,1)S(1)}, u32[]{:S(2)}, u32[]{:S(2)}) collective-permute-start(bf16[2,8,64,128]{3,2,1,0:T(8,128)(2,1)S(1)} %copy-done.24), channel_id=1, source_target_pairs={{0,1},{1,9},{2,17},{3,25},{4,0},{5,8},{6,16},{7,24},{8,3},{9,11},{... | collective-permute-start | bytes 786440 | tf_op jit(solution)/shard_map/ppermute | solution.py:353
  94.8 23.8 %collective-permute-start.14 = (bf16[2,8,64,128]{3,2,1,0:T(8,128)(2,1)S(1)}, bf16[2,8,64,128]{3,2,1,0:T(8,128)(2,1)S(1)}, u32[]{:S(2)}, u32[]{:S(2)}) collective-permute-start(bf16[2,8,64,128]{3,2,1,0:T(8,128)(2,1)S(1)} %copy-done.23), channel_id=1, source_target_pairs={{0,2},{1,10},{2,18},{3,26},{4,3},{5,11},{6,19},{7,27},{8,0},{9,8},... | collective-permute-start | bytes 786440 | tf_op jit(solution)/shard_map/ppermute | solution.py:353
  96.8 25.4 %collective-permute-start.15 = (bf16[2,8,64,128]{3,2,1,0:T(8,128)(2,1)S(1)}, bf16[2,8,64,128]{3,2,1,0:T(8,128)(2,1)S(1)}, u32[]{:S(2)}, u32[]{:S(2)}) collective-permute-start(bf16[2,8,64,128]{3,2,1,0:T(8,128)(2,1)S(1)} %copy-done.22), channel_id=1, source_target_pairs={{0,3},{1,11},{2,19},{3,27},{4,2},{5,10},{6,18},{7,26},{8,1},{9,9},... | collective-permute-start | bytes 786440 | tf_op jit(solution)/shard_map/ppermute | solution.py:353
  122.2 37.1 %all-to-all-start.3 = ((bf16[8,8,64,128]{3,2,1,0:T(8,128)(2,1)}), bf16[8,8,64,128]{3,2,1,0:T(8,128)(2,1)S(1)}, u32[]{:S(2)}, u32[]{:S(2)}) async-start(bf16[8,8,64,128]{3,2,1,0:T(8,128)(2,1)} %get-tuple-element.106), calls=%async_computation.3 | async-start | bytes 2097152 | tf_op jit(solution)/shard_map/all_to_all | solution.py:346
  125.7 24.3 %collective-permute-start.16 = (bf16[2,8,64,128]{3,2,1,0:T(8,128)(2,1)}, bf16[2,8,64,128]{3,2,1,0:T(8,128)(2,1)S(1)}, u32[]{:S(2)}, u32[]{:S(2)}) collective-permute-start(bf16[2,8,64,128]{3,2,1,0:T(8,128)(2,1)} %get-tuple-element.111), channel_id=1, source_target_pairs={{0,0},{1,8},{2,16},{3,24},{4,1},{5,9},{6,17},{7,25},{8,2},{9,10},{... | collective-permute-start | bytes 786440 | tf_op jit(solution)/shard_map/ppermute | solution.py:353
  127.7 27.6 %collective-permute-start.17 = (bf16[2,8,64,128]{3,2,1,0:T(8,128)(2,1)}, bf16[2,8,64,128]{3,2,1,0:T(8,128)(2,1)}, u32[]{:S(2)}, u32[]{:S(2)}) collective-permute-start(bf16[2,8,64,128]{3,2,1,0:T(8,128)(2,1)} %get-tuple-element.112), channel_id=1, source_target_pairs={{0,1},{1,9},{2,17},{3,25},{4,0},{5,8},{6,16},{7,24},{8,3},{9,11},{... | collective-permute-start | bytes 786440 | tf_op jit(solution)/shard_map/ppermute | solution.py:353
  130.6 24.7 %collective-permute-start.18 = (bf16[2,8,64,128]{3,2,1,0:T(8,128)(2,1)}, bf16[2,8,64,128]{3,2,1,0:T(8,128)(2,1)}, u32[]{:S(2)}, u32[]{:S(2)}) collective-permute-start(bf16[2,8,64,128]{3,2,1,0:T(8,128)(2,1)} %get-tuple-element.113), channel_id=1, source_target_pairs={{0,2},{1,10},{2,18},{3,26},{4,3},{5,11},{6,19},{7,27},{8,0},{9,8},... | collective-permute-start | bytes 786440 | tf_op jit(solution)/shard_map/ppermute | solution.py:353
  131.6 27.7 %collective-permute-start.19 = (bf16[2,8,64,128]{3,2,1,0:T(8,128)(2,1)}, bf16[2,8,64,128]{3,2,1,0:T(8,128)(2,1)}, u32[]{:S(2)}, u32[]{:S(2)}) collective-permute-start(bf16[2,8,64,128]{3,2,1,0:T(8,128)(2,1)} %get-tuple-element.114), channel_id=1, source_target_pairs={{0,3},{1,11},{2,19},{3,27},{4,2},{5,10},{6,18},{7,26},{8,1},{9,9},... | collective-permute-start | bytes 786440 | tf_op jit(solution)/shard_map/ppermute | solution.py:353
  (27 other events, 364.1 us)

commit v6 on v5

--- a/solution.py
+++ b/solution.py
@@ -276,7 +276,7 @@
 
     def project(step):
         done, part = sum(parts[:step]), parts[step]
-        batch = min(4, part)
+        batch = min(2, part)
         spread_rows = -(-(done + part) // 8) * 8 - done // 8 * 8
         by_rows = pl.BlockSpec((batch, total, width), lambda j: (j, 0, 0))
         by_lanes = pl.BlockSpec((batch, width, total), lambda j: (j, 0, 0))

time: 170 us -> 171 us (level)
  transfers between devices with their start and end apart: 24 -> 24, of which waited for: 13 -> 12; matrix products, arithmetic and copies ran while one was open for 6% -> 6% of each run, Pallas kernels for 21% -> 22%
where the time goes in v6:
time: 171 us; the launch traced here: 170 us
  Pallas kernels  62.9 us (37%)
  starting transfers between devices  48.1 us (28%)
  waiting for transfers between devices  42 us (25%)
  local copies, waits for them, and re-layouts  12.2 us (7%)
  other arithmetic  4.3 us (3%)
    pallas_call x2, Pallas kernels, per_device(): pl.pallas_call(functools.partial(attention_kernel, heads, n_cols, splits)...  34.9 us
    ppermute x8, waiting for transfers between devices, per_device(): mirrored.append(lax.ppermute(turned[shift], AXES, hops))  26.2 us
    ppermute x8, starting transfers between devices, per_device(): mirrored.append(lax.ppermute(turned[shift], AXES, hops))  19.7 us
    pallas_call x2, Pallas kernels, project(): pl.pallas_call(functools.partial(project_kernel, head_dim, batch, done, p...  13.5 us
    ppermute x12, waiting for transfers between devices, swap_over(): return lax.ppermute(array, axis, [(at, at ^ step) for at in range(count)])  13.2 us
    ppermute x12, starting transfers between devices, swap_over(): return lax.ppermute(array, axis, [(at, at ^ step) for at in range(count)])  9.53 us
    pallas_call x1, Pallas kernels, per_device(): pl.pallas_call(functools.partial(logits_kernel, n_cols, parts), out_shape...  8.75 us
    all_to_all x2, starting transfers between devices, per_device(): lax.all_to_all(updated, 'row', split_axis=0, concat_axis=0, tiled=True)  7.93 us
  transfers between devices with their start and end apart: 24, of which 12 were waited for; matrix products, arithmetic and copies ran while one was open for 6% of the time, Pallas kernels for 22%

profile of v6, /device:TPU:4, one launch (start us, length us, event | category | flops | bytes accessed | tf_op | source)
XLA Modules:
  0.0 169.9 jit_solution(11449247217636130204)
XLA Ops:
  1.3 6.1 %all-to-all-start = ((s32[32,4,16]{2,1,0:T(4,128)}), s32[32,4,16]{2,1,0:T(4,128)S(1)}, u32[]{:S(2)}, u32[]{:S(2)}) async-start(s32[32,4,16]{2,1,0:T(4,128)} %broadcast_in_dim.20), calls=%async_computation | async-start | bytes 131072 | tf_op jit(solution)/shard_map/all_to_all | solution.py:247
  8.1 3.3 %copy.25 = bf16[64,8,16,128]{3,2,0,1:T(8,128)(2,1)} copy(bf16[64,8,16,128]{3,2,1,0:T(8,128)(2,1)} %bitcast.21) | data formatting | bytes 4194304 | tf_op jit(solution)/shard_map/reshape | solution.py:249
  13.8 4.9 %all-to-all-start.1 = ((bf16[8,64,16,128]{3,2,1,0:T(8,128)(2,1)}), bf16[8,64,16,128]{3,2,1,0:T(8,128)(2,1)S(1)}, u32[]{:S(2)}, u32[]{:S(2)}) async-start(bf16[8,64,16,128]{3,2,1,0:T(8,128)(2,1)} %bitcast.20), calls=%async_computation.1 | async-start | bytes 4194304 | tf_op jit(solution)/shard_map/all_to_all | solution.py:252
  19.4 5.9 %bias_kernel.1 = f32[2,128,128]{2,1,0:T(8,128)} custom-call(s32[4,512]{1,0:T(4,128)} %reshape.10.scalars.tokens, s32[4,512]{1,0:T(4,128)} %reshape.10.scalars.tokens, f32[1,128]{1,0:T(1,128)} %get-tuple-element.60.low, f32[1,128]{1,0:T(1,128)} %get-tuple-element.61.high, bf16[64,128,128]{2,1,0:T(8,128)(2,1)} %z.1, bf16[128,128]{1,0:T(8,128)(2,1)} %pad.17.w_dist, ...), custom_call_target="tpu_custom_call" | custom-call | flops 314572800 | bytes 4194304 | tf_op jit(solution)/shard_map/bias_kernel/pallas_call | solution.py:255
  27.3 2.4 %collective-permute-start.2 = (f32[2,128,128]{2,1,0:T(8,128)}, f32[2,128,128]{2,1,0:T(8,128)S(1)}, u32[]{:S(2)}, u32[]{:S(2)}) collective-permute-start(f32[2,128,128]{2,1,0:T(8,128)} %bias_kernel.1), channel_id=1, source_target_pairs={{0,3},{1,2},{2,1},{3,0},{4,7},{5,6},{6,5},{7,4},{8,11},{9,10},{10,... | collective-permute-start | bytes 393224 | tf_op jit(solution)/shard_map/ppermute | solution.py:220
  29.7 3.2 %collective-permute-done = f32[2,128,128]{2,1,0:T(8,128)S(1)} collective-permute-done((f32[2,128,128]{2,1,0:T(8,128)}, f32[2,128,128]{2,1,0:T(8,128)S(1)}, u32[]{:S(2)}, u32[]{:S(2)}) %collective-permute-start) | collective-permute-done | bytes 131104 | tf_op jit(solution)/shard_map/ppermute | solution.py:220
  32.9 5.7 %collective-permute-done.1 = f32[2,128,128]{2,1,0:T(8,128)S(1)} collective-permute-done((f32[2,128,128]{2,1,0:T(8,128)}, f32[2,128,128]{2,1,0:T(8,128)S(1)}, u32[]{:S(2)}, u32[]{:S(2)}) %collective-permute-start.1) | collective-permute-done | bytes 131104 | tf_op jit(solution)/shard_map/ppermute | solution.py:220
  45.7 6.7 %project_kernel.2 = (bf16[8,512,128]{2,1,0:T(8,128)(2,1)}, bf16[8,128,512]{2,1,0:T(8,128)(2,1)}, bf16[8,512,128]{2,1,0:T(8,128)(2,1)}, bf16[8,512,128]{2,1,0:T(8,128)(2,1)}, bf16[8,512,128]{2,1,0:T(8,128)(2,1)}) custom-call(s32[4,512]{1,0:T(4,128)} %reshape.10.scalars.tokens, s32[4,512]{1,0:T(4,128)} %reshape.10.scalars.tokens, ...), custom_call_target="tpu_custom_call" | custom-call | flops 1048576000 | bytes 8388608 | tf_op jit(solution)/shard_map/project_kernel/pallas_call | solution.py:285
  52.4 2.8 %collective-permute-done.3.refs_2_ = f32[4,2,128,128]{3,2,1,0:T(8,128)S(1)} collective-permute-done((f32[4,2,128,128]{3,2,1,0:T(8,128)S(1)}, f32[4,2,128,128]{3,2,1,0:T(8,128)S(1)}, u32[]{:S(2)}, u32[]{:S(2)}) %collective-permute-start.3) | collective-permute-done | bytes 524320 | tf_op jit(solution)/shard_map/ppermute | solution.py:220
  58.9 6.8 %project_kernel.3 = (bf16[8,512,128]{2,1,0:T(8,128)(2,1)}, bf16[8,128,512]{2,1,0:T(8,128)(2,1)}, bf16[8,512,128]{2,1,0:T(8,128)(2,1)}, bf16[8,512,128]{2,1,0:T(8,128)(2,1)}, bf16[8,512,128]{2,1,0:T(8,128)(2,1)}) custom-call(s32[4,512]{1,0:T(4,128)} %reshape.10.scalars.tokens, s32[4,512]{1,0:T(4,128)} %reshape.10.scalars.tokens, ...), custom_call_target="tpu_custom_call" | custom-call | flops 1048576000 | bytes 8388608 | tf_op jit(solution)/shard_map/project_kernel/pallas_call | solution.py:285
  69.6 17.4 %attention_kernel.3 = (bf16[8,8,64,128]{3,2,1,0:T(8,128)(2,1)}, bf16[2,8,64,128]{3,2,1,0:T(8,128)(2,1)}, bf16[2,8,64,128]{3,2,1,0:T(8,128)(2,1)}, bf16[2,8,64,128]{3,2,1,0:T(8,128)(2,1)}, bf16[2,8,64,128]{3,2,1,0:T(8,128)(2,1)}) custom-call(s32[4,512]{1,0:T(4,128)} %reshape.10.scalars.tokens, bf16[8,128,512]{2,1,0:T(8,128)(2,1)} %get-tuple-element.95.key, ...), custom_call_target="tpu_custom_call" | custom-call | flops 8589934592 | bytes 16777216 | tf_op jit(solution)/shard_map/attention_kernel/pallas_call | solution.py:325
  87.1 4.4 %all-to-all-start.2 = ((bf16[8,8,64,128]{3,2,1,0:T(8,128)(2,1)}), bf16[8,8,64,128]{3,2,1,0:T(8,128)(2,1)S(1)}, u32[]{:S(2)}, u32[]{:S(2)}) async-start(bf16[8,8,64,128]{3,2,1,0:T(8,128)(2,1)} %get-tuple-element.100), calls=%async_computation.2 | async-start | bytes 2097152 | tf_op jit(solution)/shard_map/all_to_all | solution.py:346
  91.5 2.0 %collective-permute-start.12 = (bf16[2,8,64,128]{3,2,1,0:T(8,128)(2,1)S(1)}, bf16[2,8,64,128]{3,2,1,0:T(8,128)(2,1)S(1)}, u32[]{:S(2)}, u32[]{:S(2)}) collective-permute-start(bf16[2,8,64,128]{3,2,1,0:T(8,128)(2,1)S(1)} %copy-done.25), channel_id=1, source_target_pairs={{0,0},{1,8},{2,16},{3,24},{4,1},{5,9},{6,17},{7,25},{8,2},{9,10},{... | collective-permute-start | bytes 786440 | tf_op jit(solution)/shard_map/ppermute | solution.py:353
  93.5 1.9 %collective-permute-start.13 = (bf16[2,8,64,128]{3,2,1,0:T(8,128)(2,1)S(1)}, bf16[2,8,64,128]{3,2,1,0:T(8,128)(2,1)S(1)}, u32[]{:S(2)}, u32[]{:S(2)}) collective-permute-start(bf16[2,8,64,128]{3,2,1,0:T(8,128)(2,1)S(1)} %copy-done.24), channel_id=1, source_target_pairs={{0,1},{1,9},{2,17},{3,25},{4,0},{5,8},{6,16},{7,24},{8,3},{9,11},{... | collective-permute-start | bytes 786440 | tf_op jit(solution)/shard_map/ppermute | solution.py:353
  97.1 4.1 %collective-permute-start.15 = (bf16[2,8,64,128]{3,2,1,0:T(8,128)(2,1)S(1)}, bf16[2,8,64,128]{3,2,1,0:T(8,128)(2,1)S(1)}, u32[]{:S(2)}, u32[]{:S(2)}) collective-permute-start(bf16[2,8,64,128]{3,2,1,0:T(8,128)(2,1)S(1)} %copy-done.22), channel_id=1, source_target_pairs={{0,3},{1,11},{2,19},{3,27},{4,2},{5,10},{6,18},{7,26},{8,1},{9,9},... | collective-permute-start | bytes 786440 | tf_op jit(solution)/shard_map/ppermute | solution.py:353
  101.2 17.5 %attention_kernel.2 = (bf16[8,8,64,128]{3,2,1,0:T(8,128)(2,1)}, bf16[2,8,64,128]{3,2,1,0:T(8,128)(2,1)}, bf16[2,8,64,128]{3,2,1,0:T(8,128)(2,1)}, bf16[2,8,64,128]{3,2,1,0:T(8,128)(2,1)}, bf16[2,8,64,128]{3,2,1,0:T(8,128)(2,1)}) custom-call(s32[4,512]{1,0:T(4,128)} %reshape.10.scalars.tokens, bf16[8,128,512]{2,1,0:T(8,128)(2,1)} %get-tuple-element.82.key, ...), custom_call_target="tpu_custom_call" | custom-call | flops 8589934592 | bytes 16777216 | tf_op jit(solution)/shard_map/attention_kernel/pallas_call | solution.py:325
  119.0 3.4 %collective-permute-done.15.refs_6_ = bf16[2,8,64,128]{3,2,1,0:T(8,128)(2,1)S(1)} collective-permute-done((bf16[2,8,64,128]{3,2,1,0:T(8,128)(2,1)S(1)}, bf16[2,8,64,128]{3,2,1,0:T(8,128)(2,1)S(1)}, u32[]{:S(2)}, u32[]{:S(2)}) %collective-permute-start.15) | collective-permute-done | bytes 262176 | tf_op jit(solution)/shard_map/ppermute | solution.py:353
  122.5 3.5 %all-to-all-start.3 = ((bf16[8,8,64,128]{3,2,1,0:T(8,128)(2,1)}), bf16[8,8,64,128]{3,2,1,0:T(8,128)(2,1)S(1)}, u32[]{:S(2)}, u32[]{:S(2)}) async-start(bf16[8,8,64,128]{3,2,1,0:T(8,128)(2,1)} %get-tuple-element.106), calls=%async_computation.3 | async-start | bytes 2097152 | tf_op jit(solution)/shard_map/all_to_all | solution.py:346
  127.9 3.1 %collective-permute-start.17 = (bf16[2,8,64,128]{3,2,1,0:T(8,128)(2,1)}, bf16[2,8,64,128]{3,2,1,0:T(8,128)(2,1)}, u32[]{:S(2)}, u32[]{:S(2)}) collective-permute-start(bf16[2,8,64,128]{3,2,1,0:T(8,128)(2,1)} %get-tuple-element.112), channel_id=1, source_target_pairs={{0,1},{1,9},{2,17},{3,25},{4,0},{5,8},{6,16},{7,24},{8,3},{9,11},{... | collective-permute-start | bytes 786440 | tf_op jit(solution)/shard_map/ppermute | solution.py:353
  132.0 3.9 %collective-permute-start.19 = (bf16[2,8,64,128]{3,2,1,0:T(8,128)(2,1)}, bf16[2,8,64,128]{3,2,1,0:T(8,128)(2,1)}, u32[]{:S(2)}, u32[]{:S(2)}) collective-permute-start(bf16[2,8,64,128]{3,2,1,0:T(8,128)(2,1)} %get-tuple-element.114), channel_id=1, source_target_pairs={{0,3},{1,11},{2,19},{3,27},{4,2},{5,10},{6,18},{7,26},{8,1},{9,9},... | collective-permute-start | bytes 786440 | tf_op jit(solution)/shard_map/ppermute | solution.py:353
  137.6 12.7 %collective-permute-done.16.refs_7_ = bf16[2,8,64,128]{3,2,1,0:T(8,128)(2,1)S(1)} collective-permute-done((bf16[2,8,64,128]{3,2,1,0:T(8,128)(2,1)}, bf16[2,8,64,128]{3,2,1,0:T(8,128)(2,1)S(1)}, u32[]{:S(2)}, u32[]{:S(2)}) %collective-permute-start.16) | collective-permute-done | bytes 262176 | tf_op jit(solution)/shard_map/ppermute | solution.py:353
  150.3 5.5 %collective-permute-done.17.refs_8_ = bf16[2,8,64,128]{3,2,1,0:T(8,128)(2,1)} collective-permute-done((bf16[2,8,64,128]{3,2,1,0:T(8,128)(2,1)}, bf16[2,8,64,128]{3,2,1,0:T(8,128)(2,1)}, u32[]{:S(2)}, u32[]{:S(2)}) %collective-permute-start.17) | collective-permute-done | bytes 262176 | tf_op jit(solution)/shard_map/ppermute | solution.py:353
  155.8 4.3 %collective-permute-done.19.refs_10_ = bf16[2,8,64,128]{3,2,1,0:T(8,128)(2,1)} collective-permute-done((bf16[2,8,64,128]{3,2,1,0:T(8,128)(2,1)}, bf16[2,8,64,128]{3,2,1,0:T(8,128)(2,1)}, u32[]{:S(2)}, u32[]{:S(2)}) %collective-permute-start.19) | collective-permute-done | bytes 262176 | tf_op jit(solution)/shard_map/ppermute | solution.py:353
  161.2 8.7 %logits_kernel.1 = f32[64,128,128]{2,1,0:T(8,128)} custom-call(s32[4]{0:T(128)} %pad_add_fusion.1.refs_0_, bf16[8,8,64,128]{3,2,1,0:T(8,128)(2,1)} %copy-done, bf16[8,8,64,128]{3,2,1,0:T(8,128)(2,1)} %copy-done.1, bf16[2,8,64,128]{3,2,1,0:T(8,128)(2,1)} %copy-done.4, bf16[2,8,64,128]{3,2,1,0:T(8,128)(2,1)} %copy-done.5, bf16[2,8,64,128]{3,2,1,0:T(8,128)(2,1)} %copy-done.6, ...), custom_call_target="tpu_custom_call" | custom-call | tf_op jit(solution)/shard_map/logits_kernel/pallas_call | solution.py:360
  (104 shorter events, 29.3 us)
Async XLA Ops:
  1.3 12.5 %all-to-all-start = ((s32[32,4,16]{2,1,0:T(4,128)}), s32[32,4,16]{2,1,0:T(4,128)S(1)}, u32[]{:S(2)}, u32[]{:S(2)}) async-start(s32[32,4,16]{2,1,0:T(4,128)} %broadcast_in_dim.20), calls=%async_computation | async-start | bytes 131072 | tf_op jit(solution)/shard_map/all_to_all | solution.py:247
  13.8 30.6 %all-to-all-start.1 = ((bf16[8,64,16,128]{3,2,1,0:T(8,128)(2,1)}), bf16[8,64,16,128]{3,2,1,0:T(8,128)(2,1)S(1)}, u32[]{:S(2)}, u32[]{:S(2)}) async-start(bf16[8,64,16,128]{3,2,1,0:T(8,128)(2,1)} %bitcast.20), calls=%async_computation.1 | async-start | bytes 4194304 | tf_op jit(solution)/shard_map/all_to_all | solution.py:252
  25.3 7.6 %collective-permute-start = (f32[2,128,128]{2,1,0:T(8,128)}, f32[2,128,128]{2,1,0:T(8,128)S(1)}, u32[]{:S(2)}, u32[]{:S(2)}) collective-permute-start(f32[2,128,128]{2,1,0:T(8,128)} %bias_kernel.1), channel_id=1, source_target_pairs={{0,1},{1,0},{2,3},{3,2},{4,5},{5,4},{6,7},{7,6},{8,9},{9,8},{10,11... | collective-permute-start | bytes 393224 | tf_op jit(solution)/shard_map/ppermute | solution.py:220
  25.5 13.1 %collective-permute-start.1 = (f32[2,128,128]{2,1,0:T(8,128)}, f32[2,128,128]{2,1,0:T(8,128)S(1)}, u32[]{:S(2)}, u32[]{:S(2)}) collective-permute-start(f32[2,128,128]{2,1,0:T(8,128)} %bias_kernel.1), channel_id=1, source_target_pairs={{0,2},{1,3},{2,0},{3,1},{4,6},{5,7},{6,4},{7,5},{8,10},{9,11},{10,... | collective-permute-start | bytes 393224 | tf_op jit(solution)/shard_map/ppermute | solution.py:220
  27.3 11.3 %collective-permute-start.2 = (f32[2,128,128]{2,1,0:T(8,128)}, f32[2,128,128]{2,1,0:T(8,128)S(1)}, u32[]{:S(2)}, u32[]{:S(2)}) collective-permute-start(f32[2,128,128]{2,1,0:T(8,128)} %bias_kernel.1), channel_id=1, source_target_pairs={{0,3},{1,2},{2,1},{3,0},{4,7},{5,6},{6,5},{7,4},{8,11},{9,10},{10,... | collective-permute-start | bytes 393224 | tf_op jit(solution)/shard_map/ppermute | solution.py:220
  39.6 15.6 %collective-permute-start.3 = (f32[4,2,128,128]{3,2,1,0:T(8,128)S(1)}, f32[4,2,128,128]{3,2,1,0:T(8,128)S(1)}, u32[]{:S(2)}, u32[]{:S(2)}) collective-permute-start(f32[4,2,128,128]{3,2,1,0:T(8,128)S(1)} %pad_maximum_fusion.refs_0_), channel_id=1, source_target_pairs={{0,8},{4,12},{8,0},{12,4},{16,24},{20,28},{24,16},{28,20},{1,9},{5... | collective-permute-start | bytes 1572872 | tf_op jit(solution)/shard_map/ppermute | solution.py:220
  41.1 14.1 %collective-permute-start.4 = (f32[4,2,128,128]{3,2,1,0:T(8,128)S(1)}, f32[4,2,128,128]{3,2,1,0:T(8,128)}, u32[]{:S(2)}, u32[]{:S(2)}) collective-permute-start(f32[4,2,128,128]{3,2,1,0:T(8,128)S(1)} %pad_maximum_fusion.refs_0_), channel_id=1, source_target_pairs={{0,16},{4,20},{8,24},{12,28},{16,0},{20,4},{24,8},{28,12},{1,17},{... | collective-permute-start | bytes 1572872 | tf_op jit(solution)/shard_map/ppermute | solution.py:220
  56.4 9.3 %collective-permute-start.5 = (f32[2,2,128,128]{3,2,1,0:T(8,128)S(1)}, f32[2,2,128,128]{3,2,1,0:T(8,128)S(1)}, u32[]{:S(2)}, u32[]{:S(2)}) collective-permute-start(f32[2,2,128,128]{3,2,1,0:T(8,128)S(1)} %slice.18), channel_id=1, source_target_pairs={{0,8},{4,12},{8,0},{12,4},{16,24},{20,28},{24,16},{28,20},{1,9},{5... | collective-permute-start | bytes 786440 | tf_op jit(solution)/shard_map/ppermute | solution.py:220
  57.0 8.7 %collective-permute-start.6 = (f32[2,2,128,128]{3,2,1,0:T(8,128)S(1)}, f32[2,2,128,128]{3,2,1,0:T(8,128)S(1)}, u32[]{:S(2)}, u32[]{:S(2)}) collective-permute-start(f32[2,2,128,128]{3,2,1,0:T(8,128)S(1)} %slice.19), channel_id=1, source_target_pairs={{0,16},{4,20},{8,24},{12,28},{16,0},{20,4},{24,8},{28,12},{1,17},{... | collective-permute-start | bytes 786440 | tf_op jit(solution)/shard_map/ppermute | solution.py:220
  58.4 9.4 %collective-permute-start.7 = (f32[4,2,128,128]{3,2,1,0:T(8,128)S(1)}, f32[4,2,128,128]{3,2,1,0:T(8,128)S(1)}, u32[]{:S(2)}, u32[]{:S(2)}) collective-permute-start(f32[4,2,128,128]{3,2,1,0:T(8,128)S(1)} %pad_maximum_fusion.refs_0_), channel_id=1, source_target_pairs={{0,4},{4,0},{8,12},{12,8},{16,20},{20,16},{24,28},{28,24},{1,5},{5... | collective-permute-start | bytes 1572872 | tf_op jit(solution)/shard_map/ppermute | solution.py:220
  58.4 9.4 %collective-permute-start.8 = (f32[4,2,128,128]{3,2,1,0:T(8,128)S(1)}, f32[4,2,128,128]{3,2,1,0:T(8,128)S(1)}, u32[]{:S(2)}, u32[]{:S(2)}) collective-permute-start(f32[4,2,128,128]{3,2,1,0:T(8,128)S(1)} %collective-permute-done.3.refs_2_), channel_id=1, source_target_pairs={{0,4},{4,0},{8,12},{12,8},{16,20},{20,16},{24,28},{28,24},{1,5},{5... | collective-permute-start | bytes 1572872 | tf_op jit(solution)/shard_map/ppermute | solution.py:220
  58.9 8.9 %collective-permute-start.9 = (f32[4,2,128,128]{3,2,1,0:T(8,128)}, f32[4,2,128,128]{3,2,1,0:T(8,128)S(1)}, u32[]{:S(2)}, u32[]{:S(2)}) collective-permute-start(f32[4,2,128,128]{3,2,1,0:T(8,128)} %collective-permute-done.4.refs_4_), channel_id=1, source_target_pairs={{0,4},{4,0},{8,12},{12,8},{16,20},{20,16},{24,28},{28,24},{1,5},{5... | collective-permute-start | bytes 1572872 | tf_op jit(solution)/shard_map/ppermute | solution.py:220
  65.7 1.7 collective-permute-start.10
  66.2 1.5 collective-permute-start.11
  87.1 35.4 %all-to-all-start.2 = ((bf16[8,8,64,128]{3,2,1,0:T(8,128)(2,1)}), bf16[8,8,64,128]{3,2,1,0:T(8,128)(2,1)S(1)}, u32[]{:S(2)}, u32[]{:S(2)}) async-start(bf16[8,8,64,128]{3,2,1,0:T(8,128)(2,1)} %get-tuple-element.100), calls=%async_computation.2 | async-start | bytes 2097152 | tf_op jit(solution)/shard_map/all_to_all | solution.py:346
  91.5 27.2 %collective-permute-start.12 = (bf16[2,8,64,128]{3,2,1,0:T(8,128)(2,1)S(1)}, bf16[2,8,64,128]{3,2,1,0:T(8,128)(2,1)S(1)}, u32[]{:S(2)}, u32[]{:S(2)}) collective-permute-start(bf16[2,8,64,128]{3,2,1,0:T(8,128)(2,1)S(1)} %copy-done.25), channel_id=1, source_target_pairs={{0,0},{1,8},{2,16},{3,24},{4,1},{5,9},{6,17},{7,25},{8,2},{9,10},{... | collective-permute-start | bytes 786440 | tf_op jit(solution)/shard_map/ppermute | solution.py:353
  93.5 25.5 %collective-permute-start.13 = (bf16[2,8,64,128]{3,2,1,0:T(8,128)(2,1)S(1)}, bf16[2,8,64,128]{3,2,1,0:T(8,128)(2,1)S(1)}, u32[]{:S(2)}, u32[]{:S(2)}) collective-permute-start(bf16[2,8,64,128]{3,2,1,0:T(8,128)(2,1)S(1)} %copy-done.24), channel_id=1, source_target_pairs={{0,1},{1,9},{2,17},{3,25},{4,0},{5,8},{6,16},{7,24},{8,3},{9,11},{... | collective-permute-start | bytes 786440 | tf_op jit(solution)/shard_map/ppermute | solution.py:353
  95.4 23.6 %collective-permute-start.14 = (bf16[2,8,64,128]{3,2,1,0:T(8,128)(2,1)S(1)}, bf16[2,8,64,128]{3,2,1,0:T(8,128)(2,1)S(1)}, u32[]{:S(2)}, u32[]{:S(2)}) collective-permute-start(bf16[2,8,64,128]{3,2,1,0:T(8,128)(2,1)S(1)} %copy-done.23), channel_id=1, source_target_pairs={{0,2},{1,10},{2,18},{3,26},{4,3},{5,11},{6,19},{7,27},{8,0},{9,8},... | collective-permute-start | bytes 786440 | tf_op jit(solution)/shard_map/ppermute | solution.py:353
  97.1 25.3 %collective-permute-start.15 = (bf16[2,8,64,128]{3,2,1,0:T(8,128)(2,1)S(1)}, bf16[2,8,64,128]{3,2,1,0:T(8,128)(2,1)S(1)}, u32[]{:S(2)}, u32[]{:S(2)}) collective-permute-start(bf16[2,8,64,128]{3,2,1,0:T(8,128)(2,1)S(1)} %copy-done.22), channel_id=1, source_target_pairs={{0,3},{1,11},{2,19},{3,27},{4,2},{5,10},{6,18},{7,26},{8,1},{9,9},... | collective-permute-start | bytes 786440 | tf_op jit(solution)/shard_map/ppermute | solution.py:353
  122.5 37.6 %all-to-all-start.3 = ((bf16[8,8,64,128]{3,2,1,0:T(8,128)(2,1)}), bf16[8,8,64,128]{3,2,1,0:T(8,128)(2,1)S(1)}, u32[]{:S(2)}, u32[]{:S(2)}) async-start(bf16[8,8,64,128]{3,2,1,0:T(8,128)(2,1)} %get-tuple-element.106), calls=%async_computation.3 | async-start | bytes 2097152 | tf_op jit(solution)/shard_map/all_to_all | solution.py:346
  126.0 24.3 %collective-permute-start.16 = (bf16[2,8,64,128]{3,2,1,0:T(8,128)(2,1)}, bf16[2,8,64,128]{3,2,1,0:T(8,128)(2,1)S(1)}, u32[]{:S(2)}, u32[]{:S(2)}) collective-permute-start(bf16[2,8,64,128]{3,2,1,0:T(8,128)(2,1)} %get-tuple-element.111), channel_id=1, source_target_pairs={{0,0},{1,8},{2,16},{3,24},{4,1},{5,9},{6,17},{7,25},{8,2},{9,10},{... | collective-permute-start | bytes 786440 | tf_op jit(solution)/shard_map/ppermute | solution.py:353
  127.9 27.9 %collective-permute-start.17 = (bf16[2,8,64,128]{3,2,1,0:T(8,128)(2,1)}, bf16[2,8,64,128]{3,2,1,0:T(8,128)(2,1)}, u32[]{:S(2)}, u32[]{:S(2)}) collective-permute-start(bf16[2,8,64,128]{3,2,1,0:T(8,128)(2,1)} %get-tuple-element.112), channel_id=1, source_target_pairs={{0,1},{1,9},{2,17},{3,25},{4,0},{5,8},{6,16},{7,24},{8,3},{9,11},{... | collective-permute-start | bytes 786440 | tf_op jit(solution)/shard_map/ppermute | solution.py:353
  131.1 24.7 %collective-permute-start.18 = (bf16[2,8,64,128]{3,2,1,0:T(8,128)(2,1)}, bf16[2,8,64,128]{3,2,1,0:T(8,128)(2,1)}, u32[]{:S(2)}, u32[]{:S(2)}) collective-permute-start(bf16[2,8,64,128]{3,2,1,0:T(8,128)(2,1)} %get-tuple-element.113), channel_id=1, source_target_pairs={{0,2},{1,10},{2,18},{3,26},{4,3},{5,11},{6,19},{7,27},{8,0},{9,8},... | collective-permute-start | bytes 786440 | tf_op jit(solution)/shard_map/ppermute | solution.py:353
  132.0 28.1 %collective-permute-start.19 = (bf16[2,8,64,128]{3,2,1,0:T(8,128)(2,1)}, bf16[2,8,64,128]{3,2,1,0:T(8,128)(2,1)}, u32[]{:S(2)}, u32[]{:S(2)}) collective-permute-start(bf16[2,8,64,128]{3,2,1,0:T(8,128)(2,1)} %get-tuple-element.114), channel_id=1, source_target_pairs={{0,3},{1,11},{2,19},{3,27},{4,2},{5,10},{6,18},{7,26},{8,1},{9,9},... | collective-permute-start | bytes 786440 | tf_op jit(solution)/shard_map/ppermute | solution.py:353
  (27 other events, 366.7 us)
